TPU v7x, 32 devices: a whole 2x2x4 slice. The times are simulated.
32 devices in a mesh: groups: 2 (over y), store: 4 (over z), tensor: 4 (over x, core).
Axes of the slice: x: 2, y: 2, z: 4, core: 2. Of those that a mesh axis runs over, the one named last changes fastest.
Arguments:
- normed_input: bfloat16 [2, 128, 8192], P(None, ('groups', 'store'), 'tensor'), parts along dimension 1, may hold values from -6 to 6
- kv_weight: bfloat16 [2, 8192, 2048], P(None, 'tensor'), may hold values from -0.0625 to 0.0625
- down_adapters: bfloat16 [2, 128, 8192, 64], P(None, 'store', 'tensor'), may hold values from -0.0625 to 0.0625
- up_adapters: bfloat16 [2, 128, 64, 2048], P(None, 'store', None, 'tensor'), may hold values from -0.75 to 0.75
- request_owner: int32 [128, 1], P(('groups', 'store')), parts along dimension 0, may hold values from 0 to 3; in each aligned block of 16 rows (0 to 15, 16 to 31, ...) at most 4 rows name the same one
- request_slot: int32 [128], P(('groups', 'store')), parts along dimension 0, may hold values from 0 to 31
- request_count: int32 [8], P(('groups', 'store')), parts along dimension 0, may hold values from 8 to 16, as said below
Outputs:
- key_values: bfloat16 [2, 128, 2048], P(None, ('groups', 'store'), 'tensor'), parts along dimension 1
There are 2 independent parts, one for each index of `groups`. A program takes and returns all parts, laid end to end along the dimension named above; an argument that names none is the same for every part. Nothing has to cross between parts.
Inputs may be any that keep to these rules, and one draw needn't show every extreme that they name: `request_owner`: among the 16 rows of one store shard, at most 4 name the same owner shard. Slots of shard s at index request_count[s] or later are unused; some shard is full.
All inputs are finite; a program needn't handle non-finite values.
Results may differ from a plain program's by a relative error of at most 0.0042.
Values may be sent and summed in bfloat16 or wider, within the bound.
No kernel may reach another device: no remote copies, remote signals or barrier semaphores. Data moves between devices by JAX's collectives and lax.ppermute only.
A program may use at most 128 MiB of HBM per device.

v0:
```python
import jax
import jax.numpy as jnp
from jax import lax
from jax.sharding import PartitionSpec as P

LAYERS = 2
CAP = 4


def routing(request_owner, request_slot, request_count):
    owners_all, slots_all, counts_all = (
        lax.all_gather(request_owner[:, 0], "store", axis=0, tiled=True),
        lax.all_gather(request_slot, "store", axis=0, tiled=True),
        lax.all_gather(request_count, "store", axis=0, tiled=True),
    )
    store_count = lax.axis_size("store")
    row_count = request_slot.shape[0]
    owners_grid = owners_all.reshape(store_count, row_count)
    slots_grid = slots_all.reshape(store_count, row_count)
    position = jnp.arange(row_count, dtype=jnp.int32)
    live_grid = position[None, :] < counts_all[:, None]
    onehot = (
        (owners_grid[:, :, None] == jnp.arange(store_count, dtype=jnp.int32)[None, None, :])
        & live_grid[:, :, None]
    ).astype(jnp.int32)
    earlier = jnp.cumsum(onehot, axis=1) - onehot
    rank_grid = jnp.minimum(jnp.sum(earlier * onehot, axis=2), CAP - 1)
    own_index = lax.axis_index("store")
    mine_live = (owners_grid == own_index) & live_grid
    picked = mine_live[:, :, None] & (
        rank_grid[:, :, None] == jnp.arange(CAP, dtype=jnp.int32)[None, None, :]
    )
    chosen = jnp.sum(picked.astype(jnp.int32) * slots_grid[:, :, None], axis=1)
    filled = jnp.any(picked, axis=1)
    local_rank = lax.dynamic_index_in_dim(rank_grid, own_index, 0, keepdims=False)
    local_live = position < request_count[0]
    target = request_owner[:, 0] * CAP + local_rank
    return (chosen, filled, target, local_live)


def reduce_pair(partial_value, rank_part):
    base_part = lax.psum_scatter(partial_value, "tensor", scatter_dimension=1, tiled=True)
    rank_sum = lax.psum(rank_part, "tensor")
    return (base_part, rank_sum.astype(jnp.bfloat16))


def local(
    normed_input, kv_weight, down_adapters, up_adapters, request_owner, request_slot, request_count
):
    chosen, filled, target, local_live = routing(request_owner, request_slot, request_count)
    store_count = lax.axis_size("store")
    flat_slots = store_count * CAP
    results = []
    for layer_index in range(LAYERS):
        rows_in = normed_input[layer_index]
        partial_value = jnp.dot(rows_in, kv_weight[layer_index], preferred_element_type=jnp.float32)
        placed = (
            (target[:, None] == jnp.arange(flat_slots, dtype=jnp.int32)[None, :])
            & local_live[:, None]
        ).astype(jnp.bfloat16)
        outgoing = jnp.dot(placed.T, rows_in, preferred_element_type=jnp.float32).astype(
            jnp.bfloat16
        )
        outgoing = outgoing.reshape(store_count, CAP, rows_in.shape[1])
        incoming = lax.all_to_all(outgoing, "store", split_axis=0, concat_axis=0, tiled=True)
        down_sel = down_adapters[layer_index][chosen]
        rank_part = jnp.einsum(
            "scd,scdk->sck", incoming, down_sel, preferred_element_type=jnp.float32
        )
        base_part, rank_sum = reduce_pair(partial_value, rank_part)
        up_sel = up_adapters[layer_index][chosen]
        extra_rows = jnp.einsum(
            "sck,sckn->scn", rank_sum, up_sel, preferred_element_type=jnp.float32
        )
        returned = lax.all_to_all(extra_rows, "store", split_axis=0, concat_axis=0, tiled=True)
        delta_rows = returned.reshape(flat_slots, returned.shape[2])[target]
        mixed = jnp.where(local_live[:, None], base_part + delta_rows, jnp.float32(0.0))
        results.append(mixed.astype(jnp.bfloat16))
    return jnp.stack(results)


def solution(mesh):
    return jax.shard_map(
        local,
        mesh=mesh,
        in_specs=(
            P(None, ("groups", "store"), "tensor"),
            P(None, "tensor", None),
            P(None, "store", "tensor", None),
            P(None, "store", None, "tensor"),
            P(("groups", "store"), None),
            P(("groups", "store")),
            P(("groups", "store")),
        ),
        out_specs=P(None, ("groups", "store"), "tensor"),
        check_vma=False,
    )
```

profile of v0, /device:TPU:0, one launch (start us, length us, event | category | flops | bytes accessed | tf_op | source)
XLA Modules:
  0.0 121.4 jit_solution(3137350350007849416)
XLA Ops:
  7.2 1.2 %dynamic-slice = u32[1]{0:T(128)} dynamic-slice(u32[32]{0:T(128)} %constant.31, u32[]{:T(128)S(6)} %add.47), dynamic_slice_sizes={1} | dynamic-slice | bytes 12
  9.1 0.8 bitcast_dynamic-update-slice_fusion
  9.9 0.8 dynamic-update-slice.2
  10.7 0.8 dynamic-update-slice.1
  11.5 9.9 %all-reduce.3 = (s32[64]{0:T(128)S(1)}, s32[64]{0:T(128)S(1)}, s32[4]{0:T(128)S(1)}) all-reduce(s32[64]{0:T(128)S(1)} %dynamic-update-slice.2, s32[64]{0:T(128)S(1)} %bitcast_dynamic-update-slice_fusion, s32[4]{0:T(128)S(1)} %dynamic-update-slice.1), channel_id=1, replica_groups=mesh['groups'=2,'store'=4,'tensor'=4] {'store'}, use_global_device_ids=true, to_apply=%add.2 | all-reduce | flops 132 | bytes 1056
  22.6 1.1 convolution_convert_fusion.1
  24.4 3.3 %all-to-all-start = ((bf16[4,4,2048]{2,1,0:T(4,128)(2,1)}), bf16[4,4,2048]{2,1,0:T(4,128)(2,1)S(1)}, u32[]{:S(2)}, u32[]{:S(2)}) async-start(bf16[4,4,2048]{2,1,0:T(4,128)(2,1)} %reshape.81), calls=%async_computation.1 | async-start | bytes 131072 | tf_op jit(solution)/shard_map/all_to_all | solution.py:65
  27.7 5.3 %fusion.2 = f32[16,2048]{1,0:T(8,128)} fusion(bf16[2,2048,2048]{2,1,0:T(8,128)(2,1)} %param.8, bf16[2,16,2048]{2,1,0:T(8,128)(2,1)} %param.7), kind=kOutput, calls=%fused_computation.8 | convolution fusion | flops 134217728 | bytes 8585216 | tf_op jit(solution)/shard_map/dot_general | solution.py:56
  33.1 5.2 %fusion = f32[16,2048]{1,0:T(8,128)} fusion(bf16[2,2048,2048]{2,1,0:T(8,128)(2,1)} %param.8, bf16[2,16,2048]{2,1,0:T(8,128)(2,1)S(1)} %copy-done.2), kind=kOutput, calls=%fused_computation.6 | convolution fusion | flops 134217728 | bytes 8585216 | tf_op jit(solution)/shard_map/dot_general | solution.py:56
  38.9 12.1 %slice_bitcast_fusion.1 = (bf16[32,2048,64]{1,2,0:T(8,128)(2,1)}, bf16[32,2048,64]{1,2,0:T(8,128)(2,1)}) fusion(bf16[2,32,2048,64]{2,3,1,0:T(8,128)(2,1)} %param.9), kind=kLoop, calls=%fused_computation.12 | loop fusion | bytes 33554432 | tf_op jit(solution)/shard_map/squeeze | solution.py:66
  51.0 1.6 %slice_bitcast_fusion.3 = (bf16[32,64,512]{2,1,0:T(8,128)(2,1)S(1)}, bf16[32,64,512]{2,1,0:T(8,128)(2,1)}) fusion(bf16[2,32,64,512]{3,2,1,0:T(8,128)(2,1)S(1)} %copy-done.1), kind=kLoop, calls=%fused_computation.17 | loop fusion | bytes 8388608 | tf_op jit(solution)/shard_map/squeeze | solution.py:71
  52.6 6.2 %gather_fusion = bf16[16,2048,64]{1,2,0:T(8,128)(2,1)} fusion(bf16[32,2048,64]{1,2,0:T(8,128)(2,1)} %get-tuple-element.12, s32[1024]{0:T(1024)S(1)} %pad_clamp_fusion.1), kind=kCustom, calls=%fused_computation | custom fusion | bytes 8388672 | tf_op jit(solution)/shard_map/gather | solution.py:66
  58.7 6.1 %gather_fusion.3 = bf16[16,2048,64]{1,2,0:T(8,128)(2,1)} fusion(bf16[32,2048,64]{1,2,0:T(8,128)(2,1)} %get-tuple-element.13, s32[1024]{0:T(1024)S(1)} %pad_clamp_fusion.1), kind=kCustom, calls=%fused_computation.3 | custom fusion | bytes 8388672 | tf_op jit(solution)/shard_map/gather | solution.py:66
  65.5 3.2 %gather_fusion.4 = bf16[16,64,512]{2,1,0:T(8,128)(2,1)} fusion(bf16[32,64,512]{2,1,0:T(8,128)(2,1)} %get-tuple-element.15, s32[1024]{0:T(1024)S(1)} %pad_clamp_fusion.1), kind=kCustom, calls=%fused_computation.4 | custom fusion | bytes 2097216 | tf_op jit(solution)/shard_map/gather | solution.py:71
  69.4 5.2 %all-to-all-start.2 = ((bf16[4,4,2048]{2,1,0:T(4,128)(2,1)}), bf16[4,4,2048]{2,1,0:T(4,128)(2,1)S(1)}, u32[]{:S(2)}, u32[]{:S(2)}) async-start(bf16[4,4,2048]{2,1,0:T(4,128)(2,1)} %reshape.83), calls=%async_computation.4 | async-start | bytes 131072 | tf_op jit(solution)/shard_map/all_to_all | solution.py:65
  74.5 3.4 %fusion.8 = f32[4,4,1,64]{3,2,1,0:T(1,128)S(1)} fusion(bf16[4,4,2048,64]{2,3,1,0:T(8,128)(2,1)} %bitcast.71, bf16[4,4,2048,1]{2,1,0,3:T(4,128)(2,1)S(1)} %bitcast.74), kind=kOutput, calls=%fused_computation.20 | convolution fusion | flops 4194304 | bytes 4263936 | tf_op jit(solution)/shard_map/scd,scdk->sck/dot_general | solution.py:67
  77.9 2.4 %all-to-all-done.2 = bf16[4,4,2048]{2,1,0:T(4,128)(2,1)S(1)} async-done(((bf16[4,4,2048]{2,1,0:T(4,128)(2,1)}), bf16[4,4,2048]{2,1,0:T(4,128)(2,1)S(1)}, u32[]{:S(2)}, u32[]{:S(2)}) %all-to-all-start.2) | async-done | bytes 65568 | tf_op jit(solution)/shard_map/all_to_all | solution.py:65
  80.3 3.4 %fusion.6 = f32[4,4,1,64]{3,2,1,0:T(1,128)S(1)} fusion(bf16[4,4,2048,64]{2,3,1,0:T(8,128)(2,1)} %bitcast.70, bf16[4,4,2048,1]{2,1,0,3:T(4,128)(2,1)S(1)} %bitcast.75), kind=kOutput, calls=%fused_computation.18 | convolution fusion | flops 4194304 | bytes 4263936 | tf_op jit(solution)/shard_map/scd,scdk->sck/dot_general | solution.py:67
  83.7 10.2 %all-reduce.4 = (bf16[4,4,64]{2,1,0:T(4,128)(2,1)S(1)}, bf16[4,4,64]{2,1,0:T(4,128)(2,1)S(1)}) all-reduce(f32[4,4,64]{2,1,0:T(4,128)S(1)} %bitcast.79, f32[4,4,64]{2,1,0:T(4,128)S(1)} %bitcast.78), channel_id=1, replica_groups=mesh['groups'=2,'store'=4,'tensor'=4] {'tensor'}, use_global_device_ids=true, to_apply=%region_6.7 | all-reduce | flops 2048 | bytes 12288 | tf_op jit(solution)/shard_map/psum | solution.py:43
  94.7 3.3 %all-to-all-start.3 = ((f32[4,4,512]{2,1,0:T(4,128)}), f32[4,4,512]{2,1,0:T(4,128)S(1)}, u32[]{:S(2)}, u32[]{:S(2)}) async-start(f32[4,4,512]{2,1,0:T(4,128)} %bitcast.67), calls=%async_computation.5 | async-start | bytes 65536 | tf_op jit(solution)/shard_map/all_to_all | solution.py:75
  98.8 4.7 %all-to-all-done.3 = f32[4,4,512]{2,1,0:T(4,128)S(1)} async-done(((f32[4,4,512]{2,1,0:T(4,128)}), f32[4,4,512]{2,1,0:T(4,128)S(1)}, u32[]{:S(2)}, u32[]{:S(2)}) %all-to-all-start.3) | async-done | bytes 32800 | tf_op jit(solution)/shard_map/all_to_all | solution.py:75
  103.6 3.3 %all-to-all-start.1 = ((f32[4,4,512]{2,1,0:T(4,128)}), f32[4,4,512]{2,1,0:T(4,128)S(1)}, u32[]{:S(2)}, u32[]{:S(2)}) async-start(f32[4,4,512]{2,1,0:T(4,128)} %bitcast.68), calls=%async_computation.2 | async-start | bytes 65536 | tf_op jit(solution)/shard_map/all_to_all | solution.py:75
  107.5 5.0 %all-to-all-done.1 = f32[4,4,512]{2,1,0:T(4,128)S(1)} async-done(((f32[4,4,512]{2,1,0:T(4,128)}), f32[4,4,512]{2,1,0:T(4,128)S(1)}, u32[]{:S(2)}, u32[]{:S(2)}) %all-to-all-start.1) | async-done | bytes 32800 | tf_op jit(solution)/shard_map/all_to_all | solution.py:75
  113.1 0.9 fusion.21
  (43 shorter events, 7.4 us)
Async XLA Ops:
  6.5 26.5 %copy-start.2 = (bf16[2,16,2048]{2,1,0:T(8,128)(2,1)S(1)}, bf16[2,16,2048]{2,1,0:T(8,128)(2,1)}, u32[]{:S(2)}) copy-start(bf16[2,16,2048]{2,1,0:T(8,128)(2,1)} %param.7) | copy-start | bytes 393220
  24.4 45.0 %all-to-all-start = ((bf16[4,4,2048]{2,1,0:T(4,128)(2,1)}), bf16[4,4,2048]{2,1,0:T(4,128)(2,1)S(1)}, u32[]{:S(2)}, u32[]{:S(2)}) async-start(bf16[4,4,2048]{2,1,0:T(4,128)(2,1)} %reshape.81), calls=%async_computation.1 | async-start | bytes 131072 | tf_op jit(solution)/shard_map/all_to_all | solution.py:65
  27.6 85.5 %reduce-scatter.3.cloned.1.call-start = ((), (), s32[]{:S(2)}) async-start(), calls=%async_computation.6 | async-start | bytes 163840 | tf_op jit(solution)/shard_map/reduce_scatter | solution.py:42
  33.0 80.1 %reduce-scatter.5.cloned.1.call-start = ((), (), s32[]{:S(2)}) async-start(), calls=%async_computation.7 | async-start | bytes 163840 | tf_op jit(solution)/shard_map/reduce_scatter | solution.py:42
  38.9 12.1 %copy-start.1 = (bf16[2,32,64,512]{3,2,1,0:T(8,128)(2,1)S(1)}, bf16[2,32,64,512]{3,2,1,0:T(8,128)(2,1)}, u32[]{:S(2)}) copy-start(bf16[2,32,64,512]{3,2,1,0:T(8,128)(2,1)} %param.10) | copy-start | bytes 12582916
  69.4 24.5 %copy-start = (bf16[16,64,512]{2,1,0:T(8,128)(2,1)S(1)}, bf16[16,64,512]{2,1,0:T(8,128)(2,1)}, u32[]{:S(2)}) copy-start(bf16[16,64,512]{2,1,0:T(8,128)(2,1)} %gather_fusion.4) | copy-start | bytes 3145732
  69.4 10.9 %all-to-all-start.2 = ((bf16[4,4,2048]{2,1,0:T(4,128)(2,1)}), bf16[4,4,2048]{2,1,0:T(4,128)(2,1)S(1)}, u32[]{:S(2)}, u32[]{:S(2)}) async-start(bf16[4,4,2048]{2,1,0:T(4,128)(2,1)} %reshape.83), calls=%async_computation.4 | async-start | bytes 131072 | tf_op jit(solution)/shard_map/all_to_all | solution.py:65
  94.7 8.9 %all-to-all-start.3 = ((f32[4,4,512]{2,1,0:T(4,128)}), f32[4,4,512]{2,1,0:T(4,128)S(1)}, u32[]{:S(2)}, u32[]{:S(2)}) async-start(f32[4,4,512]{2,1,0:T(4,128)} %bitcast.67), calls=%async_computation.5 | async-start | bytes 65536 | tf_op jit(solution)/shard_map/all_to_all | solution.py:75
  103.6 8.9 %all-to-all-start.1 = ((f32[4,4,512]{2,1,0:T(4,128)}), f32[4,4,512]{2,1,0:T(4,128)S(1)}, u32[]{:S(2)}, u32[]{:S(2)}) async-start(f32[4,4,512]{2,1,0:T(4,128)} %bitcast.68), calls=%async_computation.2 | async-start | bytes 65536 | tf_op jit(solution)/shard_map/all_to_all | solution.py:75
Sparse Core Ops, SparseCore 0:
  33.1 20.9 reduce-scatter.2
  56.7 19.5 reduce-scatter.4
where the time goes:
time: 122 us; the launch traced here: 121 us
  local copies, waits for them, and re-layouts  37.4 us (31%)
  blocking collectives  20.1 us (16%)
  matrix products  19.1 us (16%)
  starting transfers between devices  15.1 us (12%)
  between operations  14.9 us (12%)
  waiting for transfers between devices  12.2 us (10%)
  other arithmetic  2.71 us (2%)
    gather x2, local copies, waits for them, and re-layouts, local(): down_sel = down_adapters[layer_index][chosen]  12.3 us
    squeeze x1, local copies, waits for them, and re-layouts, local(): down_sel = down_adapters[layer_index][chosen]  12.1 us
    dot_general x2, matrix products, local(): jnp.dot(rows_in, kv_weight[layer_index], preferred_element_type=jnp.float32)  10.5 us
    psum x1, blocking collectives, reduce_pair(): rank_sum = lax.psum(rank_part, 'tensor')  10.2 us
    unnamed x1, blocking collectives  9.89 us
    all_to_all x2, waiting for transfers between devices, local(): lax.all_to_all(extra_rows, 'store', split_axis=0, concat_axis=0, tiled=True)  9.75 us
    all_to_all x2, starting transfers between devices, local(): lax.all_to_all(outgoing, 'store', split_axis=0, concat_axis=0, tiled=True)  8.44 us
    dot_general x2, matrix products, local(): jnp.einsum('scd,scdk->sck', incoming, down_sel, preferred_element_type=jn...  6.75 us
  transfers between devices with their start and end apart: 6, of which 3 were waited for; matrix products, arithmetic and copies ran while one was open for 42% of the time, Pallas kernels for 0%

commit v1 on v0

v1 whole, which is shorter than its diff:
```python
import functools

import jax
import jax.numpy as jnp
from jax import lax
from jax.experimental import pallas as pl
from jax.experimental.pallas import tpu as pltpu
from jax.sharding import PartitionSpec as P

CAP = 4
HALVES = 2
LANES = 128
F32 = jnp.float32
BF16 = jnp.bfloat16
VMEM = pl.BlockSpec(memory_space=pltpu.VMEM)
SMEM = pl.BlockSpec(memory_space=pltpu.SMEM)
HBM = pl.BlockSpec(memory_space=pl.ANY)
VMEM_LIMIT = 48 * 1024 * 1024


def iota(shape, axis):
    return lax.broadcasted_iota(jnp.int32, shape, axis)


def ranks(owner_row, stores):
    rows = owner_row.shape[1]
    me = lax.axis_index("store").astype(F32)
    down, across = iota((rows, rows), 0), iota((rows, rows), 1)
    owner_row = owner_row.astype(F32)
    spread = jnp.broadcast_to(owner_row, (rows, rows))
    owner_col = jnp.sum(jnp.where(down == across, spread, 0.0), axis=1, keepdims=True)
    same = owner_col == spread
    rank_row = jnp.sum(jnp.where(same & (down < across), 1.0, 0.0), axis=0, keepdims=True)
    rank_col = jnp.sum(jnp.where(same & (across < down), 1.0, 0.0), axis=1, keepdims=True)

    def hop(owner):
        return jnp.where(owner < me, owner - me + stores, owner - me)

    return hop(owner_row), rank_row, hop(owner_col), rank_col


def prepare_kernel(stores, owner_ref, slot_ref, x_ref, *out_refs):
    layers, rows, depth = x_ref.shape
    half = depth // HALVES
    block = layers * HALVES * CAP
    hop_row, rank_row, _, _ = ranks(owner_ref[...], stores)
    place = hop_row * block + rank_row
    places = jnp.concatenate([place + CAP * part for part in range(layers * HALVES)], axis=1)
    pick = iota((stores * block, layers * HALVES * rows), 0).astype(F32) == places
    stacked = jnp.concatenate(
        [
            x_ref[layer, :, part * half : (part + 1) * half]
            for layer in range(layers)
            for part in range(HALVES)
        ],
        axis=0,
    )
    sent = jnp.dot(pick.astype(BF16), stacked, preferred_element_type=F32).astype(BF16)
    first = iota((stores * block, rows), 0).astype(F32) == place
    slots = jnp.sum(
        jnp.where(first, jnp.broadcast_to(slot_ref[...].astype(F32), first.shape), 0.0),
        axis=1,
        keepdims=True,
    )
    slots = jnp.broadcast_to(slots, (stores * block, LANES)).astype(BF16)
    for k, out_ref in enumerate(out_refs):
        out_ref[:, :half] = sent[k * block : (k + 1) * block]
        out_ref[:, half:] = slots[k * block : (k + 1) * block]


def base_kernel(tensors, step, x_ref, w_hbm, *refs):
    out_refs, (w_ref, total_ref, sems) = refs[:tensors], refs[tensors:]
    layers, _, depth = x_ref.shape
    width = out_refs[0].shape[2]
    chunks = depth // step

    def fetch(layer, chunk):
        rows = pl.ds(chunk * step, step)
        return pltpu.make_async_copy(
            w_hbm.at[layer, rows], w_ref.at[layer, rows], sems.at[layer, chunk]
        )

    for layer in range(layers):
        for chunk in range(chunks):
            fetch(layer, chunk).start()
    for layer in range(layers):
        for chunk in range(chunks):
            fetch(layer, chunk).wait()
            part = jnp.dot(
                x_ref[layer, :, chunk * step : (chunk + 1) * step],
                w_ref[layer, chunk * step : (chunk + 1) * step, :],
                preferred_element_type=F32,
            )
            if chunk == 0:
                total_ref[layer] = part
            else:
                total_ref[layer] += part
    me = lax.axis_index("tensor")
    for j, out_ref in enumerate(out_refs):
        start = pl.multiple_of(lax.rem(me + j, tensors) * width, width)
        out_ref[...] = total_ref[:, :, pl.ds(start, width)]


def slot_of(block_ref, half, place):
    return block_ref[:, half:].astype(F32)[place, 0].astype(jnp.int32)


def down_kernel(stores, down_hbm, *refs):
    block_refs, (out_ref, w_ref, sems) = refs[:stores], refs[stores:]
    layers, _, rank, depth = down_hbm.shape
    half = depth // HALVES

    def fetch(layer, k, c, slot):
        return pltpu.make_async_copy(
            down_hbm.at[layer, slot],
            w_ref.at[layer, k, pl.ds(c * rank, rank)],
            sems.at[layer, k, c],
        )

    slots = [[slot_of(block_refs[k], half, c) for c in range(CAP)] for k in range(stores)]
    for layer in range(layers):
        for k in range(stores):
            for c in range(CAP):
                fetch(layer, k, c, slots[k][c]).start()
    block = layers * HALVES * CAP
    row, column = iota((block, CAP * rank), 0), iota((block, CAP * rank), 1)
    for layer in range(layers):
        for k in range(stores):
            for c in range(CAP):
                fetch(layer, k, c, slots[k][c]).wait()
            kept = jnp.zeros((block, CAP * rank), F32)
            for part in range(HALVES):
                product = lax.dot_general(
                    block_refs[k][:, :half],
                    w_ref[layer, k, :, part * half : (part + 1) * half],
                    (((1,), (1,)), ((), ())),
                    preferred_element_type=F32,
                )
                mine = row == (layer * HALVES + part) * CAP + column // rank
                kept = kept + jnp.where(mine, product, 0.0)
            at = layer * stores + k
            out_ref[at : at + 1, :] = jnp.sum(kept, axis=0, keepdims=True)


def up_kernel(stores, tensors, half, up_hbm, *refs):
    part_refs, refs = refs[:tensors], refs[tensors:]
    block_refs, refs = refs[:stores], refs[stores:]
    out_refs, (w_ref, sems) = refs[:stores], refs[stores:]
    layers, _, rank, width = up_hbm.shape

    def fetch(layer, k, c, slot):
        return pltpu.make_async_copy(
            up_hbm.at[layer, slot],
            w_ref.at[layer, k, pl.ds(c * rank, rank)],
            sems.at[layer, k, c],
        )

    slots = [[slot_of(block_refs[k], half, c) for c in range(CAP)] for k in range(stores)]
    for layer in range(layers):
        for k in range(stores):
            for c in range(CAP):
                fetch(layer, k, c, slots[k][c]).start()
    low = part_refs[0][...]
    for part_ref in part_refs[1:]:
        low = low + part_ref[...]
    row, column = iota((2 * CAP, CAP * rank), 0), iota((2 * CAP, CAP * rank), 1)
    own = row == column // rank
    for layer in range(layers):
        for k in range(stores):
            at = layer * stores + k
            spread = jnp.where(own, jnp.broadcast_to(low[at : at + 1, :], own.shape), 0.0)
            for c in range(CAP):
                fetch(layer, k, c, slots[k][c]).wait()
            terms = jnp.dot(spread.astype(BF16), w_ref[layer, k], preferred_element_type=F32)
            out_refs[k][layer * CAP : (layer + 1) * CAP, :] = terms[:CAP]


def final_kernel(stores, tensors, count_ref, owner_ref, *refs):
    base_refs, term_refs, out_ref = refs[:tensors], refs[tensors : tensors + stores], refs[-1]
    layers, rows, _ = out_ref.shape
    _, _, hop_col, rank_col = ranks(owner_ref[...], stores)
    terms = jnp.concatenate([term_ref[...] for term_ref in term_refs], axis=0)
    live = iota((rows, 1), 0) < count_ref[0]
    for layer in range(layers):
        total = base_refs[0][layer]
        for base_ref in base_refs[1:]:
            total = total + base_ref[layer]
        place = hop_col * (layers * CAP) + layer * CAP + rank_col
        pick = iota((rows, stores * layers * CAP), 1).astype(F32) == place
        delta = jnp.dot(
            pick.astype(F32), terms, preferred_element_type=F32, precision=lax.Precision.HIGHEST
        )
        out_ref[layer] = jnp.where(live, total + delta, 0.0).astype(BF16)


def params():
    return pltpu.CompilerParams(vmem_limit_bytes=VMEM_LIMIT)


def local(stores, tensors, x, w, down, up, owner, slot, count):
    layers, rows, depth = x.shape
    adapters, rank, width = up.shape[1:]
    half = depth // HALVES
    block = layers * HALVES * CAP
    owner_row = owner.reshape(1, rows)
    slot_row = slot.reshape(1, rows)
    down = jnp.swapaxes(down, 2, 3)

    def shift(value, axis, size, by):
        if by % size == 0:
            return value
        return lax.ppermute(value, axis, [(i, (i + by) % size) for i in range(size)])

    payloads = pl.pallas_call(
        functools.partial(prepare_kernel, stores),
        out_shape=[jax.ShapeDtypeStruct((block, half + LANES), BF16)] * stores,
        in_specs=[VMEM] * 3,
        out_specs=[VMEM] * stores,
        compiler_params=params(),
        cost_estimate=pl.CostEstimate(
            flops=0, bytes_accessed=4 * layers * rows * depth, transcendentals=0
        ),
        name="prepare",
    )(owner_row, slot_row, x)
    blocks = [shift(payloads[k], "store", stores, k) for k in range(stores)]

    step = min(256, depth)
    base = pl.pallas_call(
        functools.partial(base_kernel, tensors, step),
        out_shape=[jax.ShapeDtypeStruct((layers, rows, width), F32)] * tensors,
        in_specs=[VMEM, HBM],
        out_specs=[VMEM] * tensors,
        scratch_shapes=[
            pltpu.VMEM(w.shape, BF16),
            pltpu.VMEM((layers, rows, w.shape[2]), F32),
            pltpu.SemaphoreType.DMA((layers, depth // step)),
        ],
        compiler_params=params(),
        cost_estimate=pl.CostEstimate(
            flops=2 * rows * w.size, bytes_accessed=2 * w.size, transcendentals=0
        ),
        name="base",
    )(x, w)
    sums = [shift(base[j], "tensor", tensors, j) for j in range(tensors)]

    low = pl.pallas_call(
        functools.partial(down_kernel, stores),
        out_shape=jax.ShapeDtypeStruct((layers * stores, CAP * rank), F32),
        in_specs=[HBM] + [VMEM] * stores,
        out_specs=VMEM,
        scratch_shapes=[
            pltpu.VMEM((layers, stores, CAP * rank, depth), BF16),
            pltpu.SemaphoreType.DMA((layers, stores, CAP)),
        ],
        compiler_params=params(),
        cost_estimate=pl.CostEstimate(
            flops=0, bytes_accessed=2 * layers * stores * CAP * rank * depth, transcendentals=0
        ),
        name="down",
    )(down, *blocks)
    lows = [shift(low, "tensor", tensors, j) for j in range(tensors)]

    terms = pl.pallas_call(
        functools.partial(up_kernel, stores, tensors, half),
        out_shape=[jax.ShapeDtypeStruct((layers * CAP, width), F32)] * stores,
        in_specs=[HBM] + [VMEM] * (tensors + stores),
        out_specs=[VMEM] * stores,
        scratch_shapes=[
            pltpu.VMEM((layers, stores, CAP * rank, width), BF16),
            pltpu.SemaphoreType.DMA((layers, stores, CAP)),
        ],
        compiler_params=params(),
        cost_estimate=pl.CostEstimate(
            flops=0, bytes_accessed=2 * layers * stores * CAP * rank * width, transcendentals=0
        ),
        name="up",
    )(up, *lows, *blocks)
    returned = [shift(terms[k], "store", stores, -k) for k in range(stores)]

    return pl.pallas_call(
        functools.partial(final_kernel, stores, tensors),
        out_shape=jax.ShapeDtypeStruct((layers, rows, width), BF16),
        in_specs=[SMEM] + [VMEM] * (1 + tensors + stores),
        out_specs=VMEM,
        compiler_params=params(),
        cost_estimate=pl.CostEstimate(
            flops=0, bytes_accessed=8 * layers * rows * width * tensors, transcendentals=0
        ),
        name="final",
    )(count, owner_row, *sums, *returned)


def solution(mesh):
    return jax.shard_map(
        functools.partial(local, mesh.shape["store"], mesh.shape["tensor"]),
        mesh=mesh,
        in_specs=(
            P(None, ("groups", "store"), "tensor"),
            P(None, "tensor", None),
            P(None, "store", "tensor", None),
            P(None, "store", None, "tensor"),
            P(("groups", "store"), None),
            P(("groups", "store")),
            P(("groups", "store")),
        ),
        out_specs=P(None, ("groups", "store"), "tensor"),
        check_vma=False,
    )
```

time: 122 us -> 43 us (0.35)
  local copies, waits for them, and re-layouts: 37.4 us -> 2.22 us
  blocking collectives: 20.1 us -> 0 us
  matrix products: 19.1 us -> 0 us
  Pallas kernels: 0 us -> 17.5 us
  between operations: 14.9 us -> 0.73 us
  starting transfers between devices: 15.1 us -> 12.1 us
  other arithmetic: 2.71 us -> 0 us
  waiting for transfers between devices: 12.2 us -> 10.4 us
    dot_general x8 -> x0, matrix products: 19.1 us -> none  [the longest x2 10.5 us: local(): jnp.dot(rows_in, kv_weight[layer_index], preferred_element_type=jnp.float32)]
    pallas_call x0 -> x5, Pallas kernels: none -> 17.5 us  [the longest x1 6.19 us: local(): pl.pallas_call(functools.partial(base_kernel, tensors, step), out_shape=[...]
    gather x6 -> x0, local copies, waits for them, and re-layouts: 17.3 us -> none  [the longest x2 12.3 us: local(): down_sel = down_adapters[layer_index][chosen]]
    all_to_all x4 -> x0, starting transfers between devices: 15 us -> none  [the longest x2 8.44 us: local(): lax.all_to_all(outgoing, 'store', split_axis=0, concat_axis=0, tiled=True)]
    squeeze x2 -> x0, local copies, waits for them, and re-layouts: 13.7 us -> none  [the longest x1 12.1 us: local(): down_sel = down_adapters[layer_index][chosen]]
    all_to_all x4 -> x0, waiting for transfers between devices: 12.1 us -> none  [the longest x2 9.75 us: local(): lax.all_to_all(extra_rows, 'store', split_axis=0, concat_axis=0, tiled=True)]
    ppermute x0 -> x12, starting transfers between devices: none -> 12.1 us  [shift(): lax.ppermute(value, axis, [(i, (i + by) % size) for i in range(size)])]
    ppermute x0 -> x12, waiting for transfers between devices: none -> 10.4 us  [shift(): lax.ppermute(value, axis, [(i, (i + by) % size) for i in range(size)])]
  transfers between devices with their start and end apart: 6 -> 12, of which waited for: 3 -> 5; matrix products, arithmetic and copies ran while one was open for 42% -> 0% of each run, Pallas kernels for 0% -> 38%
where the time goes in v1:
time: 43 us; the launch traced here: 42.9 us
  Pallas kernels  17.5 us (41%)
  starting transfers between devices  12.1 us (28%)
  waiting for transfers between devices  10.4 us (24%)
  local copies, waits for them, and re-layouts  2.22 us (5%)
  between operations  0.73 us (2%)
    ppermute x12, starting transfers between devices, shift(): lax.ppermute(value, axis, [(i, (i + by) % size) for i in range(size)])  12.1 us
    ppermute x12, waiting for transfers between devices, shift(): lax.ppermute(value, axis, [(i, (i + by) % size) for i in range(size)])  10.4 us
    pallas_call x1, Pallas kernels, local(): pl.pallas_call(functools.partial(base_kernel, tensors, step), out_shape=[...  6.19 us
    pallas_call x1, Pallas kernels, local(): pl.pallas_call(functools.partial(down_kernel, stores), out_shape=jax.Shap...  5.68 us
    pallas_call x1, Pallas kernels, local(): pl.pallas_call(functools.partial(up_kernel, stores, tensors, half), out_s...  4.32 us
    unnamed x8, local copies, waits for them, and re-layouts  2.22 us
    pallas_call x1, Pallas kernels, local(): pl.pallas_call(functools.partial(final_kernel, stores, tensors), out_shap...  0.98 us
  transfers between devices with their start and end apart: 12, of which 5 were waited for; matrix products, arithmetic and copies ran while one was open for 0% of the time, Pallas kernels for 38%

profile of v1, /device:TPU:0, one launch (start us, length us, event | category | flops | bytes accessed | tf_op | source)
XLA Modules:
  0.0 42.9 jit_solution(7530485855486945598)
XLA Ops:
  0.0 0.9 %copy-done.1 = bf16[2,16,2048]{2,1,0:T(8,128)(2,1)S(1)} copy-done((bf16[2,16,2048]{2,1,0:T(8,128)(2,1)S(1)}, bf16[2,16,2048]{2,1,0:T(8,128)(2,1)}, u32[]{:S(2)}) %copy-start.1) | copy-done | bytes 131096
  0.9 0.7 %copy-done.2 = s32[16,1]{0,1:T(1,128)S(1)} copy-done((s32[16,1]{0,1:T(1,128)S(1)}, s32[16,1]{0,1:T(1,128)}, u32[]{:S(2)}) %copy-start.2) | copy-done | bytes 88
  1.6 0.7 %copy-done.3 = s32[16]{0:T(128)S(1)} copy-done((s32[16]{0:T(128)S(1)}, s32[16]{0:T(128)}, u32[]{:S(2)}) %copy-start.3) | copy-done | bytes 88
  2.2 0.3 prepare.1
  2.5 3.1 %collective-permute-start.3 = (bf16[16,1152]{1,0:T(8,128)(2,1)S(1)}, bf16[16,1152]{1,0:T(8,128)(2,1)S(1)}, u32[]{:S(2)}, u32[]{:S(2)}) collective-permute-start(bf16[16,1152]{1,0:T(8,128)(2,1)S(1)} %get-tuple-element.22), channel_id=1, source_target_pairs={{0,4},{4,8},{8,12},{12,0},{1,5},{5,9},{9,13},{13,1},{2,6},{6,10},{... | collective-permute-start | bytes 110600 | tf_op jit(solution)/shard_map/ppermute | solution.py:212
  5.6 2.6 %collective-permute-start.4 = (bf16[16,1152]{1,0:T(8,128)(2,1)S(1)}, bf16[16,1152]{1,0:T(8,128)(2,1)S(1)}, u32[]{:S(2)}, u32[]{:S(2)}) collective-permute-start(bf16[16,1152]{1,0:T(8,128)(2,1)S(1)} %get-tuple-element.23), channel_id=1, source_target_pairs={{0,8},{4,12},{8,0},{12,4},{1,9},{5,13},{9,1},{13,5},{2,10},{6,14},... | collective-permute-start | bytes 110600 | tf_op jit(solution)/shard_map/ppermute | solution.py:212
  8.2 1.3 %collective-permute-start.5 = (bf16[16,1152]{1,0:T(8,128)(2,1)S(1)}, bf16[16,1152]{1,0:T(8,128)(2,1)S(1)}, u32[]{:S(2)}, u32[]{:S(2)}) collective-permute-start(bf16[16,1152]{1,0:T(8,128)(2,1)S(1)} %get-tuple-element.24), channel_id=1, source_target_pairs={{0,12},{4,0},{8,4},{12,8},{1,13},{5,1},{9,5},{13,9},{2,14},{6,2},{... | collective-permute-start | bytes 110600 | tf_op jit(solution)/shard_map/ppermute | solution.py:212
  9.6 6.2 %base.1 = (f32[2,16,512]{2,1,0:T(8,128)S(1)}, f32[2,16,512]{2,1,0:T(8,128)S(1)}, f32[2,16,512]{2,1,0:T(8,128)S(1)}, f32[2,16,512]{2,1,0:T(8,128)S(1)}) custom-call(bf16[2,16,2048]{2,1,0:T(8,128)(2,1)S(1)} %copy-done.1, bf16[2,2048,2048]{2,1,0:T(8,128)(2,1)} %w_hbm.1), custom_call_target="tpu_custom_call" | custom-call | flops 268435456 | bytes 16777216 | tf_op jit(solution)/shard_map/base/pallas_call | solution.py:228
  15.8 0.1 collective-permute-start
  15.8 1.6 %collective-permute-start.1 = (f32[2,16,512]{2,1,0:T(8,128)S(1)}, f32[2,16,512]{2,1,0:T(8,128)S(1)}, u32[]{:S(2)}, u32[]{:S(2)}) collective-permute-start(f32[2,16,512]{2,1,0:T(8,128)S(1)} %get-tuple-element.19), channel_id=1, source_target_pairs={{0,2},{1,3},{2,0},{3,1},{4,6},{5,7},{6,4},{7,5},{8,10},{9,11},{10,... | collective-permute-start | bytes 196616 | tf_op jit(solution)/shard_map/ppermute | solution.py:212
  17.4 1.4 %collective-permute-start.2 = (f32[2,16,512]{2,1,0:T(8,128)S(1)}, f32[2,16,512]{2,1,0:T(8,128)S(1)}, u32[]{:S(2)}, u32[]{:S(2)}) collective-permute-start(f32[2,16,512]{2,1,0:T(8,128)S(1)} %get-tuple-element.20), channel_id=1, source_target_pairs={{0,3},{1,0},{2,1},{3,2},{4,7},{5,4},{6,5},{7,6},{8,11},{9,8},{10,9... | collective-permute-start | bytes 196616 | tf_op jit(solution)/shard_map/ppermute | solution.py:212
  18.8 5.7 %down.1.refs_0_ = f32[8,256]{1,0:T(8,128)S(1)} custom-call(bf16[2,32,64,2048]{3,2,1,0:T(8,128)(2,1)} %bitcast.6, bf16[16,1152]{1,0:T(8,128)(2,1)S(1)} %get-tuple-element.21.refs_0_.refs_4_, bf16[16,1152]{1,0:T(8,128)(2,1)S(1)} %collective-permute-done.3.refs_1_.refs_5_, bf16[16,1152]{1,0:T(8,128)(2,1)S(1)} %collective-permute-done.4.refs_2_.refs_6_, ...), custom_call_target="tpu_custom_call" | custom-call | bytes 8388608 | tf_op jit(solution)/shard_map/down/pallas_call | solution.py:246
  24.5 0.1 collective-permute-start.6
  24.5 0.6 %collective-permute-start.7 = (f32[8,256]{1,0:T(8,128)S(1)}, f32[8,256]{1,0:T(8,128)S(1)}, u32[]{:S(2)}, u32[]{:S(2)}) collective-permute-start(f32[8,256]{1,0:T(8,128)S(1)} %down.1.refs_0_), channel_id=1, source_target_pairs={{0,2},{1,3},{2,0},{3,1},{4,6},{5,7},{6,4},{7,5},{8,10},{9,11},{10,... | collective-permute-start | bytes 24584 | tf_op jit(solution)/shard_map/ppermute | solution.py:212
  25.1 2.5 %collective-permute-done.6.refs_1_ = f32[8,256]{1,0:T(8,128)S(1)} collective-permute-done((f32[8,256]{1,0:T(8,128)S(1)}, f32[8,256]{1,0:T(8,128)S(1)}, u32[]{:S(2)}, u32[]{:S(2)}) %collective-permute-start.6) | collective-permute-done | bytes 8224 | tf_op jit(solution)/shard_map/ppermute | solution.py:212
  27.6 0.7 %collective-permute-done.7.refs_2_ = f32[8,256]{1,0:T(8,128)S(1)} collective-permute-done((f32[8,256]{1,0:T(8,128)S(1)}, f32[8,256]{1,0:T(8,128)S(1)}, u32[]{:S(2)}, u32[]{:S(2)}) %collective-permute-start.7) | collective-permute-done | bytes 8224 | tf_op jit(solution)/shard_map/ppermute | solution.py:212
  28.2 0.7 %collective-permute-done.8.refs_3_ = f32[8,256]{1,0:T(8,128)S(1)} collective-permute-done((f32[8,256]{1,0:T(8,128)S(1)}, f32[8,256]{1,0:T(8,128)S(1)}, u32[]{:S(2)}, u32[]{:S(2)}) %collective-permute-start.8) | collective-permute-done | bytes 8224 | tf_op jit(solution)/shard_map/ppermute | solution.py:212
  29.0 4.3 %up.1 = (f32[8,512]{1,0:T(8,128)S(1)}, f32[8,512]{1,0:T(8,128)S(1)}, f32[8,512]{1,0:T(8,128)S(1)}, f32[8,512]{1,0:T(8,128)S(1)}) custom-call(bf16[2,32,64,512]{3,2,1,0:T(8,128)(2,1)S(1)} %copy-done, f32[8,256]{1,0:T(8,128)S(1)} %down.1.refs_0_, f32[8,256]{1,0:T(8,128)S(1)} %collective-permute-done.6.refs_1_, f32[8,256]{1,0:T(8,128)S(1)} %collective-permute-done.7.refs_2_, ...), custom_call_target="tpu_custom_call" | custom-call | bytes 2097152 | tf_op jit(solution)/shard_map/up/pallas_call | solution.py:263
  33.3 0.1 collective-permute-start.10
  33.4 1.0 %collective-permute-start.11 = (f32[8,512]{1,0:T(8,128)S(1)}, f32[8,512]{1,0:T(8,128)S(1)}, u32[]{:S(2)}, u32[]{:S(2)}) collective-permute-start(f32[8,512]{1,0:T(8,128)S(1)} %get-tuple-element.28), channel_id=1, source_target_pairs={{0,4},{4,8},{8,12},{12,0},{1,5},{5,9},{9,13},{13,1},{2,6},{6,10},{... | collective-permute-start | bytes 49160 | tf_op jit(solution)/shard_map/ppermute | solution.py:212
  34.4 3.8 %collective-permute-done.10.refs_6_ = f32[8,512]{1,0:T(8,128)S(1)} collective-permute-done((f32[8,512]{1,0:T(8,128)S(1)}, f32[8,512]{1,0:T(8,128)S(1)}, u32[]{:S(2)}, u32[]{:S(2)}) %collective-permute-start.10) | collective-permute-done | bytes 16416 | tf_op jit(solution)/shard_map/ppermute | solution.py:212
  38.2 0.3 collective-permute-start.9
  39.1 2.8 %collective-permute-done.9.refs_5_ = f32[8,512]{1,0:T(8,128)S(1)} collective-permute-done((f32[8,512]{1,0:T(8,128)S(1)}, f32[8,512]{1,0:T(8,128)S(1)}, u32[]{:S(2)}, u32[]{:S(2)}) %collective-permute-start.9) | collective-permute-done | bytes 16416 | tf_op jit(solution)/shard_map/ppermute | solution.py:212
  41.9 1.0 %final.1 = bf16[2,16,512]{2,1,0:T(8,128)(2,1)} custom-call(s32[1]{0:T(128)S(6)} %copy.8.count_ref, s32[1,16]{1,0:T(1,128)S(1)} %bitcast.4, f32[2,16,512]{2,1,0:T(8,128)S(1)} %get-tuple-element.17.refs_0_, f32[2,16,512]{2,1,0:T(8,128)S(1)} %collective-permute-done.refs_1_, f32[2,16,512]{2,1,0:T(8,128)S(1)} %collective-permute-done.1.refs_2_, ...), custom_call_target="tpu_custom_call" | custom-call | bytes 524288 | tf_op jit(solution)/shard_map/final/pallas_call | solution.py:280
  (13 shorter events, 0.0 us)
Async XLA Ops:
  0.0 0.9 %copy-start.1 = (bf16[2,16,2048]{2,1,0:T(8,128)(2,1)S(1)}, bf16[2,16,2048]{2,1,0:T(8,128)(2,1)}, u32[]{:S(2)}) copy-start(bf16[2,16,2048]{2,1,0:T(8,128)(2,1)} %x_ref.3) | copy-start | bytes 393220
  0.9 0.7 %copy-start.2 = (s32[16,1]{0,1:T(1,128)S(1)}, s32[16,1]{0,1:T(1,128)}, u32[]{:S(2)}) copy-start(s32[16,1]{0,1:T(1,128)} %param.11) | copy-start | bytes 196
  1.6 0.7 %copy-start.3 = (s32[16]{0:T(128)S(1)}, s32[16]{0:T(128)}, u32[]{:S(2)}) copy-start(s32[16]{0:T(128)} %param.12) | copy-start | bytes 196
  2.5 14.8 %collective-permute-start.3 = (bf16[16,1152]{1,0:T(8,128)(2,1)S(1)}, bf16[16,1152]{1,0:T(8,128)(2,1)S(1)}, u32[]{:S(2)}, u32[]{:S(2)}) collective-permute-start(bf16[16,1152]{1,0:T(8,128)(2,1)S(1)} %get-tuple-element.22), channel_id=1, source_target_pairs={{0,4},{4,8},{8,12},{12,0},{1,5},{5,9},{9,13},{13,1},{2,6},{6,10},{... | collective-permute-start | bytes 110600 | tf_op jit(solution)/shard_map/ppermute | solution.py:212
  5.6 13.2 %collective-permute-start.4 = (bf16[16,1152]{1,0:T(8,128)(2,1)S(1)}, bf16[16,1152]{1,0:T(8,128)(2,1)S(1)}, u32[]{:S(2)}, u32[]{:S(2)}) collective-permute-start(bf16[16,1152]{1,0:T(8,128)(2,1)S(1)} %get-tuple-element.23), channel_id=1, source_target_pairs={{0,8},{4,12},{8,0},{12,4},{1,9},{5,13},{9,1},{13,5},{2,10},{6,14},... | collective-permute-start | bytes 110600 | tf_op jit(solution)/shard_map/ppermute | solution.py:212
  8.2 20.8 %copy-start = (bf16[2,32,64,512]{3,2,1,0:T(8,128)(2,1)S(1)}, bf16[2,32,64,512]{3,2,1,0:T(8,128)(2,1)}, u32[]{:S(2)}) copy-start(bf16[2,32,64,512]{3,2,1,0:T(8,128)(2,1)} %up_hbm.1) | copy-start | bytes 12582916
  8.2 10.6 %collective-permute-start.5 = (bf16[16,1152]{1,0:T(8,128)(2,1)S(1)}, bf16[16,1152]{1,0:T(8,128)(2,1)S(1)}, u32[]{:S(2)}, u32[]{:S(2)}) collective-permute-start(bf16[16,1152]{1,0:T(8,128)(2,1)S(1)} %get-tuple-element.24), channel_id=1, source_target_pairs={{0,12},{4,0},{8,4},{12,8},{1,13},{5,1},{9,5},{13,9},{2,14},{6,2},{... | collective-permute-start | bytes 110600 | tf_op jit(solution)/shard_map/ppermute | solution.py:212
  15.8 26.2 %collective-permute-start = (f32[2,16,512]{2,1,0:T(8,128)S(1)}, f32[2,16,512]{2,1,0:T(8,128)S(1)}, u32[]{:S(2)}, u32[]{:S(2)}) collective-permute-start(f32[2,16,512]{2,1,0:T(8,128)S(1)} %get-tuple-element.18), channel_id=1, source_target_pairs={{0,1},{1,2},{2,3},{3,0},{4,5},{5,6},{6,7},{7,4},{8,9},{9,10},{10,1... | collective-permute-start | bytes 196616 | tf_op jit(solution)/shard_map/ppermute | solution.py:212
  15.8 26.1 %collective-permute-start.1 = (f32[2,16,512]{2,1,0:T(8,128)S(1)}, f32[2,16,512]{2,1,0:T(8,128)S(1)}, u32[]{:S(2)}, u32[]{:S(2)}) collective-permute-start(f32[2,16,512]{2,1,0:T(8,128)S(1)} %get-tuple-element.19), channel_id=1, source_target_pairs={{0,2},{1,3},{2,0},{3,1},{4,6},{5,7},{6,4},{7,5},{8,10},{9,11},{10,... | collective-permute-start | bytes 196616 | tf_op jit(solution)/shard_map/ppermute | solution.py:212
  17.4 24.5 %collective-permute-start.2 = (f32[2,16,512]{2,1,0:T(8,128)S(1)}, f32[2,16,512]{2,1,0:T(8,128)S(1)}, u32[]{:S(2)}, u32[]{:S(2)}) collective-permute-start(f32[2,16,512]{2,1,0:T(8,128)S(1)} %get-tuple-element.20), channel_id=1, source_target_pairs={{0,3},{1,0},{2,1},{3,2},{4,7},{5,4},{6,5},{7,6},{8,11},{9,8},{10,9... | collective-permute-start | bytes 196616 | tf_op jit(solution)/shard_map/ppermute | solution.py:212
  24.5 3.1 %collective-permute-start.6 = (f32[8,256]{1,0:T(8,128)S(1)}, f32[8,256]{1,0:T(8,128)S(1)}, u32[]{:S(2)}, u32[]{:S(2)}) collective-permute-start(f32[8,256]{1,0:T(8,128)S(1)} %down.1.refs_0_), channel_id=1, source_target_pairs={{0,1},{1,2},{2,3},{3,0},{4,5},{5,6},{6,7},{7,4},{8,9},{9,10},{10,1... | collective-permute-start | bytes 24584 | tf_op jit(solution)/shard_map/ppermute | solution.py:212
  24.5 3.7 %collective-permute-start.7 = (f32[8,256]{1,0:T(8,128)S(1)}, f32[8,256]{1,0:T(8,128)S(1)}, u32[]{:S(2)}, u32[]{:S(2)}) collective-permute-start(f32[8,256]{1,0:T(8,128)S(1)} %down.1.refs_0_), channel_id=1, source_target_pairs={{0,2},{1,3},{2,0},{3,1},{4,6},{5,7},{6,4},{7,5},{8,10},{9,11},{10,... | collective-permute-start | bytes 24584 | tf_op jit(solution)/shard_map/ppermute | solution.py:212
  27.6 1.4 %collective-permute-start.8 = (f32[8,256]{1,0:T(8,128)S(1)}, f32[8,256]{1,0:T(8,128)S(1)}, u32[]{:S(2)}, u32[]{:S(2)}) collective-permute-start(f32[8,256]{1,0:T(8,128)S(1)} %down.1.refs_0_), channel_id=1, source_target_pairs={{0,3},{1,0},{2,1},{3,2},{4,7},{5,4},{6,5},{7,6},{8,11},{9,8},{10,9... | collective-permute-start | bytes 24584 | tf_op jit(solution)/shard_map/ppermute | solution.py:212
  33.3 4.9 %collective-permute-start.10 = (f32[8,512]{1,0:T(8,128)S(1)}, f32[8,512]{1,0:T(8,128)S(1)}, u32[]{:S(2)}, u32[]{:S(2)}) collective-permute-start(f32[8,512]{1,0:T(8,128)S(1)} %get-tuple-element.27), channel_id=1, source_target_pairs={{0,8},{4,12},{8,0},{12,4},{1,9},{5,13},{9,1},{13,5},{2,10},{6,14},... | collective-permute-start | bytes 49160 | tf_op jit(solution)/shard_map/ppermute | solution.py:212
  33.4 5.7 %collective-permute-start.11 = (f32[8,512]{1,0:T(8,128)S(1)}, f32[8,512]{1,0:T(8,128)S(1)}, u32[]{:S(2)}, u32[]{:S(2)}) collective-permute-start(f32[8,512]{1,0:T(8,128)S(1)} %get-tuple-element.28), channel_id=1, source_target_pairs={{0,4},{4,8},{8,12},{12,0},{1,5},{5,9},{9,13},{13,1},{2,6},{6,10},{... | collective-permute-start | bytes 49160 | tf_op jit(solution)/shard_map/ppermute | solution.py:212
  38.2 3.7 %collective-permute-start.9 = (f32[8,512]{1,0:T(8,128)S(1)}, f32[8,512]{1,0:T(8,128)S(1)}, u32[]{:S(2)}, u32[]{:S(2)}) collective-permute-start(f32[8,512]{1,0:T(8,128)S(1)} %get-tuple-element.26), channel_id=1, source_target_pairs={{0,12},{4,0},{8,4},{12,8},{1,13},{5,1},{9,5},{13,9},{2,14},{6,2},{... | collective-permute-start | bytes 49160 | tf_op jit(solution)/shard_map/ppermute | solution.py:212

commit v2 on v1

v2 whole, which is shorter than its diff:
```python
import functools

import jax
import jax.numpy as jnp
from jax import lax
from jax.experimental import pallas as pl
from jax.experimental.pallas import tpu as pltpu
from jax.sharding import PartitionSpec as P

CAP = 4
HALVES = 2
LANES = 128
F32 = jnp.float32
BF16 = jnp.bfloat16
VMEM = pl.BlockSpec(memory_space=pltpu.VMEM)
SMEM = pl.BlockSpec(memory_space=pltpu.SMEM)
HBM = pl.BlockSpec(memory_space=pl.ANY)
VMEM_LIMIT = 8 * 1024 * 1024


def iota(shape, axis):
    return lax.broadcasted_iota(jnp.int32, shape, axis)


def ranks(owner_row):
    rows = owner_row.shape[1]
    down, across = iota((rows, rows), 0), iota((rows, rows), 1)
    owner_row = (owner_row ^ lax.axis_index("store")).astype(F32)
    spread = jnp.broadcast_to(owner_row, (rows, rows))
    owner_col = jnp.sum(jnp.where(down == across, spread, 0.0), axis=1, keepdims=True)
    same = owner_col == spread
    rank_row = jnp.sum(jnp.where(same & (down < across), 1.0, 0.0), axis=0, keepdims=True)
    rank_col = jnp.sum(jnp.where(same & (across < down), 1.0, 0.0), axis=1, keepdims=True)
    return owner_row, rank_row, owner_col, rank_col


def prepare_kernel(stores, owner_hbm, slot_hbm, x_hbm, *refs):
    out_refs, (owner_ref, slot_ref, x_ref, sems) = refs[:stores], refs[stores:]
    pairs = ((owner_hbm, owner_ref), (slot_hbm, slot_ref), (x_hbm, x_ref))
    copies = [
        pltpu.make_async_copy(source, target, sems.at[i]) for i, (source, target) in enumerate(pairs)
    ]
    for copy in copies:
        copy.start()
    for copy in copies:
        copy.wait()
    layers, rows, depth = x_ref.shape
    half = depth // HALVES
    block = layers * HALVES * CAP
    hop_row, rank_row, _, _ = ranks(owner_ref[...])
    place = hop_row * block + rank_row
    places = jnp.concatenate([place + CAP * part for part in range(layers * HALVES)], axis=1)
    pick = iota((stores * block, layers * HALVES * rows), 0).astype(F32) == places
    stacked = jnp.concatenate(
        [
            x_ref[layer, :, part * half : (part + 1) * half]
            for layer in range(layers)
            for part in range(HALVES)
        ],
        axis=0,
    )
    sent = jnp.dot(pick.astype(BF16), stacked, preferred_element_type=F32).astype(BF16)
    first = iota((stores * block, rows), 0).astype(F32) == place
    slots = jnp.sum(
        jnp.where(first, jnp.broadcast_to(slot_ref[...].astype(F32), first.shape), 0.0),
        axis=1,
        keepdims=True,
    )
    slots = jnp.broadcast_to(slots, (stores * block, LANES)).astype(BF16)
    for k, out_ref in enumerate(out_refs):
        out_ref[:, :half] = sent[k * block : (k + 1) * block]
        out_ref[:, half:] = slots[k * block : (k + 1) * block]


def chunk_order(tensors):
    if tensors == 1:
        return [0]
    rest = [2 * mask for mask in chunk_order(tensors // 2)]
    return rest + [mask + 1 for mask in rest]


def base_kernel(tensors, _, x_ref, w_ref, keep_ref, send_ref):
    layers = x_ref.shape[0]
    width = keep_ref.shape[3]
    me = lax.axis_index("tensor")
    for i, mask in enumerate(chunk_order(tensors)):
        out_ref = keep_ref if i < tensors // 2 else send_ref
        columns = pl.ds(pl.multiple_of((me ^ mask) * width, width), width)
        for layer in range(layers):
            out_ref[i % (tensors // 2), layer] = jnp.dot(
                x_ref[layer], w_ref[layer, :, columns], preferred_element_type=F32
            )


def down_kernel(stores, down_ref, *refs):
    block_refs, (low_ref, slot_ref) = refs[:stores], refs[stores:]
    layers, _, rank, depth = down_ref.shape
    half = depth // HALVES
    block = layers * HALVES * CAP
    row, column = iota((CAP * rank, block), 0), iota((CAP * rank, block), 1)
    columns = []
    for k in range(stores):
        tail = block_refs[k][:, half:].astype(F32)
        slots = [tail[c, 0].astype(jnp.int32) for c in range(CAP)]
        for c in range(CAP):
            slot_ref[k * CAP + c] = slots[c]
        total = jnp.zeros((rank, block), F32)
        for layer in range(layers):
            for part in range(HALVES):
                span = slice(part * half, (part + 1) * half)
                chosen = jnp.concatenate([down_ref[layer, slot, :, span] for slot in slots], axis=0)
                product = lax.dot_general(
                    chosen,
                    block_refs[k][:, :half],
                    (((1,), (1,)), ((), ())),
                    preferred_element_type=F32,
                )
                mine = column == (layer * HALVES + part) * CAP + row // rank
                product = jnp.where(mine, product, 0.0)
                for c in range(CAP):
                    total = total + product[c * rank : (c + 1) * rank]
        columns.append(total)
    turned = jnp.concatenate(columns, axis=1).T
    for k in range(stores):
        for layer in range(layers):
            at = k * block + layer * HALVES * CAP
            low_ref[(k * layers + layer) * CAP : (k * layers + layer + 1) * CAP] = (
                turned[at : at + CAP] + turned[at + CAP : at + 2 * CAP]
            )


def up_kernel(stores, tensors, slot_ref, up_ref, keep_ref, got_ref, *refs):
    low_refs, refs = refs[:tensors], refs[tensors:]
    out_refs, (own_ref, send_ref) = refs[:stores], refs[stores:]
    layers, _, rank, width = up_ref.shape
    low = low_refs[0][...]
    for low_ref in low_refs[1:]:
        low = low + low_ref[...]
    row, column = iota((CAP, CAP * rank), 0), iota((CAP, CAP * rank), 1)
    for k in range(stores):
        for layer in range(layers):
            at = (k * layers + layer) * CAP
            spread = jnp.concatenate([low[at : at + CAP]] * CAP, axis=1)
            spread = jnp.where(row == column // rank, spread, 0.0).astype(BF16)
            chosen = jnp.concatenate(
                [up_ref[layer, slot_ref[k * CAP + c]] for c in range(CAP)], axis=0
            )
            out_refs[k][layer * CAP : (layer + 1) * CAP, :] = jnp.dot(
                spread, chosen, preferred_element_type=F32
            )
    own_ref[...] = keep_ref[0] + got_ref[0]
    send_ref[...] = keep_ref[1] + got_ref[1]


def final_kernel(stores, count_ref, owner_ref, own_ref, got_ref, *refs):
    term_refs, out_ref = refs[:stores], refs[-1]
    layers, rows, _ = out_ref.shape
    _, _, hop_col, rank_col = ranks(owner_ref[...])
    terms = jnp.concatenate([term_ref[...] for term_ref in term_refs], axis=0)
    live = iota((rows, 1), 0) < count_ref[0]
    for layer in range(layers):
        total = own_ref[layer] + got_ref[layer]
        place = hop_col * (layers * CAP) + layer * CAP + rank_col
        pick = iota((rows, stores * layers * CAP), 1).astype(F32) == place
        delta = jnp.dot(
            pick.astype(F32), terms, preferred_element_type=F32, precision=lax.Precision.HIGHEST
        )
        out_ref[layer] = jnp.where(live, total + delta, 0.0).astype(BF16)


def params():
    return pltpu.CompilerParams(vmem_limit_bytes=VMEM_LIMIT)


def cost(microseconds):
    return pl.CostEstimate(
        flops=int(microseconds * 1.1535e9), bytes_accessed=0, transcendentals=0
    )


def local(stores, tensors, x, w, down, up, owner, slot, count):
    layers, rows, depth = x.shape
    adapters, rank, width = up.shape[1:]
    half = depth // HALVES
    block = layers * HALVES * CAP
    owner_row = owner.reshape(1, rows)
    slot_row = slot.reshape(1, rows)
    down = jnp.swapaxes(down, 2, 3)

    def swap(value, axis, size, by):
        if by == 0:
            return value
        return lax.ppermute(value, axis, [(i, i ^ by) for i in range(size)])

    payloads = pl.pallas_call(
        functools.partial(prepare_kernel, stores),
        out_shape=[jax.ShapeDtypeStruct((block, half + LANES), BF16)] * stores,
        in_specs=[HBM] * 3,
        out_specs=[VMEM] * stores,
        scratch_shapes=[
            pltpu.VMEM((1, rows), jnp.int32),
            pltpu.VMEM((1, rows), jnp.int32),
            pltpu.VMEM(x.shape, BF16),
            pltpu.SemaphoreType.DMA((3,)),
        ],
        compiler_params=params(),
        cost_estimate=cost(6),
        name="prepare",
    )(owner_row, slot_row, x)
    blocks = [swap(payloads[k], "store", stores, k) for k in range(stores)]

    keep, send = pl.pallas_call(
        functools.partial(base_kernel, tensors),
        out_shape=[jax.ShapeDtypeStruct((tensors // 2, layers, rows, width), F32)] * 2,
        in_specs=[HBM] + [VMEM] * 2,
        out_specs=[VMEM] * 2,
        compiler_params=params(),
        cost_estimate=cost(6),
        name="base",
    )(payloads[0], x, w)
    got = swap(send, "tensor", tensors, 1)
    bit = 2
    while keep.shape[0] > 2:
        total, middle = keep + got, keep.shape[0] // 2
        keep, got = total[:middle], swap(total[middle:], "tensor", tensors, bit)
        bit *= 2

    low, slots = pl.pallas_call(
        functools.partial(down_kernel, stores),
        out_shape=[
            jax.ShapeDtypeStruct((stores * layers * CAP, rank), F32),
            jax.ShapeDtypeStruct((stores * CAP,), jnp.int32),
        ],
        in_specs=[VMEM] * (1 + stores),
        out_specs=[VMEM, SMEM],
        compiler_params=params(),
        cost_estimate=cost(4),
        name="down",
    )(down, *blocks)
    lows = [swap(low, "tensor", tensors, j) for j in range(tensors)]

    *terms, own, send = pl.pallas_call(
        functools.partial(up_kernel, stores, tensors),
        out_shape=[jax.ShapeDtypeStruct((layers * CAP, width), F32)] * stores
        + [jax.ShapeDtypeStruct((layers, rows, width), F32)] * 2,
        in_specs=[SMEM] + [VMEM] * (3 + tensors),
        out_specs=[VMEM] * (stores + 2),
        compiler_params=params(),
        cost_estimate=cost(1),
        name="up",
    )(slots, up, keep, got, *lows)
    returned = [swap(terms[k], "store", stores, k) for k in range(stores)]
    got = swap(send, "tensor", tensors, bit)

    return pl.pallas_call(
        functools.partial(final_kernel, stores),
        out_shape=jax.ShapeDtypeStruct((layers, rows, width), BF16),
        in_specs=[SMEM] + [VMEM] * (3 + stores),
        out_specs=VMEM,
        compiler_params=params(),
        cost_estimate=cost(1),
        name="final",
    )(count, owner_row, own, got, *returned)


def solution(mesh):
    return jax.shard_map(
        functools.partial(local, mesh.shape["store"], mesh.shape["tensor"]),
        mesh=mesh,
        in_specs=(
            P(None, ("groups", "store"), "tensor"),
            P(None, "tensor", None),
            P(None, "store", "tensor", None),
            P(None, "store", None, "tensor"),
            P(("groups", "store"), None),
            P(("groups", "store")),
            P(("groups", "store")),
        ),
        out_specs=P(None, ("groups", "store"), "tensor"),
        check_vma=False,
    )
```

time: 43 us -> 31.5 us (0.73)
  Pallas kernels: 17.5 us -> 7.61 us
  waiting for transfers between devices: 10.4 us -> 7.36 us
  local copies, waits for them, and re-layouts: 2.22 us -> 2.85 us
  starting transfers between devices: 12.1 us -> 12.7 us
    pallas_call x4, Pallas kernels: 17.2 us -> 7.08 us  [the longest x1 2.85 us: local(): pl.pallas_call(functools.partial(down_kernel, stores), out_shape=[jax.Sha...]
    ppermute x12 -> x11, waiting for transfers between devices: 10.4 us -> 7.36 us  [swap(): return lax.ppermute(value, axis, [(i, i ^ by) for i in range(size)])]
    ppermute x12 -> x11, starting transfers between devices: 12.1 us -> 12.7 us  [swap(): return lax.ppermute(value, axis, [(i, i ^ by) for i in range(size)])]
    unnamed x8 -> x22, local copies, waits for them, and re-layouts: 2.22 us -> 2.85 us
  transfers between devices with their start and end apart: 12 -> 11, of which waited for: 5 -> 6; matrix products, arithmetic and copies ran while one was open for 0% -> 0% of each run, Pallas kernels for 38% -> 16%
where the time goes in v2:
time: 31.5 us; the launch traced here: 31.3 us
  starting transfers between devices  12.7 us (40%)
  Pallas kernels  7.61 us (24%)
  waiting for transfers between devices  7.36 us (23%)
  local copies, waits for them, and re-layouts  2.85 us (9%)
  between operations  0.74 us (2%)
    ppermute x11, starting transfers between devices, swap(): return lax.ppermute(value, axis, [(i, i ^ by) for i in range(size)])  12.7 us
    ppermute x11, waiting for transfers between devices, swap(): return lax.ppermute(value, axis, [(i, i ^ by) for i in range(size)])  7.36 us
    unnamed x22, local copies, waits for them, and re-layouts  2.85 us
    pallas_call x1, Pallas kernels, local(): pl.pallas_call(functools.partial(down_kernel, stores), out_shape=[jax.Sha...  2.85 us
    pallas_call x1, Pallas kernels, local(): pl.pallas_call(functools.partial(base_kernel, tensors), out_shape=[jax.Sh...  2.28 us
    pallas_call x1, Pallas kernels, local(): pl.pallas_call(functools.partial(final_kernel, stores), out_shape=jax.Sha...  0.99 us
    pallas_call x1, Pallas kernels, local(): pl.pallas_call(functools.partial(up_kernel, stores, tensors), out_shape=[...  0.96 us
  transfers between devices with their start and end apart: 11, of which 6 were waited for; matrix products, arithmetic and copies ran while one was open for 0% of the time, Pallas kernels for 16%

profile of v2, /device:TPU:0, one launch (start us, length us, event | category | flops | bytes accessed | tf_op | source)
XLA Modules:
  0.0 31.3 jit_solution(15187966667146581294)
XLA Ops:
  0.0 1.1 %copy-done.2 = bf16[2,16,2048]{2,1,0:T(8,128)(2,1)S(1)} copy-done((bf16[2,16,2048]{2,1,0:T(8,128)(2,1)S(1)}, bf16[2,16,2048]{2,1,0:T(8,128)(2,1)}, u32[]{:S(2)}) %copy-start.2) | copy-done | bytes 131096
  1.1 0.8 %copy-done.4 = s32[16]{0:T(128)S(1)} copy-done((s32[16]{0:T(128)S(1)}, s32[16]{0:T(128)}, u32[]{:S(2)}) %copy-start.4) | copy-done | bytes 88
  1.9 0.9 %copy-done.5 = s32[16,1]{0,1:T(1,128)S(1)} copy-done((s32[16,1]{0,1:T(1,128)S(1)}, s32[16,1]{0,1:T(1,128)}, u32[]{:S(2)}) %copy-start.5) | copy-done | bytes 88
  2.8 0.5 %prepare.1 = (bf16[16,1152]{1,0:T(8,128)(2,1)S(1)}, bf16[16,1152]{1,0:T(8,128)(2,1)S(1)}, bf16[16,1152]{1,0:T(8,128)(2,1)S(1)}, bf16[16,1152]{1,0:T(8,128)(2,1)S(1)}) custom-call(s32[1,16]{1,0:T(1,128)S(1)} %bitcast.7, s32[1,16]{1,0:T(1,128)S(1)} %bitcast.6, bf16[2,16,2048]{2,1,0:T(8,128)(2,1)S(1)} %copy-done.2), custom_call_target="tpu_custom_call" | custom-call | flops 6920999936 | tf_op jit(solution)/shard_map/prepare/pallas_call | solution.py:195
  3.4 3.1 %collective-permute-start = (bf16[16,1152]{1,0:T(8,128)(2,1)S(1)}, bf16[16,1152]{1,0:T(8,128)(2,1)S(1)}, u32[]{:S(2)}, u32[]{:S(2)}) collective-permute-start(bf16[16,1152]{1,0:T(8,128)(2,1)S(1)} %get-tuple-element.20), channel_id=1, source_target_pairs={{0,4},{4,0},{8,12},{12,8},{1,5},{5,1},{9,13},{13,9},{2,6},{6,2},{1... | collective-permute-start | bytes 110600 | tf_op jit(solution)/shard_map/ppermute | solution.py:193
  6.5 2.6 %collective-permute-start.1 = (bf16[16,1152]{1,0:T(8,128)(2,1)S(1)}, bf16[16,1152]{1,0:T(8,128)(2,1)S(1)}, u32[]{:S(2)}, u32[]{:S(2)}) collective-permute-start(bf16[16,1152]{1,0:T(8,128)(2,1)S(1)} %get-tuple-element.21), channel_id=1, source_target_pairs={{0,8},{4,12},{8,0},{12,4},{1,9},{5,13},{9,1},{13,5},{2,10},{6,14},... | collective-permute-start | bytes 110600 | tf_op jit(solution)/shard_map/ppermute | solution.py:193
  9.1 0.0 copy-start
  9.1 2.3 %base.1 = (f32[2,2,16,512]{3,2,1,0:T(8,128)S(1)}, f32[2,2,16,512]{3,2,1,0:T(8,128)S(1)}) custom-call(bf16[16,1152]{1,0:T(8,128)(2,1)S(1)} %get-tuple-element.19.refs_0_._, bf16[2,16,2048]{2,1,0:T(8,128)(2,1)S(1)} %copy-done.3, bf16[2,2048,2048]{2,1,0:T(8,128)(2,1)S(1)} %copy-done.1), custom_call_target="tpu_custom_call" | custom-call | flops 6920999936 | tf_op jit(solution)/shard_map/base/pallas_call | solution.py:212
  11.4 0.0 collective-permute-done.refs_1_
  11.4 0.6 %collective-permute-done.1.refs_2_ = bf16[16,1152]{1,0:T(8,128)(2,1)S(1)} collective-permute-done((bf16[16,1152]{1,0:T(8,128)(2,1)S(1)}, bf16[16,1152]{1,0:T(8,128)(2,1)S(1)}, u32[]{:S(2)}, u32[]{:S(2)}) %collective-permute-start.1) | collective-permute-done | bytes 36896 | tf_op jit(solution)/shard_map/ppermute | solution.py:193
  12.0 2.8 %collective-permute-done.2.refs_3_ = bf16[16,1152]{1,0:T(8,128)(2,1)S(1)} collective-permute-done((bf16[16,1152]{1,0:T(8,128)(2,1)S(1)}, bf16[16,1152]{1,0:T(8,128)(2,1)S(1)}, u32[]{:S(2)}, u32[]{:S(2)}) %collective-permute-start.2) | collective-permute-done | bytes 36896 | tf_op jit(solution)/shard_map/ppermute | solution.py:193
  14.8 2.9 %down.1 = (f32[32,64]{1,0:T(8,128)S(1)}, s32[16]{0:T(128)S(1)}) custom-call(bf16[2,32,64,2048]{3,2,1,0:T(8,128)(2,1)S(1)} %bitcast.5, bf16[16,1152]{1,0:T(8,128)(2,1)S(1)} %get-tuple-element.19.refs_0_._, bf16[16,1152]{1,0:T(8,128)(2,1)S(1)} %collective-permute-done.refs_1_, bf16[16,1152]{1,0:T(8,128)(2,1)S(1)} %collective-permute-done.1.refs_2_, ...), custom_call_target="tpu_custom_call" | custom-call | flops 4614000128 | tf_op jit(solution)/shard_map/down/pallas_call | solution.py:228
  17.7 0.1 collective-permute-start.4
  17.8 1.6 %collective-permute-start.5 = (f32[32,64]{1,0:T(8,128)S(1)}, f32[32,64]{1,0:T(8,128)S(1)}, u32[]{:S(2)}, u32[]{:S(2)}) collective-permute-start(f32[32,64]{1,0:T(8,128)S(1)} %get-tuple-element.26.refs_0_), channel_id=1, source_target_pairs={{0,2},{1,3},{2,0},{3,1},{4,6},{5,7},{6,4},{7,5},{8,10},{9,11},{10,... | collective-permute-start | bytes 24584 | tf_op jit(solution)/shard_map/ppermute | solution.py:193
  19.3 0.3 collective-permute-start.6
  19.6 1.9 %collective-permute-done.5.refs_2_ = f32[32,64]{1,0:T(8,128)S(1)} collective-permute-done((f32[32,64]{1,0:T(8,128)S(1)}, f32[32,64]{1,0:T(8,128)S(1)}, u32[]{:S(2)}, u32[]{:S(2)}) %collective-permute-start.5) | collective-permute-done | bytes 8224 | tf_op jit(solution)/shard_map/ppermute | solution.py:193
  21.6 0.9 %collective-permute-done.6.refs_3_ = f32[32,64]{1,0:T(8,128)S(1)} collective-permute-done((f32[32,64]{1,0:T(8,128)S(1)}, f32[32,64]{1,0:T(8,128)S(1)}, u32[]{:S(2)}, u32[]{:S(2)}) %collective-permute-start.6) | collective-permute-done | bytes 8224 | tf_op jit(solution)/shard_map/ppermute | solution.py:193
  22.5 1.0 %up.1 = (f32[8,512]{1,0:T(8,128)S(1)}, f32[8,512]{1,0:T(8,128)S(1)}, f32[8,512]{1,0:T(8,128)S(1)}, f32[8,512]{1,0:T(8,128)S(1)}, f32[2,16,512]{2,1,0:T(8,128)S(1)}, /*index=5*/f32[2,16,512]{2,1,0:T(8,128)S(1)}) custom-call(s32[16]{0:T(128)S(1)} %get-tuple-element.23.slot_ref, bf16[2,32,64,512]{3,2,1,0:T(8,128)(2,1)S(1)} %copy-done, ...), custom_call_target="tpu_custom_call" | custom-call | flops 1153500032 | tf_op jit(solution)/shard_map/up/pallas_call | solution.py:242
  23.5 0.7 %collective-permute-start.7 = (f32[2,16,512]{2,1,0:T(8,128)S(1)}, f32[2,16,512]{2,1,0:T(8,128)S(1)}, u32[]{:S(2)}, u32[]{:S(2)}) collective-permute-start(f32[2,16,512]{2,1,0:T(8,128)S(1)} %get-tuple-element.28), channel_id=1, source_target_pairs={{0,2},{1,3},{2,0},{3,1},{4,6},{5,7},{6,4},{7,5},{8,10},{9,11},{10,... | collective-permute-start | bytes 196616 | tf_op jit(solution)/shard_map/ppermute | solution.py:193
  24.2 1.1 %collective-permute-start.10 = (f32[8,512]{1,0:T(8,128)S(1)}, f32[8,512]{1,0:T(8,128)S(1)}, u32[]{:S(2)}, u32[]{:S(2)}) collective-permute-start(f32[8,512]{1,0:T(8,128)S(1)} %get-tuple-element.32), channel_id=1, source_target_pairs={{0,12},{4,8},{8,4},{12,0},{1,13},{5,9},{9,5},{13,1},{2,14},{6,10},... | collective-permute-start | bytes 49160 | tf_op jit(solution)/shard_map/ppermute | solution.py:193
  25.3 3.2 %collective-permute-start.9 = (f32[8,512]{1,0:T(8,128)S(1)}, f32[8,512]{1,0:T(8,128)S(1)}, u32[]{:S(2)}, u32[]{:S(2)}) collective-permute-start(f32[8,512]{1,0:T(8,128)S(1)} %get-tuple-element.31), channel_id=1, source_target_pairs={{0,8},{4,12},{8,0},{12,4},{1,9},{5,13},{9,1},{13,5},{2,10},{6,14},... | collective-permute-start | bytes 49160 | tf_op jit(solution)/shard_map/ppermute | solution.py:193
  29.2 0.7 %collective-permute-done.10.refs_3_ = f32[8,512]{1,0:T(8,128)S(1)} collective-permute-done((f32[8,512]{1,0:T(8,128)S(1)}, f32[8,512]{1,0:T(8,128)S(1)}, u32[]{:S(2)}, u32[]{:S(2)}) %collective-permute-start.10) | collective-permute-done | bytes 16416 | tf_op jit(solution)/shard_map/ppermute | solution.py:193
  29.9 0.4 %collective-permute-done.9.refs_2_ = f32[8,512]{1,0:T(8,128)S(1)} collective-permute-done((f32[8,512]{1,0:T(8,128)S(1)}, f32[8,512]{1,0:T(8,128)S(1)}, u32[]{:S(2)}, u32[]{:S(2)}) %collective-permute-start.9) | collective-permute-done | bytes 16416 | tf_op jit(solution)/shard_map/ppermute | solution.py:193
  30.3 1.0 %final.1 = bf16[2,16,512]{2,1,0:T(8,128)(2,1)} custom-call(s32[1]{0:T(128)S(6)} %copy.8.count_ref, s32[1,16]{1,0:T(1,128)S(1)} %bitcast.8, f32[2,16,512]{2,1,0:T(8,128)S(1)} %get-tuple-element.27.own_ref, f32[2,16,512]{2,1,0:T(8,128)S(1)} %collective-permute-done.7.got_ref, f32[8,512]{1,0:T(8,128)S(1)} %get-tuple-element.29.refs_0_, ...), custom_call_target="tpu_custom_call" | custom-call | flops 1153500032 | tf_op jit(solution)/shard_map/final/pallas_call | solution.py:255
  (26 shorter events, 0.1 us)
Async XLA Ops:
  0.0 9.1 %copy-start.1 = (bf16[2,2048,2048]{2,1,0:T(8,128)(2,1)S(1)}, bf16[2,2048,2048]{2,1,0:T(8,128)(2,1)}, u32[]{:S(2)}) copy-start(bf16[2,2048,2048]{2,1,0:T(8,128)(2,1)} %w_ref.1) | copy-start | bytes 50331652
  0.0 1.1 %copy-start.2 = (bf16[2,16,2048]{2,1,0:T(8,128)(2,1)S(1)}, bf16[2,16,2048]{2,1,0:T(8,128)(2,1)}, u32[]{:S(2)}) copy-start(bf16[2,16,2048]{2,1,0:T(8,128)(2,1)} %x_ref.1) | copy-start | bytes 393220
  1.1 0.8 %copy-start.4 = (s32[16]{0:T(128)S(1)}, s32[16]{0:T(128)}, u32[]{:S(2)}) copy-start(s32[16]{0:T(128)} %param.12) | copy-start | bytes 196
  1.9 0.9 %copy-start.5 = (s32[16,1]{0,1:T(1,128)S(1)}, s32[16,1]{0,1:T(1,128)}, u32[]{:S(2)}) copy-start(s32[16,1]{0,1:T(1,128)} %param.11) | copy-start | bytes 196
  2.8 6.2 %copy-start.3 = (bf16[2,16,2048]{2,1,0:T(8,128)(2,1)S(1)}, bf16[2,16,2048]{2,1,0:T(8,128)(2,1)}, u32[]{:S(2)}) copy-start(bf16[2,16,2048]{2,1,0:T(8,128)(2,1)} %x_ref.1) | copy-start | bytes 393220
  2.8 12.0 %slice-start = ((s8[16777216]{0:T(1024)(128)(4,1)}), s8[4194304]{0:T(1024)(128)(4,1)S(1)}, s32[]{:S(2)}) async-start(s8[16777216]{0:T(1024)(128)(4,1)} %bitcast.3), calls=%async_computation | async-start | bytes 8388608
  2.8 12.0 %slice-start.1 = ((s8[16777216]{0:T(1024)(128)(4,1)}), s8[4194304]{0:T(1024)(128)(4,1)S(1)}, s32[]{:S(2)}) async-start(s8[16777216]{0:T(1024)(128)(4,1)} %bitcast.3), calls=%async_computation.1 | async-start | bytes 8388608
  3.4 8.0 %collective-permute-start = (bf16[16,1152]{1,0:T(8,128)(2,1)S(1)}, bf16[16,1152]{1,0:T(8,128)(2,1)S(1)}, u32[]{:S(2)}, u32[]{:S(2)}) collective-permute-start(bf16[16,1152]{1,0:T(8,128)(2,1)S(1)} %get-tuple-element.20), channel_id=1, source_target_pairs={{0,4},{4,0},{8,12},{12,8},{1,5},{5,1},{9,13},{13,9},{2,6},{6,2},{1... | collective-permute-start | bytes 110600 | tf_op jit(solution)/shard_map/ppermute | solution.py:193
  6.5 5.5 %collective-permute-start.1 = (bf16[16,1152]{1,0:T(8,128)(2,1)S(1)}, bf16[16,1152]{1,0:T(8,128)(2,1)S(1)}, u32[]{:S(2)}, u32[]{:S(2)}) collective-permute-start(bf16[16,1152]{1,0:T(8,128)(2,1)S(1)} %get-tuple-element.21), channel_id=1, source_target_pairs={{0,8},{4,12},{8,0},{12,4},{1,9},{5,13},{9,1},{13,5},{2,10},{6,14},... | collective-permute-start | bytes 110600 | tf_op jit(solution)/shard_map/ppermute | solution.py:193
  9.0 5.8 %slice-start.2 = ((s8[16777216]{0:T(1024)(128)(4,1)}), s8[4194304]{0:T(1024)(128)(4,1)S(1)}, s32[]{:S(2)}) async-start(s8[16777216]{0:T(1024)(128)(4,1)} %bitcast.3), calls=%async_computation.2 | async-start | bytes 8388608
  9.0 5.8 %collective-permute-start.2 = (bf16[16,1152]{1,0:T(8,128)(2,1)S(1)}, bf16[16,1152]{1,0:T(8,128)(2,1)S(1)}, u32[]{:S(2)}, u32[]{:S(2)}) collective-permute-start(bf16[16,1152]{1,0:T(8,128)(2,1)S(1)} %get-tuple-element.22), channel_id=1, source_target_pairs={{0,12},{4,8},{8,4},{12,0},{1,13},{5,9},{9,5},{13,1},{2,14},{6,10},... | collective-permute-start | bytes 110600 | tf_op jit(solution)/shard_map/ppermute | solution.py:193
  9.1 5.8 %slice-start.3 = ((s8[16777216]{0:T(1024)(128)(4,1)}), s8[4194304]{0:T(1024)(128)(4,1)S(1)}, s32[]{:S(2)}) async-start(s8[16777216]{0:T(1024)(128)(4,1)} %bitcast.3), calls=%async_computation.3 | async-start | bytes 8388608
  9.1 13.4 %copy-start = (bf16[2,32,64,512]{3,2,1,0:T(8,128)(2,1)S(1)}, bf16[2,32,64,512]{3,2,1,0:T(8,128)(2,1)}, u32[]{:S(2)}) copy-start(bf16[2,32,64,512]{3,2,1,0:T(8,128)(2,1)} %up_ref.1) | copy-start | bytes 12582916
  11.4 18.9 %copy-start.6 = (s32[16,1]{0,1:T(1,128)S(1)}, s32[16,1]{0,1:T(1,128)}, u32[]{:S(2)}) copy-start(s32[16,1]{0,1:T(1,128)} %param.11) | copy-start | bytes 196
  11.4 11.1 %collective-permute-start.3 = (f32[2,2,16,512]{3,2,1,0:T(8,128)S(1)}, f32[2,2,16,512]{3,2,1,0:T(8,128)S(1)}, u32[]{:S(2)}, u32[]{:S(2)}) collective-permute-start(f32[2,2,16,512]{3,2,1,0:T(8,128)S(1)} %get-tuple-element.25), channel_id=1, source_target_pairs={{0,1},{1,0},{2,3},{3,2},{4,5},{5,4},{6,7},{7,6},{8,9},{9,8},{10,11... | collective-permute-start | bytes 393224 | tf_op jit(solution)/shard_map/ppermute | solution.py:193
  17.7 1.9 %collective-permute-start.4 = (f32[32,64]{1,0:T(8,128)S(1)}, f32[32,64]{1,0:T(8,128)S(1)}, u32[]{:S(2)}, u32[]{:S(2)}) collective-permute-start(f32[32,64]{1,0:T(8,128)S(1)} %get-tuple-element.26.refs_0_), channel_id=1, source_target_pairs={{0,1},{1,0},{2,3},{3,2},{4,5},{5,4},{6,7},{7,6},{8,9},{9,8},{10,11... | collective-permute-start | bytes 24584 | tf_op jit(solution)/shard_map/ppermute | solution.py:193
  17.8 3.8 %collective-permute-start.5 = (f32[32,64]{1,0:T(8,128)S(1)}, f32[32,64]{1,0:T(8,128)S(1)}, u32[]{:S(2)}, u32[]{:S(2)}) collective-permute-start(f32[32,64]{1,0:T(8,128)S(1)} %get-tuple-element.26.refs_0_), channel_id=1, source_target_pairs={{0,2},{1,3},{2,0},{3,1},{4,6},{5,7},{6,4},{7,5},{8,10},{9,11},{10,... | collective-permute-start | bytes 24584 | tf_op jit(solution)/shard_map/ppermute | solution.py:193
  19.3 3.2 %collective-permute-start.6 = (f32[32,64]{1,0:T(8,128)S(1)}, f32[32,64]{1,0:T(8,128)S(1)}, u32[]{:S(2)}, u32[]{:S(2)}) collective-permute-start(f32[32,64]{1,0:T(8,128)S(1)} %get-tuple-element.26.refs_0_), channel_id=1, source_target_pairs={{0,3},{1,2},{2,1},{3,0},{4,7},{5,6},{6,5},{7,4},{8,11},{9,10},{10,... | collective-permute-start | bytes 24584 | tf_op jit(solution)/shard_map/ppermute | solution.py:193
  23.5 6.8 %collective-permute-start.7 = (f32[2,16,512]{2,1,0:T(8,128)S(1)}, f32[2,16,512]{2,1,0:T(8,128)S(1)}, u32[]{:S(2)}, u32[]{:S(2)}) collective-permute-start(f32[2,16,512]{2,1,0:T(8,128)S(1)} %get-tuple-element.28), channel_id=1, source_target_pairs={{0,2},{1,3},{2,0},{3,1},{4,6},{5,7},{6,4},{7,5},{8,10},{9,11},{10,... | collective-permute-start | bytes 196616 | tf_op jit(solution)/shard_map/ppermute | solution.py:193
  24.2 5.7 %collective-permute-start.10 = (f32[8,512]{1,0:T(8,128)S(1)}, f32[8,512]{1,0:T(8,128)S(1)}, u32[]{:S(2)}, u32[]{:S(2)}) collective-permute-start(f32[8,512]{1,0:T(8,128)S(1)} %get-tuple-element.32), channel_id=1, source_target_pairs={{0,12},{4,8},{8,4},{12,0},{1,13},{5,9},{9,5},{13,1},{2,14},{6,10},... | collective-permute-start | bytes 49160 | tf_op jit(solution)/shard_map/ppermute | solution.py:193
  25.3 4.6 %collective-permute-start.8 = (f32[8,512]{1,0:T(8,128)S(1)}, f32[8,512]{1,0:T(8,128)S(1)}, u32[]{:S(2)}, u32[]{:S(2)}) collective-permute-start(f32[8,512]{1,0:T(8,128)S(1)} %get-tuple-element.30), channel_id=1, source_target_pairs={{0,4},{4,0},{8,12},{12,8},{1,5},{5,1},{9,13},{13,9},{2,6},{6,2},{1... | collective-permute-start | bytes 49160 | tf_op jit(solution)/shard_map/ppermute | solution.py:193
  25.3 5.0 %collective-permute-start.9 = (f32[8,512]{1,0:T(8,128)S(1)}, f32[8,512]{1,0:T(8,128)S(1)}, u32[]{:S(2)}, u32[]{:S(2)}) collective-permute-start(f32[8,512]{1,0:T(8,128)S(1)} %get-tuple-element.31), channel_id=1, source_target_pairs={{0,8},{4,12},{8,0},{12,4},{1,9},{5,13},{9,1},{13,5},{2,10},{6,14},... | collective-permute-start | bytes 49160 | tf_op jit(solution)/shard_map/ppermute | solution.py:193

commit v3 on v2

--- a/solution.py
+++ b/solution.py
@@ -10,12 +10,15 @@
 CAP = 4
 HALVES = 2
 LANES = 128
+PIECES = 3
 F32 = jnp.float32
 BF16 = jnp.bfloat16
 VMEM = pl.BlockSpec(memory_space=pltpu.VMEM)
 SMEM = pl.BlockSpec(memory_space=pltpu.SMEM)
-HBM = pl.BlockSpec(memory_space=pl.ANY)
-VMEM_LIMIT = 8 * 1024 * 1024
+HBM = pl.BlockSpec(memory_space=pltpu.HBM)
+ANY = pl.BlockSpec(memory_space=pl.ANY)
+SMALL = 8 * 1024 * 1024
+LARGE = 48 * 1024 * 1024
 
 
 def iota(shape, axis):
@@ -35,7 +38,7 @@
 
 
 def prepare_kernel(stores, owner_hbm, slot_hbm, x_hbm, *refs):
-    out_refs, (owner_ref, slot_ref, x_ref, sems) = refs[:stores], refs[stores:]
+    out_refs, (pick_ref, owner_ref, slot_ref, x_ref, sems) = refs[:stores], refs[stores:]
     pairs = ((owner_hbm, owner_ref), (slot_hbm, slot_ref), (x_hbm, x_ref))
     copies = [
         pltpu.make_async_copy(source, target, sems.at[i]) for i, (source, target) in enumerate(pairs)
@@ -47,7 +50,7 @@
     layers, rows, depth = x_ref.shape
     half = depth // HALVES
     block = layers * HALVES * CAP
-    hop_row, rank_row, _, _ = ranks(owner_ref[...])
+    hop_row, rank_row, hop_col, rank_col = ranks(owner_ref[...])
     place = hop_row * block + rank_row
     places = jnp.concatenate([place + CAP * part for part in range(layers * HALVES)], axis=1)
     pick = iota((stores * block, layers * HALVES * rows), 0).astype(F32) == places
@@ -70,6 +73,10 @@
     for k, out_ref in enumerate(out_refs):
         out_ref[:, :half] = sent[k * block : (k + 1) * block]
         out_ref[:, half:] = slots[k * block : (k + 1) * block]
+    spots = lax.rem(iota((rows, pick_ref.shape[1]), 1), stores * layers * CAP).astype(F32)
+    place = hop_col * (layers * CAP) + rank_col
+    for layer in range(layers):
+        pick_ref[layer * rows : (layer + 1) * rows] = (spots == place + layer * CAP).astype(BF16)
 
 
 def chunk_order(tensors):
@@ -92,25 +99,38 @@
             )
 
 
-def down_kernel(stores, down_ref, *refs):
-    block_refs, (low_ref, slot_ref) = refs[:stores], refs[stores:]
-    layers, _, rank, depth = down_ref.shape
+def down_kernel(stores, down_hbm, *refs):
+    block_refs, (low_ref, slot_ref, w_ref, sems) = refs[:stores], refs[stores:]
+    layers, _, rank, depth = down_hbm.shape
     half = depth // HALVES
     block = layers * HALVES * CAP
+
+    def fetch(layer, k, c, slot):
+        return pltpu.make_async_copy(
+            down_hbm.at[layer, slot],
+            w_ref.at[layer, k, pl.ds(c * rank, rank)],
+            sems.at[layer, k, c],
+        )
+
+    slots = []
+    for k in range(stores):
+        tail = block_refs[k][:, half:].astype(F32)
+        slots.append([tail[c, 0].astype(jnp.int32) for c in range(CAP)])
+        for c in range(CAP):
+            slot_ref[k * CAP + c] = slots[k][c]
+            for layer in range(layers):
+                fetch(layer, k, c, slots[k][c]).start()
     row, column = iota((CAP * rank, block), 0), iota((CAP * rank, block), 1)
     columns = []
     for k in range(stores):
-        tail = block_refs[k][:, half:].astype(F32)
-        slots = [tail[c, 0].astype(jnp.int32) for c in range(CAP)]
         for c in range(CAP):
-            slot_ref[k * CAP + c] = slots[c]
+            for layer in range(layers):
+                fetch(layer, k, c, slots[k][c]).wait()
         total = jnp.zeros((rank, block), F32)
         for layer in range(layers):
             for part in range(HALVES):
-                span = slice(part * half, (part + 1) * half)
-                chosen = jnp.concatenate([down_ref[layer, slot, :, span] for slot in slots], axis=0)
                 product = lax.dot_general(
-                    chosen,
+                    w_ref[layer, k, :, part * half : (part + 1) * half],
                     block_refs[k][:, :half],
                     (((1,), (1,)), ((), ())),
                     preferred_element_type=F32,
@@ -129,9 +149,13 @@
             )
 
 
-def up_kernel(stores, tensors, slot_ref, up_ref, keep_ref, got_ref, *refs):
-    low_refs, refs = refs[:tensors], refs[tensors:]
-    out_refs, (own_ref, send_ref) = refs[:stores], refs[stores:]
+def pair_kernel(_, keep_ref, got_ref, own_ref, send_ref):
+    own_ref[...] = keep_ref[0] + got_ref[0]
+    send_ref[...] = keep_ref[1] + got_ref[1]
+
+
+def up_kernel(stores, tensors, _, slot_ref, up_ref, *refs):
+    low_refs, out_refs = refs[:tensors], refs[tensors:]
     layers, _, rank, width = up_ref.shape
     low = low_refs[0][...]
     for low_ref in low_refs[1:]:
@@ -148,28 +172,27 @@
             out_refs[k][layer * CAP : (layer + 1) * CAP, :] = jnp.dot(
                 spread, chosen, preferred_element_type=F32
             )
-    own_ref[...] = keep_ref[0] + got_ref[0]
-    send_ref[...] = keep_ref[1] + got_ref[1]
-
-
-def final_kernel(stores, count_ref, owner_ref, own_ref, got_ref, *refs):
-    term_refs, out_ref = refs[:stores], refs[-1]
+
+
+def final_kernel(count_ref, pick_ref, own_ref, got_ref, *refs):
+    term_refs, out_ref = refs[:-1], refs[-1]
     layers, rows, _ = out_ref.shape
-    _, _, hop_col, rank_col = ranks(owner_ref[...])
     terms = jnp.concatenate([term_ref[...] for term_ref in term_refs], axis=0)
+    pieces = []
+    for _ in range(PIECES):
+        pieces.append(terms.astype(BF16))
+        terms = terms - pieces[-1].astype(F32)
+    delta = jnp.dot(
+        pick_ref[...], jnp.concatenate(pieces, axis=0), preferred_element_type=F32
+    )
     live = iota((rows, 1), 0) < count_ref[0]
     for layer in range(layers):
-        total = own_ref[layer] + got_ref[layer]
-        place = hop_col * (layers * CAP) + layer * CAP + rank_col
-        pick = iota((rows, stores * layers * CAP), 1).astype(F32) == place
-        delta = jnp.dot(
-            pick.astype(F32), terms, preferred_element_type=F32, precision=lax.Precision.HIGHEST
-        )
-        out_ref[layer] = jnp.where(live, total + delta, 0.0).astype(BF16)
-
-
-def params():
-    return pltpu.CompilerParams(vmem_limit_bytes=VMEM_LIMIT)
+        total = own_ref[layer] + got_ref[layer] + delta[layer * rows : (layer + 1) * rows]
+        out_ref[layer] = jnp.where(live, total, 0.0).astype(BF16)
+
+
+def params(limit=SMALL):
+    return pltpu.CompilerParams(vmem_limit_bytes=limit)
 
 
 def cost(microseconds):
@@ -192,11 +215,14 @@
             return value
         return lax.ppermute(value, axis, [(i, i ^ by) for i in range(size)])
 
-    payloads = pl.pallas_call(
+    *payloads, pick = pl.pallas_call(
         functools.partial(prepare_kernel, stores),
-        out_shape=[jax.ShapeDtypeStruct((block, half + LANES), BF16)] * stores,
-        in_specs=[HBM] * 3,
-        out_specs=[VMEM] * stores,
+        out_shape=[jax.ShapeDtypeStruct((block, half + LANES), BF16)] * stores
+        + [
+            jax.ShapeDtypeStruct((layers * rows, PIECES * stores * layers * CAP), BF16),
+        ],
+        in_specs=[ANY] * 3,
+        out_specs=[VMEM] * (stores + 1),
         scratch_shapes=[
             pltpu.VMEM((1, rows), jnp.int32),
             pltpu.VMEM((1, rows), jnp.int32),
@@ -206,13 +232,13 @@
         compiler_params=params(),
         cost_estimate=cost(6),
         name="prepare",
-    )(owner_row, slot_row, x)
+    )(*(pltpu.with_memory_space_constraint(v, pltpu.HBM) for v in (owner_row, slot_row, x)))
     blocks = [swap(payloads[k], "store", stores, k) for k in range(stores)]
 
     keep, send = pl.pallas_call(
         functools.partial(base_kernel, tensors),
         out_shape=[jax.ShapeDtypeStruct((tensors // 2, layers, rows, width), F32)] * 2,
-        in_specs=[HBM] + [VMEM] * 2,
+        in_specs=[ANY] + [VMEM] * 2,
         out_specs=[VMEM] * 2,
         compiler_params=params(),
         cost_estimate=cost(6),
@@ -231,36 +257,48 @@
             jax.ShapeDtypeStruct((stores * layers * CAP, rank), F32),
             jax.ShapeDtypeStruct((stores * CAP,), jnp.int32),
         ],
-        in_specs=[VMEM] * (1 + stores),
+        in_specs=[HBM] + [VMEM] * stores,
         out_specs=[VMEM, SMEM],
-        compiler_params=params(),
+        scratch_shapes=[
+            pltpu.VMEM((layers, stores, CAP * rank, depth), BF16),
+            pltpu.SemaphoreType.DMA((layers, stores, CAP)),
+        ],
+        compiler_params=params(LARGE),
         cost_estimate=cost(4),
         name="down",
     )(down, *blocks)
     lows = [swap(low, "tensor", tensors, j) for j in range(tensors)]
-
-    *terms, own, send = pl.pallas_call(
+    own, send = pl.pallas_call(
+        pair_kernel,
+        out_shape=[jax.ShapeDtypeStruct((layers, rows, width), F32)] * 2,
+        in_specs=[ANY] + [VMEM] * 2,
+        out_specs=[VMEM] * 2,
+        compiler_params=params(),
+        cost_estimate=cost(0.3),
+        name="pair",
+    )(low, keep, got)
+    got = swap(send, "tensor", tensors, bit)
+
+    terms = pl.pallas_call(
         functools.partial(up_kernel, stores, tensors),
-        out_shape=[jax.ShapeDtypeStruct((layers * CAP, width), F32)] * stores
-        + [jax.ShapeDtypeStruct((layers, rows, width), F32)] * 2,
-        in_specs=[SMEM] + [VMEM] * (3 + tensors),
-        out_specs=[VMEM] * (stores + 2),
+        out_shape=[jax.ShapeDtypeStruct((layers * CAP, width), F32)] * stores,
+        in_specs=[ANY, SMEM] + [VMEM] * (1 + tensors),
+        out_specs=[VMEM] * stores,
         compiler_params=params(),
         cost_estimate=cost(1),
         name="up",
-    )(slots, up, keep, got, *lows)
+    )(own, slots, up, *lows)
     returned = [swap(terms[k], "store", stores, k) for k in range(stores)]
-    got = swap(send, "tensor", tensors, bit)
 
     return pl.pallas_call(
-        functools.partial(final_kernel, stores),
+        final_kernel,
         out_shape=jax.ShapeDtypeStruct((layers, rows, width), BF16),
         in_specs=[SMEM] + [VMEM] * (3 + stores),
         out_specs=VMEM,
         compiler_params=params(),
         cost_estimate=cost(1),
         name="final",
-    )(count, owner_row, own, got, *returned)
+    )(count, pick, own, got, *returned)
 
 
 def solution(mesh):

time: 31.5 us -> 31 us (0.984)
  Pallas kernels: 7.61 us -> 10.9 us
  local copies, waits for them, and re-layouts: 2.85 us -> 0.01 us
  waiting for transfers between devices: 7.36 us -> 5.79 us
  starting transfers between devices: 12.7 us -> 13.6 us
    unnamed x22 -> x6, local copies, waits for them, and re-layouts: 2.85 us -> 0.01 us
    pallas_call x1, Pallas kernels: 2.85 us -> 5.43 us  [local(): pl.pallas_call(functools.partial(down_kernel, stores), out_shape=[jax.Sha...]
    ppermute x11, waiting for transfers between devices: 7.36 us -> 5.79 us  [swap(): return lax.ppermute(value, axis, [(i, i ^ by) for i in range(size)])]
    pallas_call x1, Pallas kernels: 0.53 us -> 1.44 us  [local(): pl.pallas_call(functools.partial(prepare_kernel, stores), out_shape=[jax....]
    ppermute x11, starting transfers between devices: 12.7 us -> 13.6 us  [swap(): return lax.ppermute(value, axis, [(i, i ^ by) for i in range(size)])]
    pallas_call x1 -> x2, Pallas kernels: 0.99 us -> 0.77 us  [the longest x1 0.75 us: local(): pl.pallas_call(final_kernel, out_shape=jax.ShapeDtypeStruct((layers, rows...]
  transfers between devices with their start and end apart: 11 -> 11, of which waited for: 6 -> 6; matrix products, arithmetic and copies ran while one was open for 0% -> 0% of each run, Pallas kernels for 16% -> 28%
where the time goes in v3:
time: 31 us
  starting transfers between devices  13.6 us (44%)
  Pallas kernels  10.9 us (35%)
  waiting for transfers between devices  5.79 us (19%)
  between operations  0.7 us (2%)
    ppermute x11, starting transfers between devices, swap(): return lax.ppermute(value, axis, [(i, i ^ by) for i in range(size)])  13.6 us
    ppermute x11, waiting for transfers between devices, swap(): return lax.ppermute(value, axis, [(i, i ^ by) for i in range(size)])  5.79 us
    pallas_call x1, Pallas kernels, local(): pl.pallas_call(functools.partial(down_kernel, stores), out_shape=[jax.Sha...  5.43 us
    pallas_call x1, Pallas kernels, local(): pl.pallas_call(functools.partial(base_kernel, tensors), out_shape=[jax.Sh...  2.28 us
    pallas_call x1, Pallas kernels, local(): pl.pallas_call(functools.partial(prepare_kernel, stores), out_shape=[jax....  1.44 us
    pallas_call x1, Pallas kernels, local(): pl.pallas_call(functools.partial(up_kernel, stores, tensors), out_shape=[...  0.95 us
    pallas_call x1, Pallas kernels, local(): pl.pallas_call(final_kernel, out_shape=jax.ShapeDtypeStruct((layers, rows...  0.75 us
  transfers between devices with their start and end apart: 11, of which 6 were waited for; matrix products, arithmetic and copies ran while one was open for 0% of the time, Pallas kernels for 28%

profile of v3, /device:TPU:0, one launch (start us, length us, event | category | flops | bytes accessed | tf_op | source)
XLA Modules:
  0.0 31.0 jit_solution(8825460913593888907)
XLA Ops:
  0.0 1.4 %prepare.1 = (bf16[16,1152]{1,0:T(8,128)(2,1)S(1)}, bf16[16,1152]{1,0:T(8,128)(2,1)S(1)}, bf16[16,1152]{1,0:T(8,128)(2,1)S(1)}, bf16[16,1152]{1,0:T(8,128)(2,1)S(1)}, bf16[32,96]{1,0:T(8,128)(2,1)S(1)}) custom-call(s32[1,16]{1,0:T(1,128)} %bitcast.4, s32[1,16]{1,0:T(1,128)} %bitcast.5, bf16[2,16,2048]{2,1,0:T(8,128)(2,1)} %x_ref.1), custom_call_target="tpu_custom_call" | custom-call | flops 6920999936 | tf_op jit(solution)/shard_map/prepare/pallas_call | solution.py:218
  1.5 3.1 %collective-permute-start = (bf16[16,1152]{1,0:T(8,128)(2,1)S(1)}, bf16[16,1152]{1,0:T(8,128)(2,1)S(1)}, u32[]{:S(2)}, u32[]{:S(2)}) collective-permute-start(bf16[16,1152]{1,0:T(8,128)(2,1)S(1)} %get-tuple-element.22), channel_id=1, source_target_pairs={{0,4},{4,0},{8,12},{12,8},{1,5},{5,1},{9,13},{13,9},{2,6},{6,2},{1... | collective-permute-start | bytes 110600 | tf_op jit(solution)/shard_map/ppermute | solution.py:216
  4.5 2.6 %collective-permute-start.1 = (bf16[16,1152]{1,0:T(8,128)(2,1)S(1)}, bf16[16,1152]{1,0:T(8,128)(2,1)S(1)}, u32[]{:S(2)}, u32[]{:S(2)}) collective-permute-start(bf16[16,1152]{1,0:T(8,128)(2,1)S(1)} %get-tuple-element.23), channel_id=1, source_target_pairs={{0,8},{4,12},{8,0},{12,4},{1,9},{5,13},{9,1},{13,5},{2,10},{6,14},... | collective-permute-start | bytes 110600 | tf_op jit(solution)/shard_map/ppermute | solution.py:216
  7.1 0.0 collective-permute-start.2
  7.1 0.0 copy-start
  7.2 2.3 %base.1 = (f32[2,2,16,512]{3,2,1,0:T(8,128)S(1)}, f32[2,2,16,512]{3,2,1,0:T(8,128)S(1)}) custom-call(bf16[16,1152]{1,0:T(8,128)(2,1)S(1)} %get-tuple-element.21.refs_0_._, bf16[2,16,2048]{2,1,0:T(8,128)(2,1)S(1)} %copy-done.2, bf16[2,2048,2048]{2,1,0:T(8,128)(2,1)S(1)} %copy-done.1), custom_call_target="tpu_custom_call" | custom-call | flops 6920999936 | tf_op jit(solution)/shard_map/base/pallas_call | solution.py:238
  9.4 0.6 %collective-permute-done.1.refs_2_ = bf16[16,1152]{1,0:T(8,128)(2,1)S(1)} collective-permute-done((bf16[16,1152]{1,0:T(8,128)(2,1)S(1)}, bf16[16,1152]{1,0:T(8,128)(2,1)S(1)}, u32[]{:S(2)}, u32[]{:S(2)}) %collective-permute-start.1) | collective-permute-done | bytes 36896 | tf_op jit(solution)/shard_map/ppermute | solution.py:216
  10.1 2.8 %collective-permute-done.2.refs_3_ = bf16[16,1152]{1,0:T(8,128)(2,1)S(1)} collective-permute-done((bf16[16,1152]{1,0:T(8,128)(2,1)S(1)}, bf16[16,1152]{1,0:T(8,128)(2,1)S(1)}, u32[]{:S(2)}, u32[]{:S(2)}) %collective-permute-start.2) | collective-permute-done | bytes 36896 | tf_op jit(solution)/shard_map/ppermute | solution.py:216
  12.9 5.4 %down.1 = (f32[32,64]{1,0:T(8,128)S(1)}, s32[16]{0:T(128)S(1)}) custom-call(bf16[2,32,64,2048]{3,2,1,0:T(8,128)(2,1)} %bitcast.3, bf16[16,1152]{1,0:T(8,128)(2,1)S(1)} %get-tuple-element.21.refs_0_._, bf16[16,1152]{1,0:T(8,128)(2,1)S(1)} %collective-permute-done.refs_1_, bf16[16,1152]{1,0:T(8,128)(2,1)S(1)} %collective-permute-done.1.refs_2_, ...), custom_call_target="tpu_custom_call" | custom-call | flops 4614000128 | tf_op jit(solution)/shard_map/down/pallas_call | solution.py:254
  18.3 0.1 collective-permute-start.5
  18.4 1.6 %collective-permute-start.6 = (f32[32,64]{1,0:T(8,128)S(1)}, f32[32,64]{1,0:T(8,128)S(1)}, u32[]{:S(2)}, u32[]{:S(2)}) collective-permute-start(f32[32,64]{1,0:T(8,128)S(1)} %get-tuple-element.25._.refs_0_), channel_id=1, source_target_pairs={{0,2},{1,3},{2,0},{3,1},{4,6},{5,7},{6,4},{7,5},{8,10},{9,11},{10,... | collective-permute-start | bytes 24584 | tf_op jit(solution)/shard_map/ppermute | solution.py:216
  20.0 0.3 collective-permute-start.7
  20.3 0.0 collective-permute-done.3.got_ref
  20.3 1.6 %collective-permute-start.4 = (f32[2,16,512]{2,1,0:T(8,128)S(1)}, f32[2,16,512]{2,1,0:T(8,128)S(1)}, u32[]{:S(2)}, u32[]{:S(2)}) collective-permute-start(f32[2,16,512]{2,1,0:T(8,128)S(1)} %get-tuple-element.29), channel_id=1, source_target_pairs={{0,2},{1,3},{2,0},{3,1},{4,6},{5,7},{6,4},{7,5},{8,10},{9,11},{10,... | collective-permute-start | bytes 196616 | tf_op jit(solution)/shard_map/ppermute | solution.py:216
  21.9 0.0 collective-permute-done.5.refs_1_
  21.9 0.4 %collective-permute-done.6.refs_2_ = f32[32,64]{1,0:T(8,128)S(1)} collective-permute-done((f32[32,64]{1,0:T(8,128)S(1)}, f32[32,64]{1,0:T(8,128)S(1)}, u32[]{:S(2)}, u32[]{:S(2)}) %collective-permute-start.6) | collective-permute-done | bytes 8224 | tf_op jit(solution)/shard_map/ppermute | solution.py:216
  22.2 0.9 %collective-permute-done.7.refs_3_ = f32[32,64]{1,0:T(8,128)S(1)} collective-permute-done((f32[32,64]{1,0:T(8,128)S(1)}, f32[32,64]{1,0:T(8,128)S(1)}, u32[]{:S(2)}, u32[]{:S(2)}) %collective-permute-start.7) | collective-permute-done | bytes 8224 | tf_op jit(solution)/shard_map/ppermute | solution.py:216
  23.1 0.9 %up.1 = (f32[8,512]{1,0:T(8,128)S(1)}, f32[8,512]{1,0:T(8,128)S(1)}, f32[8,512]{1,0:T(8,128)S(1)}, f32[8,512]{1,0:T(8,128)S(1)}) custom-call(f32[2,16,512]{2,1,0:T(8,128)S(1)} %get-tuple-element.28._.own_ref, s32[16]{0:T(128)S(1)} %get-tuple-element.30.slot_ref, bf16[2,32,64,512]{3,2,1,0:T(8,128)(2,1)S(1)} %copy-done, ...), custom_call_target="tpu_custom_call" | custom-call | flops 1153500032 | tf_op jit(solution)/shard_map/up/pallas_call | solution.py:282
  24.1 1.0 %collective-permute-start.10 = (f32[8,512]{1,0:T(8,128)S(1)}, f32[8,512]{1,0:T(8,128)S(1)}, u32[]{:S(2)}, u32[]{:S(2)}) collective-permute-start(f32[8,512]{1,0:T(8,128)S(1)} %get-tuple-element.34), channel_id=1, source_target_pairs={{0,12},{4,8},{8,4},{12,0},{1,13},{5,9},{9,5},{13,1},{2,14},{6,10},... | collective-permute-start | bytes 49160 | tf_op jit(solution)/shard_map/ppermute | solution.py:216
  25.1 3.4 %collective-permute-start.9 = (f32[8,512]{1,0:T(8,128)S(1)}, f32[8,512]{1,0:T(8,128)S(1)}, u32[]{:S(2)}, u32[]{:S(2)}) collective-permute-start(f32[8,512]{1,0:T(8,128)S(1)} %get-tuple-element.33), channel_id=1, source_target_pairs={{0,8},{4,12},{8,0},{12,4},{1,9},{5,13},{9,1},{13,5},{2,10},{6,14},... | collective-permute-start | bytes 49160 | tf_op jit(solution)/shard_map/ppermute | solution.py:216
  29.1 0.5 %collective-permute-done.10.refs_3_ = f32[8,512]{1,0:T(8,128)S(1)} collective-permute-done((f32[8,512]{1,0:T(8,128)S(1)}, f32[8,512]{1,0:T(8,128)S(1)}, u32[]{:S(2)}, u32[]{:S(2)}) %collective-permute-start.10) | collective-permute-done | bytes 16416 | tf_op jit(solution)/shard_map/ppermute | solution.py:216
  29.6 0.6 %collective-permute-done.9.refs_2_ = f32[8,512]{1,0:T(8,128)S(1)} collective-permute-done((f32[8,512]{1,0:T(8,128)S(1)}, f32[8,512]{1,0:T(8,128)S(1)}, u32[]{:S(2)}, u32[]{:S(2)}) %collective-permute-start.9) | collective-permute-done | bytes 16416 | tf_op jit(solution)/shard_map/ppermute | solution.py:216
  30.2 0.0 collective-permute-done.4.got_ref
  30.2 0.8 %final.1 = bf16[2,16,512]{2,1,0:T(8,128)(2,1)} custom-call(s32[1]{0:T(128)S(6)} %copy.8.count_ref, bf16[32,96]{1,0:T(8,128)(2,1)S(1)} %get-tuple-element.20.pick_ref, f32[2,16,512]{2,1,0:T(8,128)S(1)} %get-tuple-element.28._.own_ref, f32[2,16,512]{2,1,0:T(8,128)S(1)} %collective-permute-done.4.got_ref, f32[8,512]{1,0:T(8,128)S(1)} %get-tuple-element.31.refs_0_, ...), custom_call_target="tpu_custom_call" | custom-call | flops 1153500032 | tf_op jit(solution)/shard_map/final/pallas_call | solution.py:293
  (10 shorter events, 0.0 us)
Async XLA Ops:
  0.0 7.1 %copy-start.2 = (bf16[2,16,2048]{2,1,0:T(8,128)(2,1)S(1)}, bf16[2,16,2048]{2,1,0:T(8,128)(2,1)}, u32[]{:S(2)}) copy-start(bf16[2,16,2048]{2,1,0:T(8,128)(2,1)} %x_ref.1) | copy-start | bytes 393220
  0.0 7.1 %copy-start.1 = (bf16[2,2048,2048]{2,1,0:T(8,128)(2,1)S(1)}, bf16[2,2048,2048]{2,1,0:T(8,128)(2,1)}, u32[]{:S(2)}) copy-start(bf16[2,2048,2048]{2,1,0:T(8,128)(2,1)} %w_ref.1) | copy-start | bytes 50331652
  1.5 8.0 %collective-permute-start = (bf16[16,1152]{1,0:T(8,128)(2,1)S(1)}, bf16[16,1152]{1,0:T(8,128)(2,1)S(1)}, u32[]{:S(2)}, u32[]{:S(2)}) collective-permute-start(bf16[16,1152]{1,0:T(8,128)(2,1)S(1)} %get-tuple-element.22), channel_id=1, source_target_pairs={{0,4},{4,0},{8,12},{12,8},{1,5},{5,1},{9,13},{13,9},{2,6},{6,2},{1... | collective-permute-start | bytes 110600 | tf_op jit(solution)/shard_map/ppermute | solution.py:216
  4.5 5.5 %collective-permute-start.1 = (bf16[16,1152]{1,0:T(8,128)(2,1)S(1)}, bf16[16,1152]{1,0:T(8,128)(2,1)S(1)}, u32[]{:S(2)}, u32[]{:S(2)}) collective-permute-start(bf16[16,1152]{1,0:T(8,128)(2,1)S(1)} %get-tuple-element.23), channel_id=1, source_target_pairs={{0,8},{4,12},{8,0},{12,4},{1,9},{5,13},{9,1},{13,5},{2,10},{6,14},... | collective-permute-start | bytes 110600 | tf_op jit(solution)/shard_map/ppermute | solution.py:216
  7.1 5.8 %collective-permute-start.2 = (bf16[16,1152]{1,0:T(8,128)(2,1)S(1)}, bf16[16,1152]{1,0:T(8,128)(2,1)S(1)}, u32[]{:S(2)}, u32[]{:S(2)}) collective-permute-start(bf16[16,1152]{1,0:T(8,128)(2,1)S(1)} %get-tuple-element.24), channel_id=1, source_target_pairs={{0,12},{4,8},{8,4},{12,0},{1,13},{5,9},{9,5},{13,1},{2,14},{6,10},... | collective-permute-start | bytes 110600 | tf_op jit(solution)/shard_map/ppermute | solution.py:216
  7.1 16.0 %copy-start = (bf16[2,32,64,512]{3,2,1,0:T(8,128)(2,1)S(1)}, bf16[2,32,64,512]{3,2,1,0:T(8,128)(2,1)}, u32[]{:S(2)}) copy-start(bf16[2,32,64,512]{3,2,1,0:T(8,128)(2,1)} %up_ref.1) | copy-start | bytes 12582916
  9.4 10.8 %collective-permute-start.3 = (f32[2,2,16,512]{3,2,1,0:T(8,128)S(1)}, f32[2,2,16,512]{3,2,1,0:T(8,128)S(1)}, u32[]{:S(2)}, u32[]{:S(2)}) collective-permute-start(f32[2,2,16,512]{3,2,1,0:T(8,128)S(1)} %get-tuple-element.27), channel_id=1, source_target_pairs={{0,1},{1,0},{2,3},{3,2},{4,5},{5,4},{6,7},{7,6},{8,9},{9,8},{10,11... | collective-permute-start | bytes 393224 | tf_op jit(solution)/shard_map/ppermute | solution.py:216
  18.3 3.5 %collective-permute-start.5 = (f32[32,64]{1,0:T(8,128)S(1)}, f32[32,64]{1,0:T(8,128)S(1)}, u32[]{:S(2)}, u32[]{:S(2)}) collective-permute-start(f32[32,64]{1,0:T(8,128)S(1)} %get-tuple-element.25._.refs_0_), channel_id=1, source_target_pairs={{0,1},{1,0},{2,3},{3,2},{4,5},{5,4},{6,7},{7,6},{8,9},{9,8},{10,11... | collective-permute-start | bytes 24584 | tf_op jit(solution)/shard_map/ppermute | solution.py:216
  18.4 3.8 %collective-permute-start.6 = (f32[32,64]{1,0:T(8,128)S(1)}, f32[32,64]{1,0:T(8,128)S(1)}, u32[]{:S(2)}, u32[]{:S(2)}) collective-permute-start(f32[32,64]{1,0:T(8,128)S(1)} %get-tuple-element.25._.refs_0_), channel_id=1, source_target_pairs={{0,2},{1,3},{2,0},{3,1},{4,6},{5,7},{6,4},{7,5},{8,10},{9,11},{10,... | collective-permute-start | bytes 24584 | tf_op jit(solution)/shard_map/ppermute | solution.py:216
  20.0 3.2 %collective-permute-start.7 = (f32[32,64]{1,0:T(8,128)S(1)}, f32[32,64]{1,0:T(8,128)S(1)}, u32[]{:S(2)}, u32[]{:S(2)}) collective-permute-start(f32[32,64]{1,0:T(8,128)S(1)} %get-tuple-element.25._.refs_0_), channel_id=1, source_target_pairs={{0,3},{1,2},{2,1},{3,0},{4,7},{5,6},{6,5},{7,4},{8,11},{9,10},{10,... | collective-permute-start | bytes 24584 | tf_op jit(solution)/shard_map/ppermute | solution.py:216
  20.3 9.9 %collective-permute-start.4 = (f32[2,16,512]{2,1,0:T(8,128)S(1)}, f32[2,16,512]{2,1,0:T(8,128)S(1)}, u32[]{:S(2)}, u32[]{:S(2)}) collective-permute-start(f32[2,16,512]{2,1,0:T(8,128)S(1)} %get-tuple-element.29), channel_id=1, source_target_pairs={{0,2},{1,3},{2,0},{3,1},{4,6},{5,7},{6,4},{7,5},{8,10},{9,11},{10,... | collective-permute-start | bytes 196616 | tf_op jit(solution)/shard_map/ppermute | solution.py:216
  24.1 5.6 %collective-permute-start.10 = (f32[8,512]{1,0:T(8,128)S(1)}, f32[8,512]{1,0:T(8,128)S(1)}, u32[]{:S(2)}, u32[]{:S(2)}) collective-permute-start(f32[8,512]{1,0:T(8,128)S(1)} %get-tuple-element.34), channel_id=1, source_target_pairs={{0,12},{4,8},{8,4},{12,0},{1,13},{5,9},{9,5},{13,1},{2,14},{6,10},... | collective-permute-start | bytes 49160 | tf_op jit(solution)/shard_map/ppermute | solution.py:216
  25.1 4.5 %collective-permute-start.8 = (f32[8,512]{1,0:T(8,128)S(1)}, f32[8,512]{1,0:T(8,128)S(1)}, u32[]{:S(2)}, u32[]{:S(2)}) collective-permute-start(f32[8,512]{1,0:T(8,128)S(1)} %get-tuple-element.32), channel_id=1, source_target_pairs={{0,4},{4,0},{8,12},{12,8},{1,5},{5,1},{9,13},{13,9},{2,6},{6,2},{1... | collective-permute-start | bytes 49160 | tf_op jit(solution)/shard_map/ppermute | solution.py:216
  25.1 5.1 %collective-permute-start.9 = (f32[8,512]{1,0:T(8,128)S(1)}, f32[8,512]{1,0:T(8,128)S(1)}, u32[]{:S(2)}, u32[]{:S(2)}) collective-permute-start(f32[8,512]{1,0:T(8,128)S(1)} %get-tuple-element.33), channel_id=1, source_target_pairs={{0,8},{4,12},{8,0},{12,4},{1,9},{5,13},{9,1},{13,5},{2,10},{6,14},... | collective-permute-start | bytes 49160 | tf_op jit(solution)/shard_map/ppermute | solution.py:216

commit v4 on v3

--- a/solution.py
+++ b/solution.py
@@ -18,7 +18,7 @@
 HBM = pl.BlockSpec(memory_space=pltpu.HBM)
 ANY = pl.BlockSpec(memory_space=pl.ANY)
 SMALL = 8 * 1024 * 1024
-LARGE = 48 * 1024 * 1024
+LARGE = 24 * 1024 * 1024
 
 
 def iota(shape, axis):
@@ -86,9 +86,34 @@
     return rest + [mask + 1 for mask in rest]
 
 
-def base_kernel(tensors, _, x_ref, w_ref, keep_ref, send_ref):
-    layers = x_ref.shape[0]
+def slots_of(block_ref, half):
+    tail = block_ref[:, half:].astype(F32)
+    return [tail[c, 0].astype(jnp.int32) for c in range(CAP)]
+
+
+def fetches(store_hbm, slots, chosen_ref, sems):
+    layers, _, rank, _ = store_hbm.shape
+    return [
+        pltpu.make_async_copy(
+            store_hbm.at[layer, slot],
+            chosen_ref.at[layer, pl.ds(c * rank, rank)],
+            sems.at[layer, c],
+        )
+        for layer in range(layers)
+        for c, slot in enumerate(slots)
+    ]
+
+
+def base_kernel(tensors, early, down_hbm, x_ref, w_ref, *refs):
+    block_refs, (keep_ref, send_ref, chosen_ref, sems) = refs[:early], refs[early:]
+    layers, _, depth = x_ref.shape
     width = keep_ref.shape[3]
+    copies = []
+    for i, block_ref in enumerate(block_refs):
+        slots = slots_of(block_ref, depth // HALVES)
+        copies += fetches(down_hbm, slots, chosen_ref.at[i], sems.at[i])
+    for copy in copies:
+        copy.start()
     me = lax.axis_index("tensor")
     for i, mask in enumerate(chunk_order(tensors)):
         out_ref = keep_ref if i < tensors // 2 else send_ref
@@ -97,41 +122,40 @@
             out_ref[i % (tensors // 2), layer] = jnp.dot(
                 x_ref[layer], w_ref[layer, :, columns], preferred_element_type=F32
             )
-
-
-def down_kernel(stores, down_hbm, *refs):
-    block_refs, (low_ref, slot_ref, w_ref, sems) = refs[:stores], refs[stores:]
+    for copy in copies:
+        copy.wait()
+
+
+def down_kernel(order, early, down_hbm, early_ref, *refs):
+    stores = len(order)
+    block_refs, (low_ref, slot_ref, late_ref, sems) = refs[:stores], refs[stores:]
     layers, _, rank, depth = down_hbm.shape
     half = depth // HALVES
     block = layers * HALVES * CAP
-
-    def fetch(layer, k, c, slot):
-        return pltpu.make_async_copy(
-            down_hbm.at[layer, slot],
-            w_ref.at[layer, k, pl.ds(c * rank, rank)],
-            sems.at[layer, k, c],
-        )
-
-    slots = []
-    for k in range(stores):
-        tail = block_refs[k][:, half:].astype(F32)
-        slots.append([tail[c, 0].astype(jnp.int32) for c in range(CAP)])
+    slots = [slots_of(block_ref, half) for block_ref in block_refs]
+    copies = [
+        fetches(down_hbm, slots[i], late_ref.at[i - early], sems.at[i - early])
+        for i in range(early, stores)
+    ]
+    for group in copies:
+        for copy in group:
+            copy.start()
+    for i, k in enumerate(order):
         for c in range(CAP):
-            slot_ref[k * CAP + c] = slots[k][c]
-            for layer in range(layers):
-                fetch(layer, k, c, slots[k][c]).start()
+            slot_ref[k * CAP + c] = slots[i][c]
     row, column = iota((CAP * rank, block), 0), iota((CAP * rank, block), 1)
-    columns = []
-    for k in range(stores):
-        for c in range(CAP):
-            for layer in range(layers):
-                fetch(layer, k, c, slots[k][c]).wait()
+    columns = {}
+    for i, k in enumerate(order):
+        chosen_ref = early_ref.at[i] if i < early else late_ref.at[i - early]
+        if i >= early:
+            for copy in copies[i - early]:
+                copy.wait()
         total = jnp.zeros((rank, block), F32)
         for layer in range(layers):
             for part in range(HALVES):
                 product = lax.dot_general(
-                    w_ref[layer, k, :, part * half : (part + 1) * half],
-                    block_refs[k][:, :half],
+                    chosen_ref[layer, :, part * half : (part + 1) * half],
+                    block_refs[i][:, :half],
                     (((1,), (1,)), ((), ())),
                     preferred_element_type=F32,
                 )
@@ -139,8 +163,8 @@
                 product = jnp.where(mine, product, 0.0)
                 for c in range(CAP):
                     total = total + product[c * rank : (c + 1) * rank]
-        columns.append(total)
-    turned = jnp.concatenate(columns, axis=1).T
+        columns[k] = total
+    turned = jnp.concatenate([columns[k] for k in range(stores)], axis=1).T
     for k in range(stores):
         for layer in range(layers):
             at = k * block + layer * HALVES * CAP
@@ -208,7 +232,7 @@
     block = layers * HALVES * CAP
     owner_row = owner.reshape(1, rows)
     slot_row = slot.reshape(1, rows)
-    down = jnp.swapaxes(down, 2, 3)
+    down = pltpu.with_memory_space_constraint(jnp.swapaxes(down, 2, 3), pltpu.HBM)
 
     def swap(value, axis, size, by):
         if by == 0:
@@ -233,17 +257,21 @@
         cost_estimate=cost(6),
         name="prepare",
     )(*(pltpu.with_memory_space_constraint(v, pltpu.HBM) for v in (owner_row, slot_row, x)))
-    blocks = [swap(payloads[k], "store", stores, k) for k in range(stores)]
-
-    keep, send = pl.pallas_call(
-        functools.partial(base_kernel, tensors),
-        out_shape=[jax.ShapeDtypeStruct((tensors // 2, layers, rows, width), F32)] * 2,
-        in_specs=[ANY] + [VMEM] * 2,
-        out_specs=[VMEM] * 2,
+    order = [0] + list(range(stores - 1, 0, -1))
+    early = min(2, stores)
+    blocks = [swap(payloads[k], "store", stores, k) for k in order]
+
+    keep, send, chosen = pl.pallas_call(
+        functools.partial(base_kernel, tensors, early),
+        out_shape=[jax.ShapeDtypeStruct((tensors // 2, layers, rows, width), F32)] * 2
+        + [jax.ShapeDtypeStruct((early, layers, CAP * rank, depth), BF16)],
+        in_specs=[HBM] + [VMEM] * (2 + early),
+        out_specs=[VMEM] * 3,
+        scratch_shapes=[pltpu.SemaphoreType.DMA((early, layers, CAP))],
         compiler_params=params(),
         cost_estimate=cost(6),
         name="base",
-    )(payloads[0], x, w)
+    )(down, x, w, *blocks[:early])
     got = swap(send, "tensor", tensors, 1)
     bit = 2
     while keep.shape[0] > 2:
@@ -252,21 +280,21 @@
         bit *= 2
 
     low, slots = pl.pallas_call(
-        functools.partial(down_kernel, stores),
+        functools.partial(down_kernel, order, early),
         out_shape=[
             jax.ShapeDtypeStruct((stores * layers * CAP, rank), F32),
             jax.ShapeDtypeStruct((stores * CAP,), jnp.int32),
         ],
-        in_specs=[HBM] + [VMEM] * stores,
+        in_specs=[HBM] + [VMEM] * (1 + stores),
         out_specs=[VMEM, SMEM],
         scratch_shapes=[
-            pltpu.VMEM((layers, stores, CAP * rank, depth), BF16),
-            pltpu.SemaphoreType.DMA((layers, stores, CAP)),
+            pltpu.VMEM((stores - early, layers, CAP * rank, depth), BF16),
+            pltpu.SemaphoreType.DMA((stores - early, layers, CAP)),
         ],
         compiler_params=params(LARGE),
         cost_estimate=cost(4),
         name="down",
-    )(down, *blocks)
+    )(down, chosen, *blocks)
     lows = [swap(low, "tensor", tensors, j) for j in range(tensors)]
     own, send = pl.pallas_call(
         pair_kernel,

time: 31 us -> 34.6 us (1.12)
  waiting for transfers between devices: 5.79 us -> 7.51 us
  Pallas kernels: 10.9 us -> 11.9 us
  starting transfers between devices: 13.6 us -> 14.3 us
    ppermute x11, waiting for transfers between devices: 5.79 us -> 7.51 us  [swap(): return lax.ppermute(value, axis, [(i, i ^ by) for i in range(size)])]
    pallas_call x2, Pallas kernels: 7.71 us -> 8.75 us  [the longest x1 4.4 us: local(): pl.pallas_call(functools.partial(base_kernel, tensors, early), out_shape=...]
    ppermute x11, starting transfers between devices: 13.6 us -> 14.3 us  [swap(): return lax.ppermute(value, axis, [(i, i ^ by) for i in range(size)])]
  transfers between devices with their start and end apart: 11 -> 11, of which waited for: 6 -> 4; matrix products, arithmetic and copies ran while one was open for 0% -> 0% of each run, Pallas kernels for 28% -> 28%
where the time goes in v4:
time: 34.6 us; the launch traced here: 34.5 us
  starting transfers between devices  14.3 us (41%)
  Pallas kernels  11.9 us (34%)
  waiting for transfers between devices  7.51 us (22%)
  between operations  0.74 us (2%)
    ppermute x11, starting transfers between devices, swap(): return lax.ppermute(value, axis, [(i, i ^ by) for i in range(size)])  14.3 us
    ppermute x11, waiting for transfers between devices, swap(): return lax.ppermute(value, axis, [(i, i ^ by) for i in range(size)])  7.51 us
    pallas_call x1, Pallas kernels, local(): pl.pallas_call(functools.partial(base_kernel, tensors, early), out_shape=...  4.4 us
    pallas_call x1, Pallas kernels, local(): pl.pallas_call(functools.partial(down_kernel, order, early), out_shape=[j...  4.35 us
    pallas_call x1, Pallas kernels, local(): pl.pallas_call(functools.partial(prepare_kernel, stores), out_shape=[jax....  1.44 us
    pallas_call x1, Pallas kernels, local(): pl.pallas_call(functools.partial(up_kernel, stores, tensors), out_shape=[...  0.95 us
    pallas_call x1, Pallas kernels, local(): pl.pallas_call(final_kernel, out_shape=jax.ShapeDtypeStruct((layers, rows...  0.75 us
  transfers between devices with their start and end apart: 11, of which 4 were waited for; matrix products, arithmetic and copies ran while one was open for 0% of the time, Pallas kernels for 28%

profile of v4, /device:TPU:0, one launch (start us, length us, event | category | flops | bytes accessed | tf_op | source)
XLA Modules:
  0.0 34.5 jit_solution(982800133337793061)
XLA Ops:
  0.0 1.4 %prepare.1 = (bf16[16,1152]{1,0:T(8,128)(2,1)S(1)}, bf16[16,1152]{1,0:T(8,128)(2,1)S(1)}, bf16[16,1152]{1,0:T(8,128)(2,1)S(1)}, bf16[16,1152]{1,0:T(8,128)(2,1)S(1)}, bf16[32,96]{1,0:T(8,128)(2,1)S(1)}) custom-call(s32[1,16]{1,0:T(1,128)} %bitcast.5, s32[1,16]{1,0:T(1,128)} %bitcast.6, bf16[2,16,2048]{2,1,0:T(8,128)(2,1)} %x_ref.1), custom_call_target="tpu_custom_call" | custom-call | flops 6920999936 | tf_op jit(solution)/shard_map/prepare/pallas_call | solution.py:242
  1.5 5.1 %collective-permute-start = (bf16[16,1152]{1,0:T(8,128)(2,1)S(1)}, bf16[16,1152]{1,0:T(8,128)(2,1)S(1)}, u32[]{:S(2)}, u32[]{:S(2)}) collective-permute-start(bf16[16,1152]{1,0:T(8,128)(2,1)S(1)} %get-tuple-element.23), channel_id=1, source_target_pairs={{0,12},{4,8},{8,4},{12,0},{1,13},{5,9},{9,5},{13,1},{2,14},{6,10},... | collective-permute-start | bytes 110600 | tf_op jit(solution)/shard_map/ppermute | solution.py:240
  6.6 0.0 collective-permute-start.1
  6.6 0.6 %collective-permute-start.2 = (bf16[16,1152]{1,0:T(8,128)(2,1)S(1)}, bf16[16,1152]{1,0:T(8,128)(2,1)S(1)}, u32[]{:S(2)}, u32[]{:S(2)}) collective-permute-start(bf16[16,1152]{1,0:T(8,128)(2,1)S(1)} %get-tuple-element.26), channel_id=1, source_target_pairs={{0,4},{4,0},{8,12},{12,8},{1,5},{5,1},{9,13},{13,9},{2,6},{6,2},{1... | collective-permute-start | bytes 110600 | tf_op jit(solution)/shard_map/ppermute | solution.py:240
  7.2 1.3 %collective-permute-done.refs_1_ = bf16[16,1152]{1,0:T(8,128)(2,1)S(1)} collective-permute-done((bf16[16,1152]{1,0:T(8,128)(2,1)S(1)}, bf16[16,1152]{1,0:T(8,128)(2,1)S(1)}, u32[]{:S(2)}, u32[]{:S(2)}) %collective-permute-start) | collective-permute-done | bytes 36896 | tf_op jit(solution)/shard_map/ppermute | solution.py:240
  8.5 4.4 %base.1 = (f32[2,2,16,512]{3,2,1,0:T(8,128)S(1)}, f32[2,2,16,512]{3,2,1,0:T(8,128)S(1)}, bf16[2,2,256,2048]{3,2,1,0:T(8,128)(2,1)S(1)}) custom-call(bf16[2,32,64,2048]{3,2,1,0:T(8,128)(2,1)} %bitcast.3, bf16[2,16,2048]{2,1,0:T(8,128)(2,1)S(1)} %copy-done.2, bf16[2,2048,2048]{2,1,0:T(8,128)(2,1)S(1)} %copy-done, ...), custom_call_target="tpu_custom_call" | custom-call | flops 6920999936 | tf_op jit(solution)/shard_map/base/pallas_call | solution.py:264
  12.9 0.0 copy-start.1
  12.9 0.1 collective-permute-start.3
  13.0 0.0 collective-permute-done.1.refs_2_
  13.0 4.3 %down.1 = (f32[32,64]{1,0:T(8,128)S(1)}, s32[16]{0:T(128)S(1)}) custom-call(bf16[2,32,64,2048]{3,2,1,0:T(8,128)(2,1)} %bitcast.4, bf16[2,2,256,2048]{3,2,1,0:T(8,128)(2,1)S(1)} %get-tuple-element.24.early_ref, bf16[16,1152]{1,0:T(8,128)(2,1)S(1)} %get-tuple-element.22.refs_0_, bf16[16,1152]{1,0:T(8,128)(2,1)S(1)} %collective-permute-done.refs_1_, ...), custom_call_target="tpu_custom_call" | custom-call | flops 4614000128 | tf_op jit(solution)/shard_map/down/pallas_call | solution.py:282
  17.4 2.0 %collective-permute-start.7 = (f32[32,64]{1,0:T(8,128)S(1)}, f32[32,64]{1,0:T(8,128)S(1)}, u32[]{:S(2)}, u32[]{:S(2)}) collective-permute-start(f32[32,64]{1,0:T(8,128)S(1)} %get-tuple-element.27._.refs_0_), channel_id=1, source_target_pairs={{0,3},{1,2},{2,1},{3,0},{4,7},{5,6},{6,5},{7,4},{8,11},{9,10},{10,... | collective-permute-start | bytes 24584 | tf_op jit(solution)/shard_map/ppermute | solution.py:240
  19.4 0.2 collective-permute-start.6
  19.6 0.0 collective-permute-start.5
  19.6 0.0 collective-permute-done.3.got_ref
  19.6 1.9 %collective-permute-start.4 = (f32[2,16,512]{2,1,0:T(8,128)S(1)}, f32[2,16,512]{2,1,0:T(8,128)S(1)}, u32[]{:S(2)}, u32[]{:S(2)}) collective-permute-start(f32[2,16,512]{2,1,0:T(8,128)S(1)} %get-tuple-element.31), channel_id=1, source_target_pairs={{0,2},{1,3},{2,0},{3,1},{4,6},{5,7},{6,4},{7,5},{8,10},{9,11},{10,... | collective-permute-start | bytes 196616 | tf_op jit(solution)/shard_map/ppermute | solution.py:240
  21.5 0.0 collective-permute-done.7.refs_3_
  21.5 1.8 %collective-permute-done.6.refs_2_ = f32[32,64]{1,0:T(8,128)S(1)} collective-permute-done((f32[32,64]{1,0:T(8,128)S(1)}, f32[32,64]{1,0:T(8,128)S(1)}, u32[]{:S(2)}, u32[]{:S(2)}) %collective-permute-start.6) | collective-permute-done | bytes 8224 | tf_op jit(solution)/shard_map/ppermute | solution.py:240
  23.3 0.0 collective-permute-done.5.refs_1_
  23.3 0.9 %up.1 = (f32[8,512]{1,0:T(8,128)S(1)}, f32[8,512]{1,0:T(8,128)S(1)}, f32[8,512]{1,0:T(8,128)S(1)}, f32[8,512]{1,0:T(8,128)S(1)}) custom-call(f32[2,16,512]{2,1,0:T(8,128)S(1)} %get-tuple-element.30._.own_ref, s32[16]{0:T(128)S(1)} %get-tuple-element.32.slot_ref, bf16[2,32,64,512]{3,2,1,0:T(8,128)(2,1)S(1)} %copy-done.1, ...), custom_call_target="tpu_custom_call" | custom-call | flops 1153500032 | tf_op jit(solution)/shard_map/up/pallas_call | solution.py:310
  24.2 3.9 %collective-permute-start.9 = (f32[8,512]{1,0:T(8,128)S(1)}, f32[8,512]{1,0:T(8,128)S(1)}, u32[]{:S(2)}, u32[]{:S(2)}) collective-permute-start(f32[8,512]{1,0:T(8,128)S(1)} %get-tuple-element.35), channel_id=1, source_target_pairs={{0,8},{4,12},{8,0},{12,4},{1,9},{5,13},{9,1},{13,5},{2,10},{6,14},... | collective-permute-start | bytes 49160 | tf_op jit(solution)/shard_map/ppermute | solution.py:240
  28.2 0.5 %collective-permute-start.10 = (f32[8,512]{1,0:T(8,128)S(1)}, f32[8,512]{1,0:T(8,128)S(1)}, u32[]{:S(2)}, u32[]{:S(2)}) collective-permute-start(f32[8,512]{1,0:T(8,128)S(1)} %get-tuple-element.36), channel_id=1, source_target_pairs={{0,12},{4,8},{8,4},{12,0},{1,13},{5,9},{9,5},{13,1},{2,14},{6,10},... | collective-permute-start | bytes 49160 | tf_op jit(solution)/shard_map/ppermute | solution.py:240
  29.3 0.6 %collective-permute-done.9.refs_2_ = f32[8,512]{1,0:T(8,128)S(1)} collective-permute-done((f32[8,512]{1,0:T(8,128)S(1)}, f32[8,512]{1,0:T(8,128)S(1)}, u32[]{:S(2)}, u32[]{:S(2)}) %collective-permute-start.9) | collective-permute-done | bytes 16416 | tf_op jit(solution)/shard_map/ppermute | solution.py:240
  29.9 3.8 %collective-permute-done.10.refs_3_ = f32[8,512]{1,0:T(8,128)S(1)} collective-permute-done((f32[8,512]{1,0:T(8,128)S(1)}, f32[8,512]{1,0:T(8,128)S(1)}, u32[]{:S(2)}, u32[]{:S(2)}) %collective-permute-start.10) | collective-permute-done | bytes 16416 | tf_op jit(solution)/shard_map/ppermute | solution.py:240
  33.7 0.8 %final.1 = bf16[2,16,512]{2,1,0:T(8,128)(2,1)} custom-call(s32[1]{0:T(128)S(6)} %copy.8.count_ref, bf16[32,96]{1,0:T(8,128)(2,1)S(1)} %get-tuple-element.21.pick_ref, f32[2,16,512]{2,1,0:T(8,128)S(1)} %get-tuple-element.30._.own_ref, f32[2,16,512]{2,1,0:T(8,128)S(1)} %collective-permute-done.4.got_ref, f32[8,512]{1,0:T(8,128)S(1)} %get-tuple-element.33.refs_0_, ...), custom_call_target="tpu_custom_call" | custom-call | flops 1153500032 | tf_op jit(solution)/shard_map/final/pallas_call | solution.py:321
  (10 shorter events, 0.0 us)
Async XLA Ops:
  0.0 8.5 %copy-start.2 = (bf16[2,16,2048]{2,1,0:T(8,128)(2,1)S(1)}, bf16[2,16,2048]{2,1,0:T(8,128)(2,1)}, u32[]{:S(2)}) copy-start(bf16[2,16,2048]{2,1,0:T(8,128)(2,1)} %x_ref.1) | copy-start | bytes 393220
  0.0 8.5 %copy-start = (bf16[2,2048,2048]{2,1,0:T(8,128)(2,1)S(1)}, bf16[2,2048,2048]{2,1,0:T(8,128)(2,1)}, u32[]{:S(2)}) copy-start(bf16[2,2048,2048]{2,1,0:T(8,128)(2,1)} %w_ref.1) | copy-start | bytes 50331652
  1.5 7.1 %collective-permute-start = (bf16[16,1152]{1,0:T(8,128)(2,1)S(1)}, bf16[16,1152]{1,0:T(8,128)(2,1)S(1)}, u32[]{:S(2)}, u32[]{:S(2)}) collective-permute-start(bf16[16,1152]{1,0:T(8,128)(2,1)S(1)} %get-tuple-element.23), channel_id=1, source_target_pairs={{0,12},{4,8},{8,4},{12,0},{1,13},{5,9},{9,5},{13,1},{2,14},{6,10},... | collective-permute-start | bytes 110600 | tf_op jit(solution)/shard_map/ppermute | solution.py:240
  6.6 6.4 %collective-permute-start.1 = (bf16[16,1152]{1,0:T(8,128)(2,1)S(1)}, bf16[16,1152]{1,0:T(8,128)(2,1)S(1)}, u32[]{:S(2)}, u32[]{:S(2)}) collective-permute-start(bf16[16,1152]{1,0:T(8,128)(2,1)S(1)} %get-tuple-element.25), channel_id=1, source_target_pairs={{0,8},{4,12},{8,0},{12,4},{1,9},{5,13},{9,1},{13,5},{2,10},{6,14},... | collective-permute-start | bytes 110600 | tf_op jit(solution)/shard_map/ppermute | solution.py:240
  6.6 6.5 %collective-permute-start.2 = (bf16[16,1152]{1,0:T(8,128)(2,1)S(1)}, bf16[16,1152]{1,0:T(8,128)(2,1)S(1)}, u32[]{:S(2)}, u32[]{:S(2)}) collective-permute-start(bf16[16,1152]{1,0:T(8,128)(2,1)S(1)} %get-tuple-element.26), channel_id=1, source_target_pairs={{0,4},{4,0},{8,12},{12,8},{1,5},{5,1},{9,13},{13,9},{2,6},{6,2},{1... | collective-permute-start | bytes 110600 | tf_op jit(solution)/shard_map/ppermute | solution.py:240
  12.9 10.4 %copy-start.1 = (bf16[2,32,64,512]{3,2,1,0:T(8,128)(2,1)S(1)}, bf16[2,32,64,512]{3,2,1,0:T(8,128)(2,1)}, u32[]{:S(2)}) copy-start(bf16[2,32,64,512]{3,2,1,0:T(8,128)(2,1)} %up_ref.1) | copy-start | bytes 12582916
  12.9 6.6 %collective-permute-start.3 = (f32[2,2,16,512]{3,2,1,0:T(8,128)S(1)}, f32[2,2,16,512]{3,2,1,0:T(8,128)S(1)}, u32[]{:S(2)}, u32[]{:S(2)}) collective-permute-start(f32[2,2,16,512]{3,2,1,0:T(8,128)S(1)} %get-tuple-element.29), channel_id=1, source_target_pairs={{0,1},{1,0},{2,3},{3,2},{4,5},{5,4},{6,7},{7,6},{8,9},{9,8},{10,11... | collective-permute-start | bytes 393224 | tf_op jit(solution)/shard_map/ppermute | solution.py:240
  17.4 4.1 %collective-permute-start.7 = (f32[32,64]{1,0:T(8,128)S(1)}, f32[32,64]{1,0:T(8,128)S(1)}, u32[]{:S(2)}, u32[]{:S(2)}) collective-permute-start(f32[32,64]{1,0:T(8,128)S(1)} %get-tuple-element.27._.refs_0_), channel_id=1, source_target_pairs={{0,3},{1,2},{2,1},{3,0},{4,7},{5,6},{6,5},{7,4},{8,11},{9,10},{10,... | collective-permute-start | bytes 24584 | tf_op jit(solution)/shard_map/ppermute | solution.py:240
  19.4 3.9 %collective-permute-start.6 = (f32[32,64]{1,0:T(8,128)S(1)}, f32[32,64]{1,0:T(8,128)S(1)}, u32[]{:S(2)}, u32[]{:S(2)}) collective-permute-start(f32[32,64]{1,0:T(8,128)S(1)} %get-tuple-element.27._.refs_0_), channel_id=1, source_target_pairs={{0,2},{1,3},{2,0},{3,1},{4,6},{5,7},{6,4},{7,5},{8,10},{9,11},{10,... | collective-permute-start | bytes 24584 | tf_op jit(solution)/shard_map/ppermute | solution.py:240
  19.6 3.7 %collective-permute-start.5 = (f32[32,64]{1,0:T(8,128)S(1)}, f32[32,64]{1,0:T(8,128)S(1)}, u32[]{:S(2)}, u32[]{:S(2)}) collective-permute-start(f32[32,64]{1,0:T(8,128)S(1)} %get-tuple-element.27._.refs_0_), channel_id=1, source_target_pairs={{0,1},{1,0},{2,3},{3,2},{4,5},{5,4},{6,7},{7,6},{8,9},{9,8},{10,11... | collective-permute-start | bytes 24584 | tf_op jit(solution)/shard_map/ppermute | solution.py:240
  19.6 14.1 %collective-permute-start.4 = (f32[2,16,512]{2,1,0:T(8,128)S(1)}, f32[2,16,512]{2,1,0:T(8,128)S(1)}, u32[]{:S(2)}, u32[]{:S(2)}) collective-permute-start(f32[2,16,512]{2,1,0:T(8,128)S(1)} %get-tuple-element.31), channel_id=1, source_target_pairs={{0,2},{1,3},{2,0},{3,1},{4,6},{5,7},{6,4},{7,5},{8,10},{9,11},{10,... | collective-permute-start | bytes 196616 | tf_op jit(solution)/shard_map/ppermute | solution.py:240
  24.2 5.1 %collective-permute-start.8 = (f32[8,512]{1,0:T(8,128)S(1)}, f32[8,512]{1,0:T(8,128)S(1)}, u32[]{:S(2)}, u32[]{:S(2)}) collective-permute-start(f32[8,512]{1,0:T(8,128)S(1)} %get-tuple-element.34), channel_id=1, source_target_pairs={{0,4},{4,0},{8,12},{12,8},{1,5},{5,1},{9,13},{13,9},{2,6},{6,2},{1... | collective-permute-start | bytes 49160 | tf_op jit(solution)/shard_map/ppermute | solution.py:240
  24.2 5.6 %collective-permute-start.9 = (f32[8,512]{1,0:T(8,128)S(1)}, f32[8,512]{1,0:T(8,128)S(1)}, u32[]{:S(2)}, u32[]{:S(2)}) collective-permute-start(f32[8,512]{1,0:T(8,128)S(1)} %get-tuple-element.35), channel_id=1, source_target_pairs={{0,8},{4,12},{8,0},{12,4},{1,9},{5,13},{9,1},{13,5},{2,10},{6,14},... | collective-permute-start | bytes 49160 | tf_op jit(solution)/shard_map/ppermute | solution.py:240
  28.2 5.5 %collective-permute-start.10 = (f32[8,512]{1,0:T(8,128)S(1)}, f32[8,512]{1,0:T(8,128)S(1)}, u32[]{:S(2)}, u32[]{:S(2)}) collective-permute-start(f32[8,512]{1,0:T(8,128)S(1)} %get-tuple-element.36), channel_id=1, source_target_pairs={{0,12},{4,8},{8,4},{12,0},{1,13},{5,9},{9,5},{13,1},{2,14},{6,10},... | collective-permute-start | bytes 49160 | tf_op jit(solution)/shard_map/ppermute | solution.py:240

commit v5 on v3

v5 whole, which is shorter than its diff:
```python
import functools

import jax
import jax.numpy as jnp
from jax import lax
from jax.experimental import pallas as pl
from jax.experimental.pallas import tpu as pltpu
from jax.sharding import PartitionSpec as P

CAP = 4
HALVES = 2
LANES = 128
F32 = jnp.float32
BF16 = jnp.bfloat16
VMEM = pl.BlockSpec(memory_space=pltpu.VMEM)
SMEM = pl.BlockSpec(memory_space=pltpu.SMEM)
HBM = pl.BlockSpec(memory_space=pltpu.HBM)
ANY = pl.BlockSpec(memory_space=pl.ANY)
SMALL = 8 * 1024 * 1024
LARGE = 24 * 1024 * 1024


def iota(shape, axis):
    return lax.broadcasted_iota(jnp.int32, shape, axis)


def ranks(owner_row):
    rows = owner_row.shape[1]
    down, across = iota((rows, rows), 0), iota((rows, rows), 1)
    owner_row = (owner_row ^ lax.axis_index("store")).astype(F32)
    spread = jnp.broadcast_to(owner_row, (rows, rows))
    owner_col = jnp.sum(jnp.where(down == across, spread, 0.0), axis=1, keepdims=True)
    same = owner_col == spread
    rank_row = jnp.sum(jnp.where(same & (down < across), 1.0, 0.0), axis=0, keepdims=True)
    rank_col = jnp.sum(jnp.where(same & (across < down), 1.0, 0.0), axis=1, keepdims=True)
    return owner_row, rank_row, owner_col, rank_col


def prepare_kernel(back, owner_hbm, slot_hbm, x_hbm, *refs):
    stores = len(back)
    out_refs, (pick_ref, owner_ref, slot_ref, x_ref, sems) = refs[:stores], refs[stores:]
    pairs = ((owner_hbm, owner_ref), (slot_hbm, slot_ref), (x_hbm, x_ref))
    copies = [
        pltpu.make_async_copy(source, target, sems.at[i]) for i, (source, target) in enumerate(pairs)
    ]
    for copy in copies:
        copy.start()
    for copy in copies:
        copy.wait()
    layers, rows, depth = x_ref.shape
    half = depth // HALVES
    block = layers * HALVES * CAP
    hop_row, rank_row, hop_col, rank_col = ranks(owner_ref[...])
    place = hop_row * block + rank_row
    places = jnp.concatenate([place + CAP * part for part in range(layers * HALVES)], axis=1)
    pick = iota((stores * block, layers * HALVES * rows), 0).astype(F32) == places
    stacked = jnp.concatenate(
        [
            x_ref[layer, :, part * half : (part + 1) * half]
            for layer in range(layers)
            for part in range(HALVES)
        ],
        axis=0,
    )
    sent = jnp.dot(pick.astype(BF16), stacked, preferred_element_type=F32).astype(BF16)
    first = iota((stores * block, rows), 0).astype(F32) == place
    slots = jnp.sum(
        jnp.where(first, jnp.broadcast_to(slot_ref[...].astype(F32), first.shape), 0.0),
        axis=1,
        keepdims=True,
    )
    slots = jnp.broadcast_to(slots, (stores * block, LANES)).astype(BF16)
    for k, out_ref in enumerate(out_refs):
        out_ref[:, :half] = sent[k * block : (k + 1) * block]
        out_ref[:, half:] = slots[k * block : (k + 1) * block]
    spots = iota((rows, pick_ref.shape[1]), 1).astype(F32)
    spot = sum(jnp.where(hop_col == float(k), float(i), 0.0) for i, k in enumerate(back))
    place = spot * (layers * CAP) + rank_col
    for layer in range(layers):
        pick_ref[layer * rows : (layer + 1) * rows] = (spots == place + layer * CAP).astype(BF16)


def chunk_order(tensors):
    if tensors == 1:
        return [0]
    rest = [2 * mask for mask in chunk_order(tensors // 2)]
    return rest + [mask + 1 for mask in rest]


def main_kernel(order, tensors, down_hbm, up_hbm, x_ref, w_ref, *refs):
    stores = len(order)
    block_refs, refs = refs[:stores], refs[stores:]
    keep_ref, send_ref, low_ref, up_ref, refs = *refs[:4], refs[4:]
    slot_vmem, slot_smem, chosen_ref, slot_sem, down_sems, up_sems = refs
    layers, _, rank, depth = down_hbm.shape
    half = depth // HALVES
    block = layers * HALVES * CAP
    for i in range(stores):
        tail = block_refs[i][:, half:].astype(F32)
        slot_vmem[i * 8 : (i + 1) * 8] = tail[:8].astype(jnp.int32)
    slot_copy = pltpu.make_async_copy(slot_vmem, slot_smem, slot_sem)
    slot_copy.start()
    slot_copy.wait()

    def fetches(store_hbm, target_ref, sems, i):
        return [
            pltpu.make_async_copy(
                store_hbm.at[layer, slot_smem[i * 8 + c, 0]],
                target_ref.at[i, layer, pl.ds(c * rank, rank)],
                sems.at[i, layer, c],
            )
            for layer in range(layers)
            for c in range(CAP)
        ]

    downs = [fetches(down_hbm, chosen_ref, down_sems, i) for i in range(stores)]
    ups = [fetches(up_hbm, up_ref, up_sems, i) for i in range(stores)]
    for group in downs + ups:
        for copy in group:
            copy.start()

    me = lax.axis_index("tensor")
    width = keep_ref.shape[3]
    for i, mask in enumerate(chunk_order(tensors)):
        out_ref = keep_ref if i < tensors // 2 else send_ref
        columns = pl.ds(pl.multiple_of((me ^ mask) * width, width), width)
        for layer in range(layers):
            out_ref[i % (tensors // 2), layer] = jnp.dot(
                x_ref[layer], w_ref[layer, :, columns], preferred_element_type=F32
            )

    row, column = iota((CAP * rank, block), 0), iota((CAP * rank, block), 1)
    columns = []
    for i in range(stores):
        for copy in downs[i]:
            copy.wait()
        total = jnp.zeros((rank, block), F32)
        for layer in range(layers):
            for part in range(HALVES):
                product = lax.dot_general(
                    chosen_ref[i, layer, :, part * half : (part + 1) * half],
                    block_refs[i][:, :half],
                    (((1,), (1,)), ((), ())),
                    preferred_element_type=F32,
                )
                mine = column == (layer * HALVES + part) * CAP + row // rank
                product = jnp.where(mine, product, 0.0)
                for c in range(CAP):
                    total = total + product[c * rank : (c + 1) * rank]
        columns.append(total)
    turned = jnp.concatenate(columns, axis=1).T
    for i in range(stores):
        for layer in range(layers):
            at = i * block + layer * HALVES * CAP
            low_ref[(i * layers + layer) * CAP : (i * layers + layer + 1) * CAP] = (
                turned[at : at + CAP] + turned[at + CAP : at + 2 * CAP]
            )
    for group in ups:
        for copy in group:
            copy.wait()


def pair_kernel(_, keep_ref, got_ref, own_ref, send_ref):
    own_ref[...] = keep_ref[0] + got_ref[0]
    send_ref[...] = keep_ref[1] + got_ref[1]


def up_kernel(tensors, _, up_ref, *refs):
    low_refs, out_refs = refs[:tensors], refs[tensors:]
    stores, layers, depth, width = up_ref.shape
    rank = depth // CAP
    half = width // HALVES
    low = low_refs[0][...]
    for low_ref in low_refs[1:]:
        low = low + low_ref[...]
    row, column = iota((CAP, depth), 0), iota((CAP, depth), 1)
    for i in range(stores):
        terms = []
        for layer in range(layers):
            at = (i * layers + layer) * CAP
            spread = jnp.concatenate([low[at : at + CAP]] * CAP, axis=1)
            spread = jnp.where(row == column // rank, spread, 0.0).astype(BF16)
            terms.append(jnp.dot(spread, up_ref[i, layer], preferred_element_type=F32))
        terms = jnp.concatenate(terms, axis=0)
        parts = [terms[:, part * half : (part + 1) * half] for part in range(HALVES)]
        out_refs[i][...] = jnp.concatenate(parts, axis=0).astype(BF16)


def final_kernel(count_ref, pick_ref, own_ref, got_ref, *refs):
    term_refs, out_ref = refs[:-1], refs[-1]
    layers, rows, width = out_ref.shape
    half = width // HALVES
    live = iota((rows, 1), 0) < count_ref[0]
    terms = [term_ref[...].astype(F32) for term_ref in term_refs]
    for part in range(HALVES):
        span = slice(part * half, (part + 1) * half)
        mine = slice(part * layers * CAP, (part + 1) * layers * CAP)
        stacked = jnp.concatenate([term[mine] for term in terms], axis=0).astype(BF16)
        delta = jnp.dot(pick_ref[...], stacked, preferred_element_type=F32)
        for layer in range(layers):
            total = own_ref[layer, :, span] + got_ref[layer, :, span]
            total = total + delta[layer * rows : (layer + 1) * rows]
            out_ref[layer, :, span] = jnp.where(live, total, 0.0).astype(BF16)


def params(limit=SMALL):
    return pltpu.CompilerParams(vmem_limit_bytes=limit)


def cost(microseconds):
    return pl.CostEstimate(
        flops=int(microseconds * 1.1535e9), bytes_accessed=0, transcendentals=0
    )


def local(stores, tensors, x, w, down, up, owner, slot, count):
    layers, rows, depth = x.shape
    adapters, rank, width = up.shape[1:]
    half = depth // HALVES
    block = layers * HALVES * CAP
    owner_row = owner.reshape(1, rows)
    slot_row = slot.reshape(1, rows)
    down = pltpu.with_memory_space_constraint(jnp.swapaxes(down, 2, 3), pltpu.HBM)
    up = pltpu.with_memory_space_constraint(up, pltpu.HBM)

    def swap(value, axis, size, by):
        if by == 0:
            return value
        return lax.ppermute(value, axis, [(i, i ^ by) for i in range(size)])

    order = [0] + list(range(stores - 1, 0, -1))
    back = [0] + order[2:] + order[1:2]
    *payloads, pick = pl.pallas_call(
        functools.partial(prepare_kernel, back),
        out_shape=[jax.ShapeDtypeStruct((block, half + LANES), BF16)] * stores
        + [
            jax.ShapeDtypeStruct((layers * rows, stores * layers * CAP), BF16),
        ],
        in_specs=[ANY] * 3,
        out_specs=[VMEM] * (stores + 1),
        scratch_shapes=[
            pltpu.VMEM((1, rows), jnp.int32),
            pltpu.VMEM((1, rows), jnp.int32),
            pltpu.VMEM(x.shape, BF16),
            pltpu.SemaphoreType.DMA((3,)),
        ],
        compiler_params=params(),
        cost_estimate=cost(6),
        name="prepare",
    )(*(pltpu.with_memory_space_constraint(v, pltpu.HBM) for v in (owner_row, slot_row, x)))
    blocks = [swap(payloads[k], "store", stores, k) for k in order]

    keep, send, low, chosen = pl.pallas_call(
        functools.partial(main_kernel, order, tensors),
        out_shape=[jax.ShapeDtypeStruct((tensors // 2, layers, rows, width), F32)] * 2
        + [
            jax.ShapeDtypeStruct((stores * layers * CAP, rank), F32),
            jax.ShapeDtypeStruct((stores, layers, CAP * rank, width), BF16),
        ],
        in_specs=[HBM] * 2 + [VMEM] * (2 + stores),
        out_specs=[VMEM] * 4,
        scratch_shapes=[
            pltpu.VMEM((stores * 8, LANES), jnp.int32),
            pltpu.SMEM((stores * 8, LANES), jnp.int32),
            pltpu.VMEM((stores, layers, CAP * rank, depth), BF16),
            pltpu.SemaphoreType.DMA,
            pltpu.SemaphoreType.DMA((stores, layers, CAP)),
            pltpu.SemaphoreType.DMA((stores, layers, CAP)),
        ],
        compiler_params=params(LARGE),
        cost_estimate=cost(6),
        name="main",
    )(down, up, x, w, *blocks)
    lows = [low] + [swap(low, "tensor", tensors, j) for j in range(tensors - 1, 0, -1)]
    got = swap(send, "tensor", tensors, 1)
    bit = 2
    while keep.shape[0] > 2:
        total, middle = keep + got, keep.shape[0] // 2
        keep, got = total[:middle], swap(total[middle:], "tensor", tensors, bit)
        bit *= 2

    own, send = pl.pallas_call(
        pair_kernel,
        out_shape=[jax.ShapeDtypeStruct((layers, rows, width), F32)] * 2,
        in_specs=[ANY] + [VMEM] * 2,
        out_specs=[VMEM] * 2,
        compiler_params=params(),
        cost_estimate=cost(0.3),
        name="pair",
    )(low, keep, got)
    got = swap(send, "tensor", tensors, bit)

    terms = pl.pallas_call(
        functools.partial(up_kernel, tensors),
        out_shape=[jax.ShapeDtypeStruct((layers * HALVES * CAP, width // HALVES), BF16)] * stores,
        in_specs=[ANY] + [VMEM] * (1 + tensors),
        out_specs=[VMEM] * stores,
        compiler_params=params(),
        cost_estimate=cost(1),
        name="up",
    )(own, chosen, *lows)
    returned = [swap(terms[order.index(k)], "store", stores, k) for k in back]

    return pl.pallas_call(
        final_kernel,
        out_shape=jax.ShapeDtypeStruct((layers, rows, width), BF16),
        in_specs=[SMEM] + [VMEM] * (3 + stores),
        out_specs=VMEM,
        compiler_params=params(),
        cost_estimate=cost(1),
        name="final",
    )(count, pick, own, got, *returned)


def solution(mesh):
    return jax.shard_map(
        functools.partial(local, mesh.shape["store"], mesh.shape["tensor"]),
        mesh=mesh,
        in_specs=(
            P(None, ("groups", "store"), "tensor"),
            P(None, "tensor", None),
            P(None, "store", "tensor", None),
            P(None, "store", None, "tensor"),
            P(("groups", "store"), None),
            P(("groups", "store")),
            P(("groups", "store")),
        ),
        out_specs=P(None, ("groups", "store"), "tensor"),
        check_vma=False,
    )
```

time: 31 us -> 32.3 us (1.042)
  waiting for transfers between devices: 5.79 us -> 7.19 us
  Pallas kernels: 10.9 us -> 10.2 us
  starting transfers between devices: 13.6 us -> 14 us
    ppermute x11, waiting for transfers between devices: 5.79 us -> 7.19 us  [swap(): return lax.ppermute(value, axis, [(i, i ^ by) for i in range(size)])]
    pallas_call x4 -> x3, Pallas kernels: 10.1 us -> 9.44 us  [the longest x1 7.62 us: local(): pl.pallas_call(functools.partial(main_kernel, order, tensors), out_shape=...]
    ppermute x11, starting transfers between devices: 13.6 us -> 14 us  [swap(): return lax.ppermute(value, axis, [(i, i ^ by) for i in range(size)])]
  transfers between devices with their start and end apart: 11 -> 11, of which waited for: 6 -> 5; matrix products, arithmetic and copies ran while one was open for 0% -> 0% of each run, Pallas kernels for 28% -> 1%
where the time goes in v5:
time: 32.3 us; the launch traced here: 32.1 us
  starting transfers between devices  14 us (43%)
  Pallas kernels  10.2 us (32%)
  waiting for transfers between devices  7.19 us (22%)
  between operations  0.69 us (2%)
    ppermute x11, starting transfers between devices, swap(): return lax.ppermute(value, axis, [(i, i ^ by) for i in range(size)])  14 us
    pallas_call x1, Pallas kernels, local(): pl.pallas_call(functools.partial(main_kernel, order, tensors), out_shape=...  7.62 us
    ppermute x11, waiting for transfers between devices, swap(): return lax.ppermute(value, axis, [(i, i ^ by) for i in range(size)])  7.19 us
    pallas_call x1, Pallas kernels, local(): pl.pallas_call(functools.partial(prepare_kernel, back), out_shape=[jax.Sh...  1.44 us
    pallas_call x1, Pallas kernels, local(): pl.pallas_call(final_kernel, out_shape=jax.ShapeDtypeStruct((layers, rows...  0.75 us
  transfers between devices with their start and end apart: 11, of which 5 were waited for; matrix products, arithmetic and copies ran while one was open for 0% of the time, Pallas kernels for 1%

profile of v5, /device:TPU:0, one launch (start us, length us, event | category | flops | bytes accessed | tf_op | source)
XLA Modules:
  0.0 32.1 jit_solution(3652318985964847228)
XLA Ops:
  0.0 1.4 %prepare.1 = (bf16[16,1152]{1,0:T(8,128)(2,1)S(1)}, bf16[16,1152]{1,0:T(8,128)(2,1)S(1)}, bf16[16,1152]{1,0:T(8,128)(2,1)S(1)}, bf16[16,1152]{1,0:T(8,128)(2,1)S(1)}, bf16[32,32]{1,0:T(8,128)(2,1)S(1)}) custom-call(s32[1,16]{1,0:T(1,128)} %bitcast.4, s32[1,16]{1,0:T(1,128)} %bitcast.5, bf16[2,16,2048]{2,1,0:T(8,128)(2,1)} %x_ref.1), custom_call_target="tpu_custom_call" | custom-call | flops 6920999936 | tf_op jit(solution)/shard_map/prepare/pallas_call | solution.py:233
  1.5 5.1 %collective-permute-start = (bf16[16,1152]{1,0:T(8,128)(2,1)S(1)}, bf16[16,1152]{1,0:T(8,128)(2,1)S(1)}, u32[]{:S(2)}, u32[]{:S(2)}) collective-permute-start(bf16[16,1152]{1,0:T(8,128)(2,1)S(1)} %get-tuple-element.22), channel_id=1, source_target_pairs={{0,12},{4,8},{8,4},{12,0},{1,13},{5,9},{9,5},{13,1},{2,14},{6,10},... | collective-permute-start | bytes 110600 | tf_op jit(solution)/shard_map/ppermute | solution.py:229
  6.6 0.0 collective-permute-start.1
  6.6 0.6 %collective-permute-start.2 = (bf16[16,1152]{1,0:T(8,128)(2,1)S(1)}, bf16[16,1152]{1,0:T(8,128)(2,1)S(1)}, u32[]{:S(2)}, u32[]{:S(2)}) collective-permute-start(bf16[16,1152]{1,0:T(8,128)(2,1)S(1)} %get-tuple-element.24), channel_id=1, source_target_pairs={{0,4},{4,0},{8,12},{12,8},{1,5},{5,1},{9,13},{13,9},{2,6},{6,2},{1... | collective-permute-start | bytes 110600 | tf_op jit(solution)/shard_map/ppermute | solution.py:229
  7.2 1.3 %collective-permute-done.refs_1_ = bf16[16,1152]{1,0:T(8,128)(2,1)S(1)} collective-permute-done((bf16[16,1152]{1,0:T(8,128)(2,1)S(1)}, bf16[16,1152]{1,0:T(8,128)(2,1)S(1)}, u32[]{:S(2)}, u32[]{:S(2)}) %collective-permute-start) | collective-permute-done | bytes 36896 | tf_op jit(solution)/shard_map/ppermute | solution.py:229
  8.5 2.9 %collective-permute-done.1.refs_2_ = bf16[16,1152]{1,0:T(8,128)(2,1)S(1)} collective-permute-done((bf16[16,1152]{1,0:T(8,128)(2,1)S(1)}, bf16[16,1152]{1,0:T(8,128)(2,1)S(1)}, u32[]{:S(2)}, u32[]{:S(2)}) %collective-permute-start.1) | collective-permute-done | bytes 36896 | tf_op jit(solution)/shard_map/ppermute | solution.py:229
  11.4 0.0 collective-permute-done.2.refs_3_
  11.4 7.6 %main.1 = (f32[2,2,16,512]{3,2,1,0:T(8,128)S(1)}, f32[2,2,16,512]{3,2,1,0:T(8,128)S(1)}, f32[32,64]{1,0:T(8,128)S(1)}, bf16[4,2,256,512]{3,2,1,0:T(8,128)(2,1)S(1)}) custom-call(bf16[2,32,64,2048]{3,2,1,0:T(8,128)(2,1)} %bitcast.3, bf16[2,32,64,512]{3,2,1,0:T(8,128)(2,1)} %up_hbm.1, bf16[2,16,2048]{2,1,0:T(8,128)(2,1)S(1)} %copy-done.1, ...), custom_call_target="tpu_custom_call" | custom-call | flops 6920999936 | tf_op jit(solution)/shard_map/main/pallas_call | solution.py:253
  19.1 0.1 collective-permute-start.3
  19.1 1.6 %collective-permute-start.5 = (f32[32,64]{1,0:T(8,128)S(1)}, f32[32,64]{1,0:T(8,128)S(1)}, u32[]{:S(2)}, u32[]{:S(2)}) collective-permute-start(f32[32,64]{1,0:T(8,128)S(1)} %get-tuple-element.25._.refs_0_), channel_id=1, source_target_pairs={{0,3},{1,2},{2,1},{3,0},{4,7},{5,6},{6,5},{7,4},{8,11},{9,10},{10,... | collective-permute-start | bytes 24584 | tf_op jit(solution)/shard_map/ppermute | solution.py:229
  20.7 0.5 %collective-permute-start.6 = (f32[32,64]{1,0:T(8,128)S(1)}, f32[32,64]{1,0:T(8,128)S(1)}, u32[]{:S(2)}, u32[]{:S(2)}) collective-permute-start(f32[32,64]{1,0:T(8,128)S(1)} %get-tuple-element.25._.refs_0_), channel_id=1, source_target_pairs={{0,2},{1,3},{2,0},{3,1},{4,6},{5,7},{6,4},{7,5},{8,10},{9,11},{10,... | collective-permute-start | bytes 24584 | tf_op jit(solution)/shard_map/ppermute | solution.py:229
  21.3 0.0 collective-permute-start.7
  21.3 1.6 %collective-permute-start.4 = (f32[2,16,512]{2,1,0:T(8,128)S(1)}, f32[2,16,512]{2,1,0:T(8,128)S(1)}, u32[]{:S(2)}, u32[]{:S(2)}) collective-permute-start(f32[2,16,512]{2,1,0:T(8,128)S(1)} %get-tuple-element.29), channel_id=1, source_target_pairs={{0,2},{1,3},{2,0},{3,1},{4,6},{5,7},{6,4},{7,5},{8,10},{9,11},{10,... | collective-permute-start | bytes 196616 | tf_op jit(solution)/shard_map/ppermute | solution.py:229
  22.9 0.0 collective-permute-done.5.refs_1_
  22.9 1.6 %collective-permute-done.6.refs_2_ = f32[32,64]{1,0:T(8,128)S(1)} collective-permute-done((f32[32,64]{1,0:T(8,128)S(1)}, f32[32,64]{1,0:T(8,128)S(1)}, u32[]{:S(2)}, u32[]{:S(2)}) %collective-permute-start.6) | collective-permute-done | bytes 8224 | tf_op jit(solution)/shard_map/ppermute | solution.py:229
  24.5 0.0 collective-permute-done.7.refs_3_
  24.5 0.4 %up.1 = (bf16[16,256]{1,0:T(8,128)(2,1)S(1)}, bf16[16,256]{1,0:T(8,128)(2,1)S(1)}, bf16[16,256]{1,0:T(8,128)(2,1)S(1)}, bf16[16,256]{1,0:T(8,128)(2,1)S(1)}) custom-call(f32[2,16,512]{2,1,0:T(8,128)S(1)} %get-tuple-element.28._.own_ref, bf16[4,2,256,512]{3,2,1,0:T(8,128)(2,1)S(1)} %get-tuple-element.30.up_ref, f32[32,64]{1,0:T(8,128)S(1)} %get-tuple-element.25._.refs_0_, ...), custom_call_target="tpu_custom_call" | custom-call | flops 1153500032 | tf_op jit(solution)/shard_map/up/pallas_call | solution.py:293
  24.9 1.9 %collective-permute-start.10 = (bf16[16,256]{1,0:T(8,128)(2,1)S(1)}, bf16[16,256]{1,0:T(8,128)(2,1)S(1)}, u32[]{:S(2)}, u32[]{:S(2)}) collective-permute-start(bf16[16,256]{1,0:T(8,128)(2,1)S(1)} %get-tuple-element.34), channel_id=1, source_target_pairs={{0,12},{4,8},{8,4},{12,0},{1,13},{5,9},{9,5},{13,1},{2,14},{6,10},... | collective-permute-start | bytes 24584 | tf_op jit(solution)/shard_map/ppermute | solution.py:229
  26.8 0.2 collective-permute-start.8
  27.0 2.3 %collective-permute-start.9 = (bf16[16,256]{1,0:T(8,128)(2,1)S(1)}, bf16[16,256]{1,0:T(8,128)(2,1)S(1)}, u32[]{:S(2)}, u32[]{:S(2)}) collective-permute-start(bf16[16,256]{1,0:T(8,128)(2,1)S(1)} %get-tuple-element.33), channel_id=1, source_target_pairs={{0,4},{4,0},{8,12},{12,8},{1,5},{5,1},{9,13},{13,9},{2,6},{6,2},{1... | collective-permute-start | bytes 24584 | tf_op jit(solution)/shard_map/ppermute | solution.py:229
  30.0 0.4 %collective-permute-done.10.refs_3_ = bf16[16,256]{1,0:T(8,128)(2,1)S(1)} collective-permute-done((bf16[16,256]{1,0:T(8,128)(2,1)S(1)}, bf16[16,256]{1,0:T(8,128)(2,1)S(1)}, u32[]{:S(2)}, u32[]{:S(2)}) %collective-permute-start.10) | collective-permute-done | bytes 8224 | tf_op jit(solution)/shard_map/ppermute | solution.py:229
  30.4 0.9 %collective-permute-done.8.refs_1_ = bf16[16,256]{1,0:T(8,128)(2,1)S(1)} collective-permute-done((bf16[16,256]{1,0:T(8,128)(2,1)S(1)}, bf16[16,256]{1,0:T(8,128)(2,1)S(1)}, u32[]{:S(2)}, u32[]{:S(2)}) %collective-permute-start.8) | collective-permute-done | bytes 8224 | tf_op jit(solution)/shard_map/ppermute | solution.py:229
  31.3 0.0 collective-permute-done.9.refs_2_
  31.3 0.7 %final.1 = bf16[2,16,512]{2,1,0:T(8,128)(2,1)} custom-call(s32[1]{0:T(128)S(6)} %copy.8.count_ref, bf16[32,32]{1,0:T(8,128)(2,1)S(1)} %get-tuple-element.20.pick_ref, f32[2,16,512]{2,1,0:T(8,128)S(1)} %get-tuple-element.28._.own_ref, f32[2,16,512]{2,1,0:T(8,128)S(1)} %collective-permute-done.4.got_ref, bf16[16,256]{1,0:T(8,128)(2,1)S(1)} %get-tuple-element.31.refs_0_, ...), custom_call_target="tpu_custom_call" | custom-call | flops 1153500032 | tf_op jit(solution)/shard_map/final/pallas_call | solution.py:304
  (7 shorter events, 0.0 us)
Async XLA Ops:
  0.0 11.4 %copy-start.1 = (bf16[2,16,2048]{2,1,0:T(8,128)(2,1)S(1)}, bf16[2,16,2048]{2,1,0:T(8,128)(2,1)}, u32[]{:S(2)}) copy-start(bf16[2,16,2048]{2,1,0:T(8,128)(2,1)} %x_ref.1) | copy-start | bytes 393220
  0.0 11.4 %copy-start = (bf16[2,2048,2048]{2,1,0:T(8,128)(2,1)S(1)}, bf16[2,2048,2048]{2,1,0:T(8,128)(2,1)}, u32[]{:S(2)}) copy-start(bf16[2,2048,2048]{2,1,0:T(8,128)(2,1)} %w_ref.1) | copy-start | bytes 50331652
  1.5 7.1 %collective-permute-start = (bf16[16,1152]{1,0:T(8,128)(2,1)S(1)}, bf16[16,1152]{1,0:T(8,128)(2,1)S(1)}, u32[]{:S(2)}, u32[]{:S(2)}) collective-permute-start(bf16[16,1152]{1,0:T(8,128)(2,1)S(1)} %get-tuple-element.22), channel_id=1, source_target_pairs={{0,12},{4,8},{8,4},{12,0},{1,13},{5,9},{9,5},{13,1},{2,14},{6,10},... | collective-permute-start | bytes 110600 | tf_op jit(solution)/shard_map/ppermute | solution.py:229
  6.6 4.9 %collective-permute-start.1 = (bf16[16,1152]{1,0:T(8,128)(2,1)S(1)}, bf16[16,1152]{1,0:T(8,128)(2,1)S(1)}, u32[]{:S(2)}, u32[]{:S(2)}) collective-permute-start(bf16[16,1152]{1,0:T(8,128)(2,1)S(1)} %get-tuple-element.23), channel_id=1, source_target_pairs={{0,8},{4,12},{8,0},{12,4},{1,9},{5,13},{9,1},{13,5},{2,10},{6,14},... | collective-permute-start | bytes 110600 | tf_op jit(solution)/shard_map/ppermute | solution.py:229
  6.6 4.9 %collective-permute-start.2 = (bf16[16,1152]{1,0:T(8,128)(2,1)S(1)}, bf16[16,1152]{1,0:T(8,128)(2,1)S(1)}, u32[]{:S(2)}, u32[]{:S(2)}) collective-permute-start(bf16[16,1152]{1,0:T(8,128)(2,1)S(1)} %get-tuple-element.24), channel_id=1, source_target_pairs={{0,4},{4,0},{8,12},{12,8},{1,5},{5,1},{9,13},{13,9},{2,6},{6,2},{1... | collective-permute-start | bytes 110600 | tf_op jit(solution)/shard_map/ppermute | solution.py:229
  19.1 2.2 %collective-permute-start.3 = (f32[2,2,16,512]{3,2,1,0:T(8,128)S(1)}, f32[2,2,16,512]{3,2,1,0:T(8,128)S(1)}, u32[]{:S(2)}, u32[]{:S(2)}) collective-permute-start(f32[2,2,16,512]{3,2,1,0:T(8,128)S(1)} %get-tuple-element.27), channel_id=1, source_target_pairs={{0,1},{1,0},{2,3},{3,2},{4,5},{5,4},{6,7},{7,6},{8,9},{9,8},{10,11... | collective-permute-start | bytes 393224 | tf_op jit(solution)/shard_map/ppermute | solution.py:229
  19.1 3.7 %collective-permute-start.5 = (f32[32,64]{1,0:T(8,128)S(1)}, f32[32,64]{1,0:T(8,128)S(1)}, u32[]{:S(2)}, u32[]{:S(2)}) collective-permute-start(f32[32,64]{1,0:T(8,128)S(1)} %get-tuple-element.25._.refs_0_), channel_id=1, source_target_pairs={{0,3},{1,2},{2,1},{3,0},{4,7},{5,6},{6,5},{7,4},{8,11},{9,10},{10,... | collective-permute-start | bytes 24584 | tf_op jit(solution)/shard_map/ppermute | solution.py:229
  20.7 3.7 %collective-permute-start.6 = (f32[32,64]{1,0:T(8,128)S(1)}, f32[32,64]{1,0:T(8,128)S(1)}, u32[]{:S(2)}, u32[]{:S(2)}) collective-permute-start(f32[32,64]{1,0:T(8,128)S(1)} %get-tuple-element.25._.refs_0_), channel_id=1, source_target_pairs={{0,2},{1,3},{2,0},{3,1},{4,6},{5,7},{6,4},{7,5},{8,10},{9,11},{10,... | collective-permute-start | bytes 24584 | tf_op jit(solution)/shard_map/ppermute | solution.py:229
  21.3 3.2 %collective-permute-start.7 = (f32[32,64]{1,0:T(8,128)S(1)}, f32[32,64]{1,0:T(8,128)S(1)}, u32[]{:S(2)}, u32[]{:S(2)}) collective-permute-start(f32[32,64]{1,0:T(8,128)S(1)} %get-tuple-element.25._.refs_0_), channel_id=1, source_target_pairs={{0,1},{1,0},{2,3},{3,2},{4,5},{5,4},{6,7},{7,6},{8,9},{9,8},{10,11... | collective-permute-start | bytes 24584 | tf_op jit(solution)/shard_map/ppermute | solution.py:229
  21.3 10.0 %collective-permute-start.4 = (f32[2,16,512]{2,1,0:T(8,128)S(1)}, f32[2,16,512]{2,1,0:T(8,128)S(1)}, u32[]{:S(2)}, u32[]{:S(2)}) collective-permute-start(f32[2,16,512]{2,1,0:T(8,128)S(1)} %get-tuple-element.29), channel_id=1, source_target_pairs={{0,2},{1,3},{2,0},{3,1},{4,6},{5,7},{6,4},{7,5},{8,10},{9,11},{10,... | collective-permute-start | bytes 196616 | tf_op jit(solution)/shard_map/ppermute | solution.py:229
  24.9 5.5 %collective-permute-start.10 = (bf16[16,256]{1,0:T(8,128)(2,1)S(1)}, bf16[16,256]{1,0:T(8,128)(2,1)S(1)}, u32[]{:S(2)}, u32[]{:S(2)}) collective-permute-start(bf16[16,256]{1,0:T(8,128)(2,1)S(1)} %get-tuple-element.34), channel_id=1, source_target_pairs={{0,12},{4,8},{8,4},{12,0},{1,13},{5,9},{9,5},{13,1},{2,14},{6,10},... | collective-permute-start | bytes 24584 | tf_op jit(solution)/shard_map/ppermute | solution.py:229
  26.8 4.5 %collective-permute-start.8 = (bf16[16,256]{1,0:T(8,128)(2,1)S(1)}, bf16[16,256]{1,0:T(8,128)(2,1)S(1)}, u32[]{:S(2)}, u32[]{:S(2)}) collective-permute-start(bf16[16,256]{1,0:T(8,128)(2,1)S(1)} %get-tuple-element.32), channel_id=1, source_target_pairs={{0,8},{4,12},{8,0},{12,4},{1,9},{5,13},{9,1},{13,5},{2,10},{6,14},... | collective-permute-start | bytes 24584 | tf_op jit(solution)/shard_map/ppermute | solution.py:229
  27.0 4.3 %collective-permute-start.9 = (bf16[16,256]{1,0:T(8,128)(2,1)S(1)}, bf16[16,256]{1,0:T(8,128)(2,1)S(1)}, u32[]{:S(2)}, u32[]{:S(2)}) collective-permute-start(bf16[16,256]{1,0:T(8,128)(2,1)S(1)} %get-tuple-element.33), channel_id=1, source_target_pairs={{0,4},{4,0},{8,12},{12,8},{1,5},{5,1},{9,13},{13,9},{2,6},{6,2},{1... | collective-permute-start | bytes 24584 | tf_op jit(solution)/shard_map/ppermute | solution.py:229

commit v6 on v5

--- a/solution.py
+++ b/solution.py
@@ -87,58 +87,79 @@
     return rest + [mask + 1 for mask in rest]
 
 
-def main_kernel(order, tensors, down_hbm, up_hbm, x_ref, w_ref, *refs):
-    stores = len(order)
-    block_refs, refs = refs[:stores], refs[stores:]
-    keep_ref, send_ref, low_ref, up_ref, refs = *refs[:4], refs[4:]
-    slot_vmem, slot_smem, chosen_ref, slot_sem, down_sems, up_sems = refs
+def slot_copy(block_refs, half, vmem_ref, smem_ref, sem):
+    for i, block_ref in enumerate(block_refs):
+        tail = block_ref[:, half:].astype(F32)
+        vmem_ref[i * 8 : (i + 1) * 8] = tail[:8].astype(jnp.int32)
+    copy = pltpu.make_async_copy(vmem_ref, smem_ref, sem)
+    copy.start()
+    return copy
+
+
+def fetches(store_hbm, smem_ref, i, target_ref, sems):
+    rank = store_hbm.shape[2]
+    return [
+        pltpu.make_async_copy(
+            store_hbm.at[:, smem_ref[i * 8 + c, 0]],
+            target_ref.at[:, pl.ds(c * rank, rank)],
+            sems.at[c],
+        )
+        for c in range(CAP)
+    ]
+
+
+def start_some(waiting, count):
+    for copy in waiting[:count]:
+        copy.start()
+    del waiting[:count]
+
+
+def base_kernel(tensors, early, down_hbm, x_ref, w_ref, *refs):
+    block_refs, refs = refs[:early], refs[early:]
+    keep_ref, send_ref, chosen_ref, slot_vmem, slot_smem, slot_sem, sems = refs
+    layers, _, depth = x_ref.shape
+    width = keep_ref.shape[3]
+    slots = slot_copy(block_refs, depth // HALVES, slot_vmem, slot_smem, slot_sem)
+    me = lax.axis_index("tensor")
+    copies, waiting = [], []
+    for i, mask in enumerate(chunk_order(tensors)):
+        out_ref = keep_ref if i < tensors // 2 else send_ref
+        columns = pl.ds(pl.multiple_of((me ^ mask) * width, width), width)
+        for layer in range(layers):
+            out_ref[i % (tensors // 2), layer] = jnp.dot(
+                x_ref[layer], w_ref[layer, :, columns], preferred_element_type=F32
+            )
+            if not copies:
+                slots.wait()
+                for j in range(early):
+                    copies += fetches(down_hbm, slot_smem, j, chosen_ref.at[j], sems.at[j])
+                waiting = list(copies)
+            start_some(waiting, 2)
+    start_some(waiting, len(waiting))
+    for copy in copies:
+        copy.wait()
+
+
+def down_kernel(early, down_hbm, up_hbm, early_ref, *refs):
+    stores = len(refs) - 9
+    block_refs, (low_ref, up_ref, late_ref, *refs) = refs[:stores], refs[stores:]
+    slot_vmem, slot_smem, slot_sem, down_sems, up_sems, kept_ref = refs
     layers, _, rank, depth = down_hbm.shape
     half = depth // HALVES
     block = layers * HALVES * CAP
+    slots = slot_copy(block_refs, half, slot_vmem, slot_smem, slot_sem)
+    row, column = iota((CAP * rank, block), 0), iota((CAP * rank, block), 1)
+    copies, waiting = [], []
     for i in range(stores):
-        tail = block_refs[i][:, half:].astype(F32)
-        slot_vmem[i * 8 : (i + 1) * 8] = tail[:8].astype(jnp.int32)
-    slot_copy = pltpu.make_async_copy(slot_vmem, slot_smem, slot_sem)
-    slot_copy.start()
-    slot_copy.wait()
-
-    def fetches(store_hbm, target_ref, sems, i):
-        return [
-            pltpu.make_async_copy(
-                store_hbm.at[layer, slot_smem[i * 8 + c, 0]],
-                target_ref.at[i, layer, pl.ds(c * rank, rank)],
-                sems.at[i, layer, c],
-            )
-            for layer in range(layers)
-            for c in range(CAP)
-        ]
-
-    downs = [fetches(down_hbm, chosen_ref, down_sems, i) for i in range(stores)]
-    ups = [fetches(up_hbm, up_ref, up_sems, i) for i in range(stores)]
-    for group in downs + ups:
-        for copy in group:
-            copy.start()
-
-    me = lax.axis_index("tensor")
-    width = keep_ref.shape[3]
-    for i, mask in enumerate(chunk_order(tensors)):
-        out_ref = keep_ref if i < tensors // 2 else send_ref
-        columns = pl.ds(pl.multiple_of((me ^ mask) * width, width), width)
-        for layer in range(layers):
-            out_ref[i % (tensors // 2), layer] = jnp.dot(
-                x_ref[layer], w_ref[layer, :, columns], preferred_element_type=F32
-            )
-
-    row, column = iota((CAP * rank, block), 0), iota((CAP * rank, block), 1)
-    columns = []
-    for i in range(stores):
-        for copy in downs[i]:
-            copy.wait()
+        chosen_ref = early_ref.at[i] if i < early else late_ref.at[i - early]
+        if i >= early:
+            for copy in copies[i - early]:
+                copy.wait()
         total = jnp.zeros((rank, block), F32)
         for layer in range(layers):
             for part in range(HALVES):
                 product = lax.dot_general(
-                    chosen_ref[i, layer, :, part * half : (part + 1) * half],
+                    chosen_ref[layer, :, part * half : (part + 1) * half],
                     block_refs[i][:, :half],
                     (((1,), (1,)), ((), ())),
                     preferred_element_type=F32,
@@ -147,8 +168,22 @@
                 product = jnp.where(mine, product, 0.0)
                 for c in range(CAP):
                     total = total + product[c * rank : (c + 1) * rank]
-        columns.append(total)
-    turned = jnp.concatenate(columns, axis=1).T
+                if not copies:
+                    slots.wait()
+                    for j in range(early, stores):
+                        at = j - early
+                        copies.append(
+                            fetches(down_hbm, slot_smem, j, late_ref.at[at], down_sems.at[at])
+                        )
+                    ups = [
+                        fetches(up_hbm, slot_smem, j, up_ref.at[j], up_sems.at[j])
+                        for j in range(stores)
+                    ]
+                    waiting = sum(copies + ups, [])
+                start_some(waiting, 2)
+        kept_ref[:, i * block : (i + 1) * block] = total
+    start_some(waiting, len(waiting))
+    turned = kept_ref[...].T
     for i in range(stores):
         for layer in range(layers):
             at = i * block + layer * HALVES * CAP
@@ -250,27 +285,45 @@
     )(*(pltpu.with_memory_space_constraint(v, pltpu.HBM) for v in (owner_row, slot_row, x)))
     blocks = [swap(payloads[k], "store", stores, k) for k in order]
 
-    keep, send, low, chosen = pl.pallas_call(
-        functools.partial(main_kernel, order, tensors),
+    early = min(2, stores)
+    keep, send, chosen = pl.pallas_call(
+        functools.partial(base_kernel, tensors, early),
         out_shape=[jax.ShapeDtypeStruct((tensors // 2, layers, rows, width), F32)] * 2
-        + [
+        + [jax.ShapeDtypeStruct((early, layers, CAP * rank, depth), BF16)],
+        in_specs=[HBM] + [VMEM] * (2 + early),
+        out_specs=[VMEM] * 3,
+        scratch_shapes=[
+            pltpu.VMEM((early * 8, LANES), jnp.int32),
+            pltpu.SMEM((early * 8, LANES), jnp.int32),
+            pltpu.SemaphoreType.DMA,
+            pltpu.SemaphoreType.DMA((early, CAP)),
+        ],
+        compiler_params=params(),
+        cost_estimate=cost(6),
+        name="base",
+    )(down, x, w, *blocks[:early])
+
+    low, chosen = pl.pallas_call(
+        functools.partial(down_kernel, early),
+        out_shape=[
             jax.ShapeDtypeStruct((stores * layers * CAP, rank), F32),
             jax.ShapeDtypeStruct((stores, layers, CAP * rank, width), BF16),
         ],
-        in_specs=[HBM] * 2 + [VMEM] * (2 + stores),
-        out_specs=[VMEM] * 4,
+        in_specs=[HBM] * 2 + [VMEM] * (1 + stores),
+        out_specs=[VMEM] * 2,
         scratch_shapes=[
+            pltpu.VMEM((stores - early, layers, CAP * rank, depth), BF16),
             pltpu.VMEM((stores * 8, LANES), jnp.int32),
             pltpu.SMEM((stores * 8, LANES), jnp.int32),
-            pltpu.VMEM((stores, layers, CAP * rank, depth), BF16),
             pltpu.SemaphoreType.DMA,
-            pltpu.SemaphoreType.DMA((stores, layers, CAP)),
-            pltpu.SemaphoreType.DMA((stores, layers, CAP)),
+            pltpu.SemaphoreType.DMA((stores - early, CAP)),
+            pltpu.SemaphoreType.DMA((stores, CAP)),
+            pltpu.VMEM((rank, stores * block), F32),
         ],
         compiler_params=params(LARGE),
-        cost_estimate=cost(6),
-        name="main",
-    )(down, up, x, w, *blocks)
+        cost_estimate=cost(4),
+        name="down",
+    )(down, up, chosen, *blocks)
     lows = [low] + [swap(low, "tensor", tensors, j) for j in range(tensors - 1, 0, -1)]
     got = swap(send, "tensor", tensors, 1)
     bit = 2

time: 32.3 us -> 33.6 us (1.040)
  Pallas kernels: 10.2 us -> 12.4 us
  waiting for transfers between devices: 7.19 us -> 5.99 us
    pallas_call x1 -> x2, Pallas kernels: 7.62 us -> 9.78 us  [the longest x1 5.16 us: local(): pl.pallas_call(functools.partial(down_kernel, early), out_shape=[jax.Shap...]
    ppermute x11, waiting for transfers between devices: 7.19 us -> 5.99 us  [swap(): return lax.ppermute(value, axis, [(i, i ^ by) for i in range(size)])]
    ppermute x11, starting transfers between devices: 14 us -> 14.3 us  [swap(): return lax.ppermute(value, axis, [(i, i ^ by) for i in range(size)])]
  transfers between devices with their start and end apart: 11 -> 11, of which waited for: 5 -> 4; matrix products, arithmetic and copies ran while one was open for 0% -> 0% of each run, Pallas kernels for 1% -> 30%
where the time goes in v6:
time: 33.6 us; the launch traced here: 33.4 us
  starting transfers between devices  14.3 us (43%)
  Pallas kernels  12.4 us (37%)
  waiting for transfers between devices  5.99 us (18%)
  between operations  0.72 us (2%)
    ppermute x11, starting transfers between devices, swap(): return lax.ppermute(value, axis, [(i, i ^ by) for i in range(size)])  14.3 us
    ppermute x11, waiting for transfers between devices, swap(): return lax.ppermute(value, axis, [(i, i ^ by) for i in range(size)])  5.99 us
    pallas_call x1, Pallas kernels, local(): pl.pallas_call(functools.partial(down_kernel, early), out_shape=[jax.Shap...  5.16 us
    pallas_call x1, Pallas kernels, local(): pl.pallas_call(functools.partial(base_kernel, tensors, early), out_shape=...  4.62 us
    pallas_call x1, Pallas kernels, local(): pl.pallas_call(functools.partial(prepare_kernel, back), out_shape=[jax.Sh...  1.44 us
    pallas_call x1, Pallas kernels, local(): pl.pallas_call(final_kernel, out_shape=jax.ShapeDtypeStruct((layers, rows...  0.75 us
  transfers between devices with their start and end apart: 11, of which 4 were waited for; matrix products, arithmetic and copies ran while one was open for 0% of the time, Pallas kernels for 30%

profile of v6, /device:TPU:0, one launch (start us, length us, event | category | flops | bytes accessed | tf_op | source)
XLA Modules:
  0.0 33.4 jit_solution(1926542788866073497)
XLA Ops:
  0.0 1.4 %prepare.1 = (bf16[16,1152]{1,0:T(8,128)(2,1)S(1)}, bf16[16,1152]{1,0:T(8,128)(2,1)S(1)}, bf16[16,1152]{1,0:T(8,128)(2,1)S(1)}, bf16[16,1152]{1,0:T(8,128)(2,1)S(1)}, bf16[32,32]{1,0:T(8,128)(2,1)S(1)}) custom-call(s32[1,16]{1,0:T(1,128)} %bitcast.5, s32[1,16]{1,0:T(1,128)} %bitcast.6, bf16[2,16,2048]{2,1,0:T(8,128)(2,1)} %x_ref.1), custom_call_target="tpu_custom_call" | custom-call | flops 6920999936 | tf_op jit(solution)/shard_map/prepare/pallas_call | solution.py:268
  1.5 5.1 %collective-permute-start = (bf16[16,1152]{1,0:T(8,128)(2,1)S(1)}, bf16[16,1152]{1,0:T(8,128)(2,1)S(1)}, u32[]{:S(2)}, u32[]{:S(2)}) collective-permute-start(bf16[16,1152]{1,0:T(8,128)(2,1)S(1)} %get-tuple-element.23), channel_id=1, source_target_pairs={{0,12},{4,8},{8,4},{12,0},{1,13},{5,9},{9,5},{13,1},{2,14},{6,10},... | collective-permute-start | bytes 110600 | tf_op jit(solution)/shard_map/ppermute | solution.py:264
  6.6 0.0 collective-permute-start.1
  6.6 0.6 %collective-permute-start.2 = (bf16[16,1152]{1,0:T(8,128)(2,1)S(1)}, bf16[16,1152]{1,0:T(8,128)(2,1)S(1)}, u32[]{:S(2)}, u32[]{:S(2)}) collective-permute-start(bf16[16,1152]{1,0:T(8,128)(2,1)S(1)} %get-tuple-element.26), channel_id=1, source_target_pairs={{0,4},{4,0},{8,12},{12,8},{1,5},{5,1},{9,13},{13,9},{2,6},{6,2},{1... | collective-permute-start | bytes 110600 | tf_op jit(solution)/shard_map/ppermute | solution.py:264
  7.2 1.3 %collective-permute-done.refs_1_ = bf16[16,1152]{1,0:T(8,128)(2,1)S(1)} collective-permute-done((bf16[16,1152]{1,0:T(8,128)(2,1)S(1)}, bf16[16,1152]{1,0:T(8,128)(2,1)S(1)}, u32[]{:S(2)}, u32[]{:S(2)}) %collective-permute-start) | collective-permute-done | bytes 36896 | tf_op jit(solution)/shard_map/ppermute | solution.py:264
  8.5 4.6 %base.1 = (f32[2,2,16,512]{3,2,1,0:T(8,128)S(1)}, f32[2,2,16,512]{3,2,1,0:T(8,128)S(1)}, bf16[2,2,256,2048]{3,2,1,0:T(8,128)(2,1)S(1)}) custom-call(bf16[2,32,64,2048]{3,2,1,0:T(8,128)(2,1)} %bitcast.3, bf16[2,16,2048]{2,1,0:T(8,128)(2,1)S(1)} %copy-done.1, bf16[2,2048,2048]{2,1,0:T(8,128)(2,1)S(1)} %copy-done, ...), custom_call_target="tpu_custom_call" | custom-call | flops 6920999936 | tf_op jit(solution)/shard_map/base/pallas_call | solution.py:289
  13.1 0.1 collective-permute-start.3
  13.2 0.0 collective-permute-done.1.refs_2_
  13.2 0.0 collective-permute-done.2.refs_3_
  13.2 5.2 %down.1 = (f32[32,64]{1,0:T(8,128)S(1)}, bf16[4,2,256,512]{3,2,1,0:T(8,128)(2,1)S(1)}) custom-call(bf16[2,32,64,2048]{3,2,1,0:T(8,128)(2,1)} %bitcast.4, bf16[2,32,64,512]{3,2,1,0:T(8,128)(2,1)} %up_hbm.1, bf16[2,2,256,2048]{3,2,1,0:T(8,128)(2,1)S(1)} %get-tuple-element.24.early_ref, bf16[16,1152]{1,0:T(8,128)(2,1)S(1)} %get-tuple-element.22.refs_0_, ...), custom_call_target="tpu_custom_call" | custom-call | flops 4614000128 | tf_op jit(solution)/shard_map/down/pallas_call | solution.py:306
  18.4 2.0 %collective-permute-start.5 = (f32[32,64]{1,0:T(8,128)S(1)}, f32[32,64]{1,0:T(8,128)S(1)}, u32[]{:S(2)}, u32[]{:S(2)}) collective-permute-start(f32[32,64]{1,0:T(8,128)S(1)} %get-tuple-element.27._.refs_0_), channel_id=1, source_target_pairs={{0,3},{1,2},{2,1},{3,0},{4,7},{5,6},{6,5},{7,4},{8,11},{9,10},{10,... | collective-permute-start | bytes 24584 | tf_op jit(solution)/shard_map/ppermute | solution.py:264
  20.4 0.2 collective-permute-start.6
  20.6 0.0 collective-permute-start.7
  20.6 0.0 collective-permute-done.3.got_ref
  20.6 1.9 %collective-permute-start.4 = (f32[2,16,512]{2,1,0:T(8,128)S(1)}, f32[2,16,512]{2,1,0:T(8,128)S(1)}, u32[]{:S(2)}, u32[]{:S(2)}) collective-permute-start(f32[2,16,512]{2,1,0:T(8,128)S(1)} %get-tuple-element.31), channel_id=1, source_target_pairs={{0,2},{1,3},{2,0},{3,1},{4,6},{5,7},{6,4},{7,5},{8,10},{9,11},{10,... | collective-permute-start | bytes 196616 | tf_op jit(solution)/shard_map/ppermute | solution.py:264
  22.5 1.8 %collective-permute-done.6.refs_2_ = f32[32,64]{1,0:T(8,128)S(1)} collective-permute-done((f32[32,64]{1,0:T(8,128)S(1)}, f32[32,64]{1,0:T(8,128)S(1)}, u32[]{:S(2)}, u32[]{:S(2)}) %collective-permute-start.6) | collective-permute-done | bytes 8224 | tf_op jit(solution)/shard_map/ppermute | solution.py:264
  24.3 0.4 %up.1 = (bf16[16,256]{1,0:T(8,128)(2,1)S(1)}, bf16[16,256]{1,0:T(8,128)(2,1)S(1)}, bf16[16,256]{1,0:T(8,128)(2,1)S(1)}, bf16[16,256]{1,0:T(8,128)(2,1)S(1)}) custom-call(f32[2,16,512]{2,1,0:T(8,128)S(1)} %get-tuple-element.30._.own_ref, bf16[4,2,256,512]{3,2,1,0:T(8,128)(2,1)S(1)} %get-tuple-element.32.up_ref, f32[32,64]{1,0:T(8,128)S(1)} %get-tuple-element.27._.refs_0_, ...), custom_call_target="tpu_custom_call" | custom-call | flops 1153500032 | tf_op jit(solution)/shard_map/up/pallas_call | solution.py:346
  24.7 3.4 %collective-permute-start.10 = (bf16[16,256]{1,0:T(8,128)(2,1)S(1)}, bf16[16,256]{1,0:T(8,128)(2,1)S(1)}, u32[]{:S(2)}, u32[]{:S(2)}) collective-permute-start(bf16[16,256]{1,0:T(8,128)(2,1)S(1)} %get-tuple-element.36), channel_id=1, source_target_pairs={{0,12},{4,8},{8,4},{12,0},{1,13},{5,9},{9,5},{13,1},{2,14},{6,10},... | collective-permute-start | bytes 24584 | tf_op jit(solution)/shard_map/ppermute | solution.py:264
  28.1 1.0 %collective-permute-start.9 = (bf16[16,256]{1,0:T(8,128)(2,1)S(1)}, bf16[16,256]{1,0:T(8,128)(2,1)S(1)}, u32[]{:S(2)}, u32[]{:S(2)}) collective-permute-start(bf16[16,256]{1,0:T(8,128)(2,1)S(1)} %get-tuple-element.35), channel_id=1, source_target_pairs={{0,4},{4,0},{8,12},{12,8},{1,5},{5,1},{9,13},{13,9},{2,6},{6,2},{1... | collective-permute-start | bytes 24584 | tf_op jit(solution)/shard_map/ppermute | solution.py:264
  29.8 0.4 %collective-permute-done.10.refs_3_ = bf16[16,256]{1,0:T(8,128)(2,1)S(1)} collective-permute-done((bf16[16,256]{1,0:T(8,128)(2,1)S(1)}, bf16[16,256]{1,0:T(8,128)(2,1)S(1)}, u32[]{:S(2)}, u32[]{:S(2)}) %collective-permute-start.10) | collective-permute-done | bytes 8224 | tf_op jit(solution)/shard_map/ppermute | solution.py:264
  30.2 2.5 %collective-permute-done.8.refs_1_ = bf16[16,256]{1,0:T(8,128)(2,1)S(1)} collective-permute-done((bf16[16,256]{1,0:T(8,128)(2,1)S(1)}, bf16[16,256]{1,0:T(8,128)(2,1)S(1)}, u32[]{:S(2)}, u32[]{:S(2)}) %collective-permute-start.8) | collective-permute-done | bytes 8224 | tf_op jit(solution)/shard_map/ppermute | solution.py:264
  32.7 0.0 collective-permute-done.9.refs_2_
  32.7 0.0 collective-permute-done.4.got_ref
  32.7 0.7 %final.1 = bf16[2,16,512]{2,1,0:T(8,128)(2,1)} custom-call(s32[1]{0:T(128)S(6)} %copy.8.count_ref, bf16[32,32]{1,0:T(8,128)(2,1)S(1)} %get-tuple-element.21.pick_ref, f32[2,16,512]{2,1,0:T(8,128)S(1)} %get-tuple-element.30._.own_ref, f32[2,16,512]{2,1,0:T(8,128)S(1)} %collective-permute-done.4.got_ref, bf16[16,256]{1,0:T(8,128)(2,1)S(1)} %get-tuple-element.33.refs_0_, ...), custom_call_target="tpu_custom_call" | custom-call | flops 1153500032 | tf_op jit(solution)/shard_map/final/pallas_call | solution.py:357
  (8 shorter events, 0.0 us)
Async XLA Ops:
  0.0 8.5 %copy-start = (bf16[2,2048,2048]{2,1,0:T(8,128)(2,1)S(1)}, bf16[2,2048,2048]{2,1,0:T(8,128)(2,1)}, u32[]{:S(2)}) copy-start(bf16[2,2048,2048]{2,1,0:T(8,128)(2,1)} %w_ref.1) | copy-start | bytes 50331652
  0.0 8.5 %copy-start.1 = (bf16[2,16,2048]{2,1,0:T(8,128)(2,1)S(1)}, bf16[2,16,2048]{2,1,0:T(8,128)(2,1)}, u32[]{:S(2)}) copy-start(bf16[2,16,2048]{2,1,0:T(8,128)(2,1)} %x_ref.1) | copy-start | bytes 393220
  1.5 7.1 %collective-permute-start = (bf16[16,1152]{1,0:T(8,128)(2,1)S(1)}, bf16[16,1152]{1,0:T(8,128)(2,1)S(1)}, u32[]{:S(2)}, u32[]{:S(2)}) collective-permute-start(bf16[16,1152]{1,0:T(8,128)(2,1)S(1)} %get-tuple-element.23), channel_id=1, source_target_pairs={{0,12},{4,8},{8,4},{12,0},{1,13},{5,9},{9,5},{13,1},{2,14},{6,10},... | collective-permute-start | bytes 110600 | tf_op jit(solution)/shard_map/ppermute | solution.py:264
  6.6 6.7 %collective-permute-start.1 = (bf16[16,1152]{1,0:T(8,128)(2,1)S(1)}, bf16[16,1152]{1,0:T(8,128)(2,1)S(1)}, u32[]{:S(2)}, u32[]{:S(2)}) collective-permute-start(bf16[16,1152]{1,0:T(8,128)(2,1)S(1)} %get-tuple-element.25), channel_id=1, source_target_pairs={{0,8},{4,12},{8,0},{12,4},{1,9},{5,13},{9,1},{13,5},{2,10},{6,14},... | collective-permute-start | bytes 110600 | tf_op jit(solution)/shard_map/ppermute | solution.py:264
  6.6 6.7 %collective-permute-start.2 = (bf16[16,1152]{1,0:T(8,128)(2,1)S(1)}, bf16[16,1152]{1,0:T(8,128)(2,1)S(1)}, u32[]{:S(2)}, u32[]{:S(2)}) collective-permute-start(bf16[16,1152]{1,0:T(8,128)(2,1)S(1)} %get-tuple-element.26), channel_id=1, source_target_pairs={{0,4},{4,0},{8,12},{12,8},{1,5},{5,1},{9,13},{13,9},{2,6},{6,2},{1... | collective-permute-start | bytes 110600 | tf_op jit(solution)/shard_map/ppermute | solution.py:264
  13.1 7.4 %collective-permute-start.3 = (f32[2,2,16,512]{3,2,1,0:T(8,128)S(1)}, f32[2,2,16,512]{3,2,1,0:T(8,128)S(1)}, u32[]{:S(2)}, u32[]{:S(2)}) collective-permute-start(f32[2,2,16,512]{3,2,1,0:T(8,128)S(1)} %get-tuple-element.29), channel_id=1, source_target_pairs={{0,1},{1,0},{2,3},{3,2},{4,5},{5,4},{6,7},{7,6},{8,9},{9,8},{10,11... | collective-permute-start | bytes 393224 | tf_op jit(solution)/shard_map/ppermute | solution.py:264
  18.4 4.1 %collective-permute-start.5 = (f32[32,64]{1,0:T(8,128)S(1)}, f32[32,64]{1,0:T(8,128)S(1)}, u32[]{:S(2)}, u32[]{:S(2)}) collective-permute-start(f32[32,64]{1,0:T(8,128)S(1)} %get-tuple-element.27._.refs_0_), channel_id=1, source_target_pairs={{0,3},{1,2},{2,1},{3,0},{4,7},{5,6},{6,5},{7,4},{8,11},{9,10},{10,... | collective-permute-start | bytes 24584 | tf_op jit(solution)/shard_map/ppermute | solution.py:264
  20.4 3.9 %collective-permute-start.6 = (f32[32,64]{1,0:T(8,128)S(1)}, f32[32,64]{1,0:T(8,128)S(1)}, u32[]{:S(2)}, u32[]{:S(2)}) collective-permute-start(f32[32,64]{1,0:T(8,128)S(1)} %get-tuple-element.27._.refs_0_), channel_id=1, source_target_pairs={{0,2},{1,3},{2,0},{3,1},{4,6},{5,7},{6,4},{7,5},{8,10},{9,11},{10,... | collective-permute-start | bytes 24584 | tf_op jit(solution)/shard_map/ppermute | solution.py:264
  20.6 3.7 %collective-permute-start.7 = (f32[32,64]{1,0:T(8,128)S(1)}, f32[32,64]{1,0:T(8,128)S(1)}, u32[]{:S(2)}, u32[]{:S(2)}) collective-permute-start(f32[32,64]{1,0:T(8,128)S(1)} %get-tuple-element.27._.refs_0_), channel_id=1, source_target_pairs={{0,1},{1,0},{2,3},{3,2},{4,5},{5,4},{6,7},{7,6},{8,9},{9,8},{10,11... | collective-permute-start | bytes 24584 | tf_op jit(solution)/shard_map/ppermute | solution.py:264
  20.6 12.1 %collective-permute-start.4 = (f32[2,16,512]{2,1,0:T(8,128)S(1)}, f32[2,16,512]{2,1,0:T(8,128)S(1)}, u32[]{:S(2)}, u32[]{:S(2)}) collective-permute-start(f32[2,16,512]{2,1,0:T(8,128)S(1)} %get-tuple-element.31), channel_id=1, source_target_pairs={{0,2},{1,3},{2,0},{3,1},{4,6},{5,7},{6,4},{7,5},{8,10},{9,11},{10,... | collective-permute-start | bytes 196616 | tf_op jit(solution)/shard_map/ppermute | solution.py:264
  24.7 5.5 %collective-permute-start.10 = (bf16[16,256]{1,0:T(8,128)(2,1)S(1)}, bf16[16,256]{1,0:T(8,128)(2,1)S(1)}, u32[]{:S(2)}, u32[]{:S(2)}) collective-permute-start(bf16[16,256]{1,0:T(8,128)(2,1)S(1)} %get-tuple-element.36), channel_id=1, source_target_pairs={{0,12},{4,8},{8,4},{12,0},{1,13},{5,9},{9,5},{13,1},{2,14},{6,10},... | collective-permute-start | bytes 24584 | tf_op jit(solution)/shard_map/ppermute | solution.py:264
  28.1 4.5 %collective-permute-start.8 = (bf16[16,256]{1,0:T(8,128)(2,1)S(1)}, bf16[16,256]{1,0:T(8,128)(2,1)S(1)}, u32[]{:S(2)}, u32[]{:S(2)}) collective-permute-start(bf16[16,256]{1,0:T(8,128)(2,1)S(1)} %get-tuple-element.34), channel_id=1, source_target_pairs={{0,8},{4,12},{8,0},{12,4},{1,9},{5,13},{9,1},{13,5},{2,10},{6,14},... | collective-permute-start | bytes 24584 | tf_op jit(solution)/shard_map/ppermute | solution.py:264
  28.1 4.5 %collective-permute-start.9 = (bf16[16,256]{1,0:T(8,128)(2,1)S(1)}, bf16[16,256]{1,0:T(8,128)(2,1)S(1)}, u32[]{:S(2)}, u32[]{:S(2)}) collective-permute-start(bf16[16,256]{1,0:T(8,128)(2,1)S(1)} %get-tuple-element.35), channel_id=1, source_target_pairs={{0,4},{4,0},{8,12},{12,8},{1,5},{5,1},{9,13},{13,9},{2,6},{6,2},{1... | collective-permute-start | bytes 24584 | tf_op jit(solution)/shard_map/ppermute | solution.py:264

commit v7 on v6

--- a/solution.py
+++ b/solution.py
@@ -96,22 +96,19 @@
     return copy
 
 
-def fetches(store_hbm, smem_ref, i, target_ref, sems):
+def fetch(store_hbm, slot, target_ref, sem, c):
     rank = store_hbm.shape[2]
-    return [
-        pltpu.make_async_copy(
-            store_hbm.at[:, smem_ref[i * 8 + c, 0]],
-            target_ref.at[:, pl.ds(c * rank, rank)],
-            sems.at[c],
-        )
-        for c in range(CAP)
-    ]
-
-
-def start_some(waiting, count):
-    for copy in waiting[:count]:
-        copy.start()
-    del waiting[:count]
+    return pltpu.make_async_copy(
+        store_hbm.at[:, slot], target_ref.at[:, pl.ds(pl.multiple_of(c * rank, rank), rank)], sem
+    )
+
+
+def each_slot(body):
+    def step(c, carry):
+        body(c)
+        return carry
+
+    lax.fori_loop(0, CAP, step, 0)
 
 
 def base_kernel(tensors, early, down_hbm, x_ref, w_ref, *refs):
@@ -120,8 +117,15 @@
     layers, _, depth = x_ref.shape
     width = keep_ref.shape[3]
     slots = slot_copy(block_refs, depth // HALVES, slot_vmem, slot_smem, slot_sem)
+    slots.wait()
+
+    def copy(i, c):
+        slot = slot_smem[i * 8 + c, 0]
+        return fetch(down_hbm, slot, chosen_ref.at[i], sems.at[i, c], c)
+
+    for i in range(early):
+        each_slot(lambda c, i=i: copy(i, c).start())
     me = lax.axis_index("tensor")
-    copies, waiting = [], []
     for i, mask in enumerate(chunk_order(tensors)):
         out_ref = keep_ref if i < tensors // 2 else send_ref
         columns = pl.ds(pl.multiple_of((me ^ mask) * width, width), width)
@@ -129,15 +133,8 @@
             out_ref[i % (tensors // 2), layer] = jnp.dot(
                 x_ref[layer], w_ref[layer, :, columns], preferred_element_type=F32
             )
-            if not copies:
-                slots.wait()
-                for j in range(early):
-                    copies += fetches(down_hbm, slot_smem, j, chosen_ref.at[j], sems.at[j])
-                waiting = list(copies)
-            start_some(waiting, 2)
-    start_some(waiting, len(waiting))
-    for copy in copies:
-        copy.wait()
+    for i in range(early):
+        each_slot(lambda c, i=i: copy(i, c).wait())
 
 
 def down_kernel(early, down_hbm, up_hbm, early_ref, *refs):
@@ -148,13 +145,24 @@
     half = depth // HALVES
     block = layers * HALVES * CAP
     slots = slot_copy(block_refs, half, slot_vmem, slot_smem, slot_sem)
+    slots.wait()
+
+    def copy_down(i, c):
+        target_ref = late_ref.at[i - early]
+        return fetch(down_hbm, slot_smem[i * 8 + c, 0], target_ref, down_sems.at[i - early, c], c)
+
+    def copy_up(i, c):
+        return fetch(up_hbm, slot_smem[i * 8 + c, 0], up_ref.at[i], up_sems.at[i, c], c)
+
+    for i in range(early, stores):
+        each_slot(lambda c, i=i: copy_down(i, c).start())
+    for i in range(stores):
+        each_slot(lambda c, i=i: copy_up(i, c).start())
     row, column = iota((CAP * rank, block), 0), iota((CAP * rank, block), 1)
-    copies, waiting = [], []
     for i in range(stores):
         chosen_ref = early_ref.at[i] if i < early else late_ref.at[i - early]
         if i >= early:
-            for copy in copies[i - early]:
-                copy.wait()
+            each_slot(lambda c, i=i: copy_down(i, c).wait())
         total = jnp.zeros((rank, block), F32)
         for layer in range(layers):
             for part in range(HALVES):
@@ -168,21 +176,7 @@
                 product = jnp.where(mine, product, 0.0)
                 for c in range(CAP):
                     total = total + product[c * rank : (c + 1) * rank]
-                if not copies:
-                    slots.wait()
-                    for j in range(early, stores):
-                        at = j - early
-                        copies.append(
-                            fetches(down_hbm, slot_smem, j, late_ref.at[at], down_sems.at[at])
-                        )
-                    ups = [
-                        fetches(up_hbm, slot_smem, j, up_ref.at[j], up_sems.at[j])
-                        for j in range(stores)
-                    ]
-                    waiting = sum(copies + ups, [])
-                start_some(waiting, 2)
         kept_ref[:, i * block : (i + 1) * block] = total
-    start_some(waiting, len(waiting))
     turned = kept_ref[...].T
     for i in range(stores):
         for layer in range(layers):
@@ -190,9 +184,8 @@
             low_ref[(i * layers + layer) * CAP : (i * layers + layer + 1) * CAP] = (
                 turned[at : at + CAP] + turned[at + CAP : at + 2 * CAP]
             )
-    for group in ups:
-        for copy in group:
-            copy.wait()
+    for i in range(stores):
+        each_slot(lambda c, i=i: copy_up(i, c).wait())
 
 
 def pair_kernel(_, keep_ref, got_ref, own_ref, send_ref):

time: 33.6 us -> 31.1 us (0.926)
  Pallas kernels: 12.4 us -> 9.95 us
    pallas_call x1, Pallas kernels: 4.62 us -> 3.13 us  [local(): pl.pallas_call(functools.partial(base_kernel, tensors, early), out_shape=...]
    pallas_call x1, Pallas kernels: 5.16 us -> 4.24 us  [local(): pl.pallas_call(functools.partial(down_kernel, early), out_shape=[jax.Shap...]
  transfers between devices with their start and end apart: 11 -> 11, of which waited for: 4 -> 4; matrix products, arithmetic and copies ran while one was open for 0% -> 0% of each run, Pallas kernels for 30% -> 25%
where the time goes in v7:
time: 31.1 us; the launch traced here: 31 us
  starting transfers between devices  14.3 us (46%)
  Pallas kernels  9.95 us (32%)
  waiting for transfers between devices  5.97 us (19%)
  between operations  0.72 us (2%)
    ppermute x11, starting transfers between devices, swap(): return lax.ppermute(value, axis, [(i, i ^ by) for i in range(size)])  14.3 us
    ppermute x11, waiting for transfers between devices, swap(): return lax.ppermute(value, axis, [(i, i ^ by) for i in range(size)])  5.97 us
    pallas_call x1, Pallas kernels, local(): pl.pallas_call(functools.partial(down_kernel, early), out_shape=[jax.Shap...  4.24 us
    pallas_call x1, Pallas kernels, local(): pl.pallas_call(functools.partial(base_kernel, tensors, early), out_shape=...  3.13 us
    pallas_call x1, Pallas kernels, local(): pl.pallas_call(functools.partial(prepare_kernel, back), out_shape=[jax.Sh...  1.44 us
    pallas_call x1, Pallas kernels, local(): pl.pallas_call(final_kernel, out_shape=jax.ShapeDtypeStruct((layers, rows...  0.75 us
  transfers between devices with their start and end apart: 11, of which 4 were waited for; matrix products, arithmetic and copies ran while one was open for 0% of the time, Pallas kernels for 25%

profile of v7, /device:TPU:0, one launch (start us, length us, event | category | flops | bytes accessed | tf_op | source)
XLA Modules:
  0.0 31.0 jit_solution(16680585880826099656)
XLA Ops:
  0.0 1.4 %prepare.1 = (bf16[16,1152]{1,0:T(8,128)(2,1)S(1)}, bf16[16,1152]{1,0:T(8,128)(2,1)S(1)}, bf16[16,1152]{1,0:T(8,128)(2,1)S(1)}, bf16[16,1152]{1,0:T(8,128)(2,1)S(1)}, bf16[32,32]{1,0:T(8,128)(2,1)S(1)}) custom-call(s32[1,16]{1,0:T(1,128)} %bitcast.5, s32[1,16]{1,0:T(1,128)} %bitcast.6, bf16[2,16,2048]{2,1,0:T(8,128)(2,1)} %x_ref.1), custom_call_target="tpu_custom_call" | custom-call | flops 6920999936 | tf_op jit(solution)/shard_map/prepare/pallas_call | solution.py:261
  1.5 5.1 %collective-permute-start = (bf16[16,1152]{1,0:T(8,128)(2,1)S(1)}, bf16[16,1152]{1,0:T(8,128)(2,1)S(1)}, u32[]{:S(2)}, u32[]{:S(2)}) collective-permute-start(bf16[16,1152]{1,0:T(8,128)(2,1)S(1)} %get-tuple-element.23), channel_id=1, source_target_pairs={{0,12},{4,8},{8,4},{12,0},{1,13},{5,9},{9,5},{13,1},{2,14},{6,10},... | collective-permute-start | bytes 110600 | tf_op jit(solution)/shard_map/ppermute | solution.py:257
  6.6 0.0 collective-permute-start.1
  6.6 0.6 %collective-permute-start.2 = (bf16[16,1152]{1,0:T(8,128)(2,1)S(1)}, bf16[16,1152]{1,0:T(8,128)(2,1)S(1)}, u32[]{:S(2)}, u32[]{:S(2)}) collective-permute-start(bf16[16,1152]{1,0:T(8,128)(2,1)S(1)} %get-tuple-element.26), channel_id=1, source_target_pairs={{0,4},{4,0},{8,12},{12,8},{1,5},{5,1},{9,13},{13,9},{2,6},{6,2},{1... | collective-permute-start | bytes 110600 | tf_op jit(solution)/shard_map/ppermute | solution.py:257
  7.2 1.3 %collective-permute-done.refs_1_ = bf16[16,1152]{1,0:T(8,128)(2,1)S(1)} collective-permute-done((bf16[16,1152]{1,0:T(8,128)(2,1)S(1)}, bf16[16,1152]{1,0:T(8,128)(2,1)S(1)}, u32[]{:S(2)}, u32[]{:S(2)}) %collective-permute-start) | collective-permute-done | bytes 36896 | tf_op jit(solution)/shard_map/ppermute | solution.py:257
  8.5 3.1 %base.1 = (f32[2,2,16,512]{3,2,1,0:T(8,128)S(1)}, f32[2,2,16,512]{3,2,1,0:T(8,128)S(1)}, bf16[2,2,256,2048]{3,2,1,0:T(8,128)(2,1)S(1)}) custom-call(bf16[2,32,64,2048]{3,2,1,0:T(8,128)(2,1)} %bitcast.3, bf16[2,16,2048]{2,1,0:T(8,128)(2,1)S(1)} %copy-done.1, bf16[2,2048,2048]{2,1,0:T(8,128)(2,1)S(1)} %copy-done, ...), custom_call_target="tpu_custom_call" | custom-call | flops 6920999936 | tf_op jit(solution)/shard_map/base/pallas_call | solution.py:282
  11.7 0.1 collective-permute-start.3
  11.7 0.0 collective-permute-done.1.refs_2_
  11.8 4.2 %down.1 = (f32[32,64]{1,0:T(8,128)S(1)}, bf16[4,2,256,512]{3,2,1,0:T(8,128)(2,1)S(1)}) custom-call(bf16[2,32,64,2048]{3,2,1,0:T(8,128)(2,1)} %bitcast.4, bf16[2,32,64,512]{3,2,1,0:T(8,128)(2,1)} %up_hbm.1, bf16[2,2,256,2048]{3,2,1,0:T(8,128)(2,1)S(1)} %get-tuple-element.24.early_ref, bf16[16,1152]{1,0:T(8,128)(2,1)S(1)} %get-tuple-element.22.refs_0_, ...), custom_call_target="tpu_custom_call" | custom-call | flops 4614000128 | tf_op jit(solution)/shard_map/down/pallas_call | solution.py:299
  16.0 2.0 %collective-permute-start.5 = (f32[32,64]{1,0:T(8,128)S(1)}, f32[32,64]{1,0:T(8,128)S(1)}, u32[]{:S(2)}, u32[]{:S(2)}) collective-permute-start(f32[32,64]{1,0:T(8,128)S(1)} %get-tuple-element.27._.refs_0_), channel_id=1, source_target_pairs={{0,3},{1,2},{2,1},{3,0},{4,7},{5,6},{6,5},{7,4},{8,11},{9,10},{10,... | collective-permute-start | bytes 24584 | tf_op jit(solution)/shard_map/ppermute | solution.py:257
  18.0 0.2 collective-permute-start.6
  18.2 0.0 collective-permute-start.7
  18.2 0.0 collective-permute-done.3.got_ref
  18.2 1.9 %collective-permute-start.4 = (f32[2,16,512]{2,1,0:T(8,128)S(1)}, f32[2,16,512]{2,1,0:T(8,128)S(1)}, u32[]{:S(2)}, u32[]{:S(2)}) collective-permute-start(f32[2,16,512]{2,1,0:T(8,128)S(1)} %get-tuple-element.31), channel_id=1, source_target_pairs={{0,2},{1,3},{2,0},{3,1},{4,6},{5,7},{6,4},{7,5},{8,10},{9,11},{10,... | collective-permute-start | bytes 196616 | tf_op jit(solution)/shard_map/ppermute | solution.py:257
  20.1 1.8 %collective-permute-done.6.refs_2_ = f32[32,64]{1,0:T(8,128)S(1)} collective-permute-done((f32[32,64]{1,0:T(8,128)S(1)}, f32[32,64]{1,0:T(8,128)S(1)}, u32[]{:S(2)}, u32[]{:S(2)}) %collective-permute-start.6) | collective-permute-done | bytes 8224 | tf_op jit(solution)/shard_map/ppermute | solution.py:257
  21.9 0.0 collective-permute-done.7.refs_3_
  21.9 0.4 %up.1 = (bf16[16,256]{1,0:T(8,128)(2,1)S(1)}, bf16[16,256]{1,0:T(8,128)(2,1)S(1)}, bf16[16,256]{1,0:T(8,128)(2,1)S(1)}, bf16[16,256]{1,0:T(8,128)(2,1)S(1)}) custom-call(f32[2,16,512]{2,1,0:T(8,128)S(1)} %get-tuple-element.30._.own_ref, bf16[4,2,256,512]{3,2,1,0:T(8,128)(2,1)S(1)} %get-tuple-element.32.up_ref, f32[32,64]{1,0:T(8,128)S(1)} %get-tuple-element.27._.refs_0_, ...), custom_call_target="tpu_custom_call" | custom-call | flops 1153500032 | tf_op jit(solution)/shard_map/up/pallas_call | solution.py:339
  22.3 3.4 %collective-permute-start.10 = (bf16[16,256]{1,0:T(8,128)(2,1)S(1)}, bf16[16,256]{1,0:T(8,128)(2,1)S(1)}, u32[]{:S(2)}, u32[]{:S(2)}) collective-permute-start(bf16[16,256]{1,0:T(8,128)(2,1)S(1)} %get-tuple-element.36), channel_id=1, source_target_pairs={{0,12},{4,8},{8,4},{12,0},{1,13},{5,9},{9,5},{13,1},{2,14},{6,10},... | collective-permute-start | bytes 24584 | tf_op jit(solution)/shard_map/ppermute | solution.py:257
  25.7 0.0 collective-permute-start.8
  25.7 1.0 %collective-permute-start.9 = (bf16[16,256]{1,0:T(8,128)(2,1)S(1)}, bf16[16,256]{1,0:T(8,128)(2,1)S(1)}, u32[]{:S(2)}, u32[]{:S(2)}) collective-permute-start(bf16[16,256]{1,0:T(8,128)(2,1)S(1)} %get-tuple-element.35), channel_id=1, source_target_pairs={{0,4},{4,0},{8,12},{12,8},{1,5},{5,1},{9,13},{13,9},{2,6},{6,2},{1... | collective-permute-start | bytes 24584 | tf_op jit(solution)/shard_map/ppermute | solution.py:257
  27.4 0.4 %collective-permute-done.10.refs_3_ = bf16[16,256]{1,0:T(8,128)(2,1)S(1)} collective-permute-done((bf16[16,256]{1,0:T(8,128)(2,1)S(1)}, bf16[16,256]{1,0:T(8,128)(2,1)S(1)}, u32[]{:S(2)}, u32[]{:S(2)}) %collective-permute-start.10) | collective-permute-done | bytes 8224 | tf_op jit(solution)/shard_map/ppermute | solution.py:257
  27.8 2.5 %collective-permute-done.8.refs_1_ = bf16[16,256]{1,0:T(8,128)(2,1)S(1)} collective-permute-done((bf16[16,256]{1,0:T(8,128)(2,1)S(1)}, bf16[16,256]{1,0:T(8,128)(2,1)S(1)}, u32[]{:S(2)}, u32[]{:S(2)}) %collective-permute-start.8) | collective-permute-done | bytes 8224 | tf_op jit(solution)/shard_map/ppermute | solution.py:257
  30.2 0.0 collective-permute-done.9.refs_2_
  30.2 0.7 %final.1 = bf16[2,16,512]{2,1,0:T(8,128)(2,1)} custom-call(s32[1]{0:T(128)S(6)} %copy.8.count_ref, bf16[32,32]{1,0:T(8,128)(2,1)S(1)} %get-tuple-element.21.pick_ref, f32[2,16,512]{2,1,0:T(8,128)S(1)} %get-tuple-element.30._.own_ref, f32[2,16,512]{2,1,0:T(8,128)S(1)} %collective-permute-done.4.got_ref, bf16[16,256]{1,0:T(8,128)(2,1)S(1)} %get-tuple-element.33.refs_0_, ...), custom_call_target="tpu_custom_call" | custom-call | flops 1153500032 | tf_op jit(solution)/shard_map/final/pallas_call | solution.py:350
  (8 shorter events, 0.0 us)
Async XLA Ops:
  0.0 8.5 %copy-start = (bf16[2,2048,2048]{2,1,0:T(8,128)(2,1)S(1)}, bf16[2,2048,2048]{2,1,0:T(8,128)(2,1)}, u32[]{:S(2)}) copy-start(bf16[2,2048,2048]{2,1,0:T(8,128)(2,1)} %w_ref.1) | copy-start | bytes 50331652
  0.0 8.5 %copy-start.1 = (bf16[2,16,2048]{2,1,0:T(8,128)(2,1)S(1)}, bf16[2,16,2048]{2,1,0:T(8,128)(2,1)}, u32[]{:S(2)}) copy-start(bf16[2,16,2048]{2,1,0:T(8,128)(2,1)} %x_ref.1) | copy-start | bytes 393220
  1.5 7.1 %collective-permute-start = (bf16[16,1152]{1,0:T(8,128)(2,1)S(1)}, bf16[16,1152]{1,0:T(8,128)(2,1)S(1)}, u32[]{:S(2)}, u32[]{:S(2)}) collective-permute-start(bf16[16,1152]{1,0:T(8,128)(2,1)S(1)} %get-tuple-element.23), channel_id=1, source_target_pairs={{0,12},{4,8},{8,4},{12,0},{1,13},{5,9},{9,5},{13,1},{2,14},{6,10},... | collective-permute-start | bytes 110600 | tf_op jit(solution)/shard_map/ppermute | solution.py:257
  6.6 5.2 %collective-permute-start.1 = (bf16[16,1152]{1,0:T(8,128)(2,1)S(1)}, bf16[16,1152]{1,0:T(8,128)(2,1)S(1)}, u32[]{:S(2)}, u32[]{:S(2)}) collective-permute-start(bf16[16,1152]{1,0:T(8,128)(2,1)S(1)} %get-tuple-element.25), channel_id=1, source_target_pairs={{0,8},{4,12},{8,0},{12,4},{1,9},{5,13},{9,1},{13,5},{2,10},{6,14},... | collective-permute-start | bytes 110600 | tf_op jit(solution)/shard_map/ppermute | solution.py:257
  6.6 5.2 %collective-permute-start.2 = (bf16[16,1152]{1,0:T(8,128)(2,1)S(1)}, bf16[16,1152]{1,0:T(8,128)(2,1)S(1)}, u32[]{:S(2)}, u32[]{:S(2)}) collective-permute-start(bf16[16,1152]{1,0:T(8,128)(2,1)S(1)} %get-tuple-element.26), channel_id=1, source_target_pairs={{0,4},{4,0},{8,12},{12,8},{1,5},{5,1},{9,13},{13,9},{2,6},{6,2},{1... | collective-permute-start | bytes 110600 | tf_op jit(solution)/shard_map/ppermute | solution.py:257
  11.7 6.5 %collective-permute-start.3 = (f32[2,2,16,512]{3,2,1,0:T(8,128)S(1)}, f32[2,2,16,512]{3,2,1,0:T(8,128)S(1)}, u32[]{:S(2)}, u32[]{:S(2)}) collective-permute-start(f32[2,2,16,512]{3,2,1,0:T(8,128)S(1)} %get-tuple-element.29), channel_id=1, source_target_pairs={{0,1},{1,0},{2,3},{3,2},{4,5},{5,4},{6,7},{7,6},{8,9},{9,8},{10,11... | collective-permute-start | bytes 393224 | tf_op jit(solution)/shard_map/ppermute | solution.py:257
  16.0 4.1 %collective-permute-start.5 = (f32[32,64]{1,0:T(8,128)S(1)}, f32[32,64]{1,0:T(8,128)S(1)}, u32[]{:S(2)}, u32[]{:S(2)}) collective-permute-start(f32[32,64]{1,0:T(8,128)S(1)} %get-tuple-element.27._.refs_0_), channel_id=1, source_target_pairs={{0,3},{1,2},{2,1},{3,0},{4,7},{5,6},{6,5},{7,4},{8,11},{9,10},{10,... | collective-permute-start | bytes 24584 | tf_op jit(solution)/shard_map/ppermute | solution.py:257
  18.0 3.9 %collective-permute-start.6 = (f32[32,64]{1,0:T(8,128)S(1)}, f32[32,64]{1,0:T(8,128)S(1)}, u32[]{:S(2)}, u32[]{:S(2)}) collective-permute-start(f32[32,64]{1,0:T(8,128)S(1)} %get-tuple-element.27._.refs_0_), channel_id=1, source_target_pairs={{0,2},{1,3},{2,0},{3,1},{4,6},{5,7},{6,4},{7,5},{8,10},{9,11},{10,... | collective-permute-start | bytes 24584 | tf_op jit(solution)/shard_map/ppermute | solution.py:257
  18.2 3.7 %collective-permute-start.7 = (f32[32,64]{1,0:T(8,128)S(1)}, f32[32,64]{1,0:T(8,128)S(1)}, u32[]{:S(2)}, u32[]{:S(2)}) collective-permute-start(f32[32,64]{1,0:T(8,128)S(1)} %get-tuple-element.27._.refs_0_), channel_id=1, source_target_pairs={{0,1},{1,0},{2,3},{3,2},{4,5},{5,4},{6,7},{7,6},{8,9},{9,8},{10,11... | collective-permute-start | bytes 24584 | tf_op jit(solution)/shard_map/ppermute | solution.py:257
  18.2 12.0 %collective-permute-start.4 = (f32[2,16,512]{2,1,0:T(8,128)S(1)}, f32[2,16,512]{2,1,0:T(8,128)S(1)}, u32[]{:S(2)}, u32[]{:S(2)}) collective-permute-start(f32[2,16,512]{2,1,0:T(8,128)S(1)} %get-tuple-element.31), channel_id=1, source_target_pairs={{0,2},{1,3},{2,0},{3,1},{4,6},{5,7},{6,4},{7,5},{8,10},{9,11},{10,... | collective-permute-start | bytes 196616 | tf_op jit(solution)/shard_map/ppermute | solution.py:257
  22.3 5.5 %collective-permute-start.10 = (bf16[16,256]{1,0:T(8,128)(2,1)S(1)}, bf16[16,256]{1,0:T(8,128)(2,1)S(1)}, u32[]{:S(2)}, u32[]{:S(2)}) collective-permute-start(bf16[16,256]{1,0:T(8,128)(2,1)S(1)} %get-tuple-element.36), channel_id=1, source_target_pairs={{0,12},{4,8},{8,4},{12,0},{1,13},{5,9},{9,5},{13,1},{2,14},{6,10},... | collective-permute-start | bytes 24584 | tf_op jit(solution)/shard_map/ppermute | solution.py:257
  25.7 4.5 %collective-permute-start.8 = (bf16[16,256]{1,0:T(8,128)(2,1)S(1)}, bf16[16,256]{1,0:T(8,128)(2,1)S(1)}, u32[]{:S(2)}, u32[]{:S(2)}) collective-permute-start(bf16[16,256]{1,0:T(8,128)(2,1)S(1)} %get-tuple-element.34), channel_id=1, source_target_pairs={{0,8},{4,12},{8,0},{12,4},{1,9},{5,13},{9,1},{13,5},{2,10},{6,14},... | collective-permute-start | bytes 24584 | tf_op jit(solution)/shard_map/ppermute | solution.py:257
  25.7 4.5 %collective-permute-start.9 = (bf16[16,256]{1,0:T(8,128)(2,1)S(1)}, bf16[16,256]{1,0:T(8,128)(2,1)S(1)}, u32[]{:S(2)}, u32[]{:S(2)}) collective-permute-start(bf16[16,256]{1,0:T(8,128)(2,1)S(1)} %get-tuple-element.35), channel_id=1, source_target_pairs={{0,4},{4,0},{8,12},{12,8},{1,5},{5,1},{9,13},{13,9},{2,6},{6,2},{1... | collective-permute-start | bytes 24584 | tf_op jit(solution)/shard_map/ppermute | solution.py:257

commit v8 on v7

--- a/solution.py
+++ b/solution.py
@@ -45,7 +45,7 @@
     ]
     for copy in copies:
         copy.start()
-    for copy in copies:
+    for copy in copies[:2]:
         copy.wait()
     layers, rows, depth = x_ref.shape
     half = depth // HALVES
@@ -54,6 +54,12 @@
     place = hop_row * block + rank_row
     places = jnp.concatenate([place + CAP * part for part in range(layers * HALVES)], axis=1)
     pick = iota((stores * block, layers * HALVES * rows), 0).astype(F32) == places
+    spots = iota((rows, pick_ref.shape[1]), 1).astype(F32)
+    spot = sum(jnp.where(hop_col == float(k), float(i), 0.0) for i, k in enumerate(back))
+    back_place = spot * (layers * CAP) + rank_col
+    for layer in range(layers):
+        pick_ref[layer * rows : (layer + 1) * rows] = (spots == back_place + layer * CAP).astype(BF16)
+    copies[2].wait()
     stacked = jnp.concatenate(
         [
             x_ref[layer, :, part * half : (part + 1) * half]
@@ -73,11 +79,6 @@
     for k, out_ref in enumerate(out_refs):
         out_ref[:, :half] = sent[k * block : (k + 1) * block]
         out_ref[:, half:] = slots[k * block : (k + 1) * block]
-    spots = iota((rows, pick_ref.shape[1]), 1).astype(F32)
-    spot = sum(jnp.where(hop_col == float(k), float(i), 0.0) for i, k in enumerate(back))
-    place = spot * (layers * CAP) + rank_col
-    for layer in range(layers):
-        pick_ref[layer * rows : (layer + 1) * rows] = (spots == place + layer * CAP).astype(BF16)
 
 
 def chunk_order(tensors):
@@ -87,13 +88,11 @@
     return rest + [mask + 1 for mask in rest]
 
 
-def slot_copy(block_refs, half, vmem_ref, smem_ref, sem):
+def read_slots(block_refs, half, slot_ref):
     for i, block_ref in enumerate(block_refs):
         tail = block_ref[:, half:].astype(F32)
-        vmem_ref[i * 8 : (i + 1) * 8] = tail[:8].astype(jnp.int32)
-    copy = pltpu.make_async_copy(vmem_ref, smem_ref, sem)
-    copy.start()
-    return copy
+        for c in range(CAP):
+            slot_ref[i * CAP + c] = tail[c, 0].astype(jnp.int32)
 
 
 def fetch(store_hbm, slot, target_ref, sem, c):
@@ -111,20 +110,22 @@
     lax.fori_loop(0, CAP, step, 0)
 
 
-def base_kernel(tensors, early, down_hbm, x_ref, w_ref, *refs):
+def base_kernel(tensors, early, down_hbm, up_hbm, x_ref, w_ref, *refs):
     block_refs, refs = refs[:early], refs[early:]
-    keep_ref, send_ref, chosen_ref, slot_vmem, slot_smem, slot_sem, sems = refs
+    keep_ref, send_ref, chosen_ref, up_ref, slot_ref, down_sems, up_sems = refs
     layers, _, depth = x_ref.shape
     width = keep_ref.shape[3]
-    slots = slot_copy(block_refs, depth // HALVES, slot_vmem, slot_smem, slot_sem)
-    slots.wait()
-
-    def copy(i, c):
-        slot = slot_smem[i * 8 + c, 0]
-        return fetch(down_hbm, slot, chosen_ref.at[i], sems.at[i, c], c)
-
-    for i in range(early):
-        each_slot(lambda c, i=i: copy(i, c).start())
+    read_slots(block_refs, depth // HALVES, slot_ref)
+
+    def copy_down(i, c):
+        return fetch(down_hbm, slot_ref[i * CAP + c], chosen_ref.at[i], down_sems.at[i, c], c)
+
+    def copy_up(i, c):
+        return fetch(up_hbm, slot_ref[i * CAP + c], up_ref.at[i], up_sems.at[i, c], c)
+
+    for copy in (copy_down, copy_up):
+        for i in range(early):
+            each_slot(lambda c, i=i, copy=copy: copy(i, c).start())
     me = lax.axis_index("tensor")
     for i, mask in enumerate(chunk_order(tensors)):
         out_ref = keep_ref if i < tensors // 2 else send_ref
@@ -133,36 +134,35 @@
             out_ref[i % (tensors // 2), layer] = jnp.dot(
                 x_ref[layer], w_ref[layer, :, columns], preferred_element_type=F32
             )
-    for i in range(early):
-        each_slot(lambda c, i=i: copy(i, c).wait())
+    for copy in (copy_down, copy_up):
+        for i in range(early):
+            each_slot(lambda c, i=i, copy=copy: copy(i, c).wait())
 
 
 def down_kernel(early, down_hbm, up_hbm, early_ref, *refs):
-    stores = len(refs) - 9
-    block_refs, (low_ref, up_ref, late_ref, *refs) = refs[:stores], refs[stores:]
-    slot_vmem, slot_smem, slot_sem, down_sems, up_sems, kept_ref = refs
+    stores = len(refs) - 7
+    block_refs, refs = refs[:stores], refs[stores:]
+    low_ref, up_ref, late_ref, slot_ref, down_sems, up_sems, kept_ref = refs
     layers, _, rank, depth = down_hbm.shape
     half = depth // HALVES
     block = layers * HALVES * CAP
-    slots = slot_copy(block_refs, half, slot_vmem, slot_smem, slot_sem)
-    slots.wait()
+    late = stores - early
+    read_slots(block_refs[early:], half, slot_ref)
 
     def copy_down(i, c):
-        target_ref = late_ref.at[i - early]
-        return fetch(down_hbm, slot_smem[i * 8 + c, 0], target_ref, down_sems.at[i - early, c], c)
+        return fetch(down_hbm, slot_ref[i * CAP + c], late_ref.at[i], down_sems.at[i, c], c)
 
     def copy_up(i, c):
-        return fetch(up_hbm, slot_smem[i * 8 + c, 0], up_ref.at[i], up_sems.at[i, c], c)
-
-    for i in range(early, stores):
-        each_slot(lambda c, i=i: copy_down(i, c).start())
-    for i in range(stores):
-        each_slot(lambda c, i=i: copy_up(i, c).start())
+        return fetch(up_hbm, slot_ref[i * CAP + c], up_ref.at[i], up_sems.at[i, c], c)
+
+    for copy in (copy_down, copy_up):
+        for i in range(late):
+            each_slot(lambda c, i=i, copy=copy: copy(i, c).start())
     row, column = iota((CAP * rank, block), 0), iota((CAP * rank, block), 1)
     for i in range(stores):
         chosen_ref = early_ref.at[i] if i < early else late_ref.at[i - early]
         if i >= early:
-            each_slot(lambda c, i=i: copy_down(i, c).wait())
+            each_slot(lambda c, i=i: copy_down(i - early, c).wait())
         total = jnp.zeros((rank, block), F32)
         for layer in range(layers):
             for part in range(HALVES):
@@ -184,7 +184,7 @@
             low_ref[(i * layers + layer) * CAP : (i * layers + layer + 1) * CAP] = (
                 turned[at : at + CAP] + turned[at + CAP : at + 2 * CAP]
             )
-    for i in range(stores):
+    for i in range(late):
         each_slot(lambda c, i=i: copy_up(i, c).wait())
 
 
@@ -193,25 +193,26 @@
     send_ref[...] = keep_ref[1] + got_ref[1]
 
 
-def up_kernel(tensors, _, up_ref, *refs):
+def up_kernel(tensors, _, early_ref, late_ref, *refs):
     low_refs, out_refs = refs[:tensors], refs[tensors:]
-    stores, layers, depth, width = up_ref.shape
+    early, layers, depth, width = early_ref.shape
     rank = depth // CAP
     half = width // HALVES
     low = low_refs[0][...]
     for low_ref in low_refs[1:]:
         low = low + low_ref[...]
     row, column = iota((CAP, depth), 0), iota((CAP, depth), 1)
-    for i in range(stores):
+    for i, out_ref in enumerate(out_refs):
+        up_ref = early_ref.at[i] if i < early else late_ref.at[i - early]
         terms = []
         for layer in range(layers):
             at = (i * layers + layer) * CAP
             spread = jnp.concatenate([low[at : at + CAP]] * CAP, axis=1)
             spread = jnp.where(row == column // rank, spread, 0.0).astype(BF16)
-            terms.append(jnp.dot(spread, up_ref[i, layer], preferred_element_type=F32))
+            terms.append(jnp.dot(spread, up_ref[layer], preferred_element_type=F32))
         terms = jnp.concatenate(terms, axis=0)
         parts = [terms[:, part * half : (part + 1) * half] for part in range(HALVES)]
-        out_refs[i][...] = jnp.concatenate(parts, axis=0).astype(BF16)
+        out_ref[...] = jnp.concatenate(parts, axis=0).astype(BF16)
 
 
 def final_kernel(count_ref, pick_ref, own_ref, got_ref, *refs):
@@ -256,7 +257,7 @@
             return value
         return lax.ppermute(value, axis, [(i, i ^ by) for i in range(size)])
 
-    order = [0] + list(range(stores - 1, 0, -1))
+    order = [0] + list(range(stores // 2, stores)) + list(range(stores // 2 - 1, 0, -1))
     back = [0] + order[2:] + order[1:2]
     *payloads, pick = pl.pallas_call(
         functools.partial(prepare_kernel, back),
@@ -279,38 +280,39 @@
     blocks = [swap(payloads[k], "store", stores, k) for k in order]
 
     early = min(2, stores)
-    keep, send, chosen = pl.pallas_call(
+    keep, send, chosen, early_up = pl.pallas_call(
         functools.partial(base_kernel, tensors, early),
         out_shape=[jax.ShapeDtypeStruct((tensors // 2, layers, rows, width), F32)] * 2
-        + [jax.ShapeDtypeStruct((early, layers, CAP * rank, depth), BF16)],
-        in_specs=[HBM] + [VMEM] * (2 + early),
-        out_specs=[VMEM] * 3,
+        + [
+            jax.ShapeDtypeStruct((early, layers, CAP * rank, depth), BF16),
+            jax.ShapeDtypeStruct((early, layers, CAP * rank, width), BF16),
+        ],
+        in_specs=[HBM] * 2 + [VMEM] * (2 + early),
+        out_specs=[VMEM] * 4,
         scratch_shapes=[
-            pltpu.VMEM((early * 8, LANES), jnp.int32),
-            pltpu.SMEM((early * 8, LANES), jnp.int32),
-            pltpu.SemaphoreType.DMA,
+            pltpu.SMEM((early * CAP,), jnp.int32),
+            pltpu.SemaphoreType.DMA((early, CAP)),
             pltpu.SemaphoreType.DMA((early, CAP)),
         ],
         compiler_params=params(),
         cost_estimate=cost(6),
         name="base",
-    )(down, x, w, *blocks[:early])
-
-    low, chosen = pl.pallas_call(
+    )(down, up, x, w, *blocks[:early])
+
+    late = stores - early
+    low, late_up = pl.pallas_call(
         functools.partial(down_kernel, early),
         out_shape=[
             jax.ShapeDtypeStruct((stores * layers * CAP, rank), F32),
-            jax.ShapeDtypeStruct((stores, layers, CAP * rank, width), BF16),
+            jax.ShapeDtypeStruct((late, layers, CAP * rank, width), BF16),
         ],
         in_specs=[HBM] * 2 + [VMEM] * (1 + stores),
         out_specs=[VMEM] * 2,
         scratch_shapes=[
-            pltpu.VMEM((stores - early, layers, CAP * rank, depth), BF16),
-            pltpu.VMEM((stores * 8, LANES), jnp.int32),
-            pltpu.SMEM((stores * 8, LANES), jnp.int32),
-            pltpu.SemaphoreType.DMA,
-            pltpu.SemaphoreType.DMA((stores - early, CAP)),
-            pltpu.SemaphoreType.DMA((stores, CAP)),
+            pltpu.VMEM((late, layers, CAP * rank, depth), BF16),
+            pltpu.SMEM((late * CAP,), jnp.int32),
+            pltpu.SemaphoreType.DMA((late, CAP)),
+            pltpu.SemaphoreType.DMA((late, CAP)),
             pltpu.VMEM((rank, stores * block), F32),
         ],
         compiler_params=params(LARGE),
@@ -339,12 +341,12 @@
     terms = pl.pallas_call(
         functools.partial(up_kernel, tensors),
         out_shape=[jax.ShapeDtypeStruct((layers * HALVES * CAP, width // HALVES), BF16)] * stores,
-        in_specs=[ANY] + [VMEM] * (1 + tensors),
+        in_specs=[ANY] + [VMEM] * (2 + tensors),
         out_specs=[VMEM] * stores,
         compiler_params=params(),
         cost_estimate=cost(1),
         name="up",
-    )(own, chosen, *lows)
+    )(own, early_up, late_up, *lows)
     returned = [swap(terms[order.index(k)], "store", stores, k) for k in back]
 
     return pl.pallas_call(

time: 31.1 us -> 29 us (0.932)
  Pallas kernels: 9.95 us -> 8.45 us
  starting transfers between devices: 14.3 us -> 13.9 us
    pallas_call x1, Pallas kernels: 4.24 us -> 3.35 us  [local(): pl.pallas_call(functools.partial(down_kernel, early), out_shape=[jax.Shap...]
    ppermute x11, starting transfers between devices: 14.3 us -> 13.9 us  [swap(): return lax.ppermute(value, axis, [(i, i ^ by) for i in range(size)])]
    pallas_call x1, Pallas kernels: 3.13 us -> 2.68 us  [local(): pl.pallas_call(functools.partial(base_kernel, tensors, early), out_shape=...]
  transfers between devices with their start and end apart: 11 -> 11, of which waited for: 4 -> 4; matrix products, arithmetic and copies ran while one was open for 0% -> 0% of each run, Pallas kernels for 25% -> 22%
where the time goes in v8:
time: 29 us; the launch traced here: 28.9 us
  starting transfers between devices  13.9 us (48%)
  Pallas kernels  8.45 us (29%)
  waiting for transfers between devices  5.82 us (20%)
  between operations  0.71 us (2%)
    ppermute x11, starting transfers between devices, swap(): return lax.ppermute(value, axis, [(i, i ^ by) for i in range(size)])  13.9 us
    ppermute x11, waiting for transfers between devices, swap(): return lax.ppermute(value, axis, [(i, i ^ by) for i in range(size)])  5.82 us
    pallas_call x1, Pallas kernels, local(): pl.pallas_call(functools.partial(down_kernel, early), out_shape=[jax.Shap...  3.35 us
    pallas_call x1, Pallas kernels, local(): pl.pallas_call(functools.partial(base_kernel, tensors, early), out_shape=...  2.68 us
    pallas_call x1, Pallas kernels, local(): pl.pallas_call(functools.partial(prepare_kernel, back), out_shape=[jax.Sh...  1.28 us
    pallas_call x1, Pallas kernels, local(): pl.pallas_call(final_kernel, out_shape=jax.ShapeDtypeStruct((layers, rows...  0.75 us
  transfers between devices with their start and end apart: 11, of which 4 were waited for; matrix products, arithmetic and copies ran while one was open for 0% of the time, Pallas kernels for 22%

profile of v8, /device:TPU:0, one launch (start us, length us, event | category | flops | bytes accessed | tf_op | source)
XLA Modules:
  0.0 28.9 jit_solution(1900659475281663316)
XLA Ops:
  0.0 1.3 %prepare.1 = (bf16[16,1152]{1,0:T(8,128)(2,1)S(1)}, bf16[16,1152]{1,0:T(8,128)(2,1)S(1)}, bf16[16,1152]{1,0:T(8,128)(2,1)S(1)}, bf16[16,1152]{1,0:T(8,128)(2,1)S(1)}, bf16[32,32]{1,0:T(8,128)(2,1)S(1)}) custom-call(s32[1,16]{1,0:T(1,128)} %bitcast.5, s32[1,16]{1,0:T(1,128)} %bitcast.6, bf16[2,16,2048]{2,1,0:T(8,128)(2,1)} %x_ref.1), custom_call_target="tpu_custom_call" | custom-call | flops 6920999936 | tf_op jit(solution)/shard_map/prepare/pallas_call | solution.py:262
  1.3 4.1 %collective-permute-start = (bf16[16,1152]{1,0:T(8,128)(2,1)S(1)}, bf16[16,1152]{1,0:T(8,128)(2,1)S(1)}, u32[]{:S(2)}, u32[]{:S(2)}) collective-permute-start(bf16[16,1152]{1,0:T(8,128)(2,1)S(1)} %get-tuple-element.24), channel_id=1, source_target_pairs={{0,8},{4,12},{8,0},{12,4},{1,9},{5,13},{9,1},{13,5},{2,10},{6,14},... | collective-permute-start | bytes 110600 | tf_op jit(solution)/shard_map/ppermute | solution.py:258
  5.4 1.4 %collective-permute-start.1 = (bf16[16,1152]{1,0:T(8,128)(2,1)S(1)}, bf16[16,1152]{1,0:T(8,128)(2,1)S(1)}, u32[]{:S(2)}, u32[]{:S(2)}) collective-permute-start(bf16[16,1152]{1,0:T(8,128)(2,1)S(1)} %get-tuple-element.26), channel_id=1, source_target_pairs={{0,12},{4,8},{8,4},{12,0},{1,13},{5,9},{9,5},{13,1},{2,14},{6,10},... | collective-permute-start | bytes 110600 | tf_op jit(solution)/shard_map/ppermute | solution.py:258
  6.7 0.2 collective-permute-start.2
  7.0 0.8 %collective-permute-done.refs_1_ = bf16[16,1152]{1,0:T(8,128)(2,1)S(1)} collective-permute-done((bf16[16,1152]{1,0:T(8,128)(2,1)S(1)}, bf16[16,1152]{1,0:T(8,128)(2,1)S(1)}, u32[]{:S(2)}, u32[]{:S(2)}) %collective-permute-start) | collective-permute-done | bytes 36896 | tf_op jit(solution)/shard_map/ppermute | solution.py:258
  7.7 2.7 %base.1 = (f32[2,2,16,512]{3,2,1,0:T(8,128)S(1)}, f32[2,2,16,512]{3,2,1,0:T(8,128)S(1)}, bf16[2,2,256,2048]{3,2,1,0:T(8,128)(2,1)S(1)}, bf16[2,2,256,512]{3,2,1,0:T(8,128)(2,1)S(1)}) custom-call(bf16[2,32,64,2048]{3,2,1,0:T(8,128)(2,1)} %bitcast.3, bf16[2,32,64,512]{3,2,1,0:T(8,128)(2,1)} %up_hbm.3, bf16[2,16,2048]{2,1,0:T(8,128)(2,1)S(1)} %copy-done.1, ...), custom_call_target="tpu_custom_call" | custom-call | flops 6920999936 | tf_op jit(solution)/shard_map/base/pallas_call | solution.py:283
  10.4 0.1 collective-permute-start.3
  10.5 0.7 %collective-permute-done.1.refs_2_ = bf16[16,1152]{1,0:T(8,128)(2,1)S(1)} collective-permute-done((bf16[16,1152]{1,0:T(8,128)(2,1)S(1)}, bf16[16,1152]{1,0:T(8,128)(2,1)S(1)}, u32[]{:S(2)}, u32[]{:S(2)}) %collective-permute-start.1) | collective-permute-done | bytes 36896 | tf_op jit(solution)/shard_map/ppermute | solution.py:258
  11.1 3.3 %down.1 = (f32[32,64]{1,0:T(8,128)S(1)}, bf16[2,2,256,512]{3,2,1,0:T(8,128)(2,1)S(1)}) custom-call(bf16[2,32,64,2048]{3,2,1,0:T(8,128)(2,1)} %bitcast.4, bf16[2,32,64,512]{3,2,1,0:T(8,128)(2,1)} %up_hbm.3, bf16[2,2,256,2048]{3,2,1,0:T(8,128)(2,1)S(1)} %get-tuple-element.25.early_ref, bf16[16,1152]{1,0:T(8,128)(2,1)S(1)} %get-tuple-element.23.refs_0_, ...), custom_call_target="tpu_custom_call" | custom-call | flops 4614000128 | tf_op jit(solution)/shard_map/down/pallas_call | solution.py:303
  14.5 1.2 %collective-permute-start.5 = (f32[32,64]{1,0:T(8,128)S(1)}, f32[32,64]{1,0:T(8,128)S(1)}, u32[]{:S(2)}, u32[]{:S(2)}) collective-permute-start(f32[32,64]{1,0:T(8,128)S(1)} %get-tuple-element.28._.refs_0_), channel_id=1, source_target_pairs={{0,3},{1,2},{2,1},{3,0},{4,7},{5,6},{6,5},{7,4},{8,11},{9,10},{10,... | collective-permute-start | bytes 24584 | tf_op jit(solution)/shard_map/ppermute | solution.py:258
  15.7 0.4 %collective-permute-start.6 = (f32[32,64]{1,0:T(8,128)S(1)}, f32[32,64]{1,0:T(8,128)S(1)}, u32[]{:S(2)}, u32[]{:S(2)}) collective-permute-start(f32[32,64]{1,0:T(8,128)S(1)} %get-tuple-element.28._.refs_0_), channel_id=1, source_target_pairs={{0,2},{1,3},{2,0},{3,1},{4,6},{5,7},{6,4},{7,5},{8,10},{9,11},{10,... | collective-permute-start | bytes 24584 | tf_op jit(solution)/shard_map/ppermute | solution.py:258
  16.1 0.3 collective-permute-start.7
  16.4 0.0 collective-permute-done.3.got_ref
  16.5 1.6 %collective-permute-start.4 = (f32[2,16,512]{2,1,0:T(8,128)S(1)}, f32[2,16,512]{2,1,0:T(8,128)S(1)}, u32[]{:S(2)}, u32[]{:S(2)}) collective-permute-start(f32[2,16,512]{2,1,0:T(8,128)S(1)} %get-tuple-element.32), channel_id=1, source_target_pairs={{0,2},{1,3},{2,0},{3,1},{4,6},{5,7},{6,4},{7,5},{8,10},{9,11},{10,... | collective-permute-start | bytes 196616 | tf_op jit(solution)/shard_map/ppermute | solution.py:258
  18.0 1.6 %collective-permute-done.6.refs_2_ = f32[32,64]{1,0:T(8,128)S(1)} collective-permute-done((f32[32,64]{1,0:T(8,128)S(1)}, f32[32,64]{1,0:T(8,128)S(1)}, u32[]{:S(2)}, u32[]{:S(2)}) %collective-permute-start.6) | collective-permute-done | bytes 8224 | tf_op jit(solution)/shard_map/ppermute | solution.py:258
  19.6 0.0 collective-permute-done.7.refs_3_
  19.6 0.4 %up.1 = (bf16[16,256]{1,0:T(8,128)(2,1)S(1)}, bf16[16,256]{1,0:T(8,128)(2,1)S(1)}, bf16[16,256]{1,0:T(8,128)(2,1)S(1)}, bf16[16,256]{1,0:T(8,128)(2,1)S(1)}) custom-call(f32[2,16,512]{2,1,0:T(8,128)S(1)} %get-tuple-element.31._.own_ref, bf16[2,2,256,512]{3,2,1,0:T(8,128)(2,1)S(1)} %get-tuple-element.33.early_ref, ...), custom_call_target="tpu_custom_call" | custom-call | flops 1153500032 | tf_op jit(solution)/shard_map/up/pallas_call | solution.py:341
  20.0 2.7 %collective-permute-start.10 = (bf16[16,256]{1,0:T(8,128)(2,1)S(1)}, bf16[16,256]{1,0:T(8,128)(2,1)S(1)}, u32[]{:S(2)}, u32[]{:S(2)}) collective-permute-start(bf16[16,256]{1,0:T(8,128)(2,1)S(1)} %get-tuple-element.38), channel_id=1, source_target_pairs={{0,8},{4,12},{8,0},{12,4},{1,9},{5,13},{9,1},{13,5},{2,10},{6,14},... | collective-permute-start | bytes 24584 | tf_op jit(solution)/shard_map/ppermute | solution.py:258
  22.7 1.5 %collective-permute-start.8 = (bf16[16,256]{1,0:T(8,128)(2,1)S(1)}, bf16[16,256]{1,0:T(8,128)(2,1)S(1)}, u32[]{:S(2)}, u32[]{:S(2)}) collective-permute-start(bf16[16,256]{1,0:T(8,128)(2,1)S(1)} %get-tuple-element.36), channel_id=1, source_target_pairs={{0,12},{4,8},{8,4},{12,0},{1,13},{5,9},{9,5},{13,1},{2,14},{6,10},... | collective-permute-start | bytes 24584 | tf_op jit(solution)/shard_map/ppermute | solution.py:258
  24.2 0.5 %collective-permute-start.9 = (bf16[16,256]{1,0:T(8,128)(2,1)S(1)}, bf16[16,256]{1,0:T(8,128)(2,1)S(1)}, u32[]{:S(2)}, u32[]{:S(2)}) collective-permute-start(bf16[16,256]{1,0:T(8,128)(2,1)S(1)} %get-tuple-element.37), channel_id=1, source_target_pairs={{0,4},{4,0},{8,12},{12,8},{1,5},{5,1},{9,13},{13,9},{2,6},{6,2},{1... | collective-permute-start | bytes 24584 | tf_op jit(solution)/shard_map/ppermute | solution.py:258
  25.3 2.8 %collective-permute-done.8.refs_1_ = bf16[16,256]{1,0:T(8,128)(2,1)S(1)} collective-permute-done((bf16[16,256]{1,0:T(8,128)(2,1)S(1)}, bf16[16,256]{1,0:T(8,128)(2,1)S(1)}, u32[]{:S(2)}, u32[]{:S(2)}) %collective-permute-start.8) | collective-permute-done | bytes 8224 | tf_op jit(solution)/shard_map/ppermute | solution.py:258
  28.1 0.0 collective-permute-done.9.refs_2_
  28.1 0.0 collective-permute-done.4.got_ref
  28.1 0.7 %final.1 = bf16[2,16,512]{2,1,0:T(8,128)(2,1)} custom-call(s32[1]{0:T(128)S(6)} %copy.8.count_ref, bf16[32,32]{1,0:T(8,128)(2,1)S(1)} %get-tuple-element.22.pick_ref, f32[2,16,512]{2,1,0:T(8,128)S(1)} %get-tuple-element.31._.own_ref, f32[2,16,512]{2,1,0:T(8,128)S(1)} %collective-permute-done.4.got_ref, bf16[16,256]{1,0:T(8,128)(2,1)S(1)} %get-tuple-element.35.refs_0_, ...), custom_call_target="tpu_custom_call" | custom-call | flops 1153500032 | tf_op jit(solution)/shard_map/final/pallas_call | solution.py:352
  (8 shorter events, 0.0 us)
Async XLA Ops:
  0.0 7.7 %copy-start.1 = (bf16[2,16,2048]{2,1,0:T(8,128)(2,1)S(1)}, bf16[2,16,2048]{2,1,0:T(8,128)(2,1)}, u32[]{:S(2)}) copy-start(bf16[2,16,2048]{2,1,0:T(8,128)(2,1)} %x_ref.1) | copy-start | bytes 393220
  0.0 7.7 %copy-start = (bf16[2,2048,2048]{2,1,0:T(8,128)(2,1)S(1)}, bf16[2,2048,2048]{2,1,0:T(8,128)(2,1)}, u32[]{:S(2)}) copy-start(bf16[2,2048,2048]{2,1,0:T(8,128)(2,1)} %w_ref.1) | copy-start | bytes 50331652
  1.3 6.4 %collective-permute-start = (bf16[16,1152]{1,0:T(8,128)(2,1)S(1)}, bf16[16,1152]{1,0:T(8,128)(2,1)S(1)}, u32[]{:S(2)}, u32[]{:S(2)}) collective-permute-start(bf16[16,1152]{1,0:T(8,128)(2,1)S(1)} %get-tuple-element.24), channel_id=1, source_target_pairs={{0,8},{4,12},{8,0},{12,4},{1,9},{5,13},{9,1},{13,5},{2,10},{6,14},... | collective-permute-start | bytes 110600 | tf_op jit(solution)/shard_map/ppermute | solution.py:258
  5.4 5.8 %collective-permute-start.1 = (bf16[16,1152]{1,0:T(8,128)(2,1)S(1)}, bf16[16,1152]{1,0:T(8,128)(2,1)S(1)}, u32[]{:S(2)}, u32[]{:S(2)}) collective-permute-start(bf16[16,1152]{1,0:T(8,128)(2,1)S(1)} %get-tuple-element.26), channel_id=1, source_target_pairs={{0,12},{4,8},{8,4},{12,0},{1,13},{5,9},{9,5},{13,1},{2,14},{6,10},... | collective-permute-start | bytes 110600 | tf_op jit(solution)/shard_map/ppermute | solution.py:258
  6.7 4.4 %collective-permute-start.2 = (bf16[16,1152]{1,0:T(8,128)(2,1)S(1)}, bf16[16,1152]{1,0:T(8,128)(2,1)S(1)}, u32[]{:S(2)}, u32[]{:S(2)}) collective-permute-start(bf16[16,1152]{1,0:T(8,128)(2,1)S(1)} %get-tuple-element.27), channel_id=1, source_target_pairs={{0,4},{4,0},{8,12},{12,8},{1,5},{5,1},{9,13},{13,9},{2,6},{6,2},{1... | collective-permute-start | bytes 110600 | tf_op jit(solution)/shard_map/ppermute | solution.py:258
  10.4 6.0 %collective-permute-start.3 = (f32[2,2,16,512]{3,2,1,0:T(8,128)S(1)}, f32[2,2,16,512]{3,2,1,0:T(8,128)S(1)}, u32[]{:S(2)}, u32[]{:S(2)}) collective-permute-start(f32[2,2,16,512]{3,2,1,0:T(8,128)S(1)} %get-tuple-element.30), channel_id=1, source_target_pairs={{0,1},{1,0},{2,3},{3,2},{4,5},{5,4},{6,7},{7,6},{8,9},{9,8},{10,11... | collective-permute-start | bytes 393224 | tf_op jit(solution)/shard_map/ppermute | solution.py:258
  14.5 3.5 %collective-permute-start.5 = (f32[32,64]{1,0:T(8,128)S(1)}, f32[32,64]{1,0:T(8,128)S(1)}, u32[]{:S(2)}, u32[]{:S(2)}) collective-permute-start(f32[32,64]{1,0:T(8,128)S(1)} %get-tuple-element.28._.refs_0_), channel_id=1, source_target_pairs={{0,3},{1,2},{2,1},{3,0},{4,7},{5,6},{6,5},{7,4},{8,11},{9,10},{10,... | collective-permute-start | bytes 24584 | tf_op jit(solution)/shard_map/ppermute | solution.py:258
  15.7 3.9 %collective-permute-start.6 = (f32[32,64]{1,0:T(8,128)S(1)}, f32[32,64]{1,0:T(8,128)S(1)}, u32[]{:S(2)}, u32[]{:S(2)}) collective-permute-start(f32[32,64]{1,0:T(8,128)S(1)} %get-tuple-element.28._.refs_0_), channel_id=1, source_target_pairs={{0,2},{1,3},{2,0},{3,1},{4,6},{5,7},{6,4},{7,5},{8,10},{9,11},{10,... | collective-permute-start | bytes 24584 | tf_op jit(solution)/shard_map/ppermute | solution.py:258
  16.1 3.5 %collective-permute-start.7 = (f32[32,64]{1,0:T(8,128)S(1)}, f32[32,64]{1,0:T(8,128)S(1)}, u32[]{:S(2)}, u32[]{:S(2)}) collective-permute-start(f32[32,64]{1,0:T(8,128)S(1)} %get-tuple-element.28._.refs_0_), channel_id=1, source_target_pairs={{0,1},{1,0},{2,3},{3,2},{4,5},{5,4},{6,7},{7,6},{8,9},{9,8},{10,11... | collective-permute-start | bytes 24584 | tf_op jit(solution)/shard_map/ppermute | solution.py:258
  16.5 11.7 %collective-permute-start.4 = (f32[2,16,512]{2,1,0:T(8,128)S(1)}, f32[2,16,512]{2,1,0:T(8,128)S(1)}, u32[]{:S(2)}, u32[]{:S(2)}) collective-permute-start(f32[2,16,512]{2,1,0:T(8,128)S(1)} %get-tuple-element.32), channel_id=1, source_target_pairs={{0,2},{1,3},{2,0},{3,1},{4,6},{5,7},{6,4},{7,5},{8,10},{9,11},{10,... | collective-permute-start | bytes 196616 | tf_op jit(solution)/shard_map/ppermute | solution.py:258
  20.0 5.3 %collective-permute-start.10 = (bf16[16,256]{1,0:T(8,128)(2,1)S(1)}, bf16[16,256]{1,0:T(8,128)(2,1)S(1)}, u32[]{:S(2)}, u32[]{:S(2)}) collective-permute-start(bf16[16,256]{1,0:T(8,128)(2,1)S(1)} %get-tuple-element.38), channel_id=1, source_target_pairs={{0,8},{4,12},{8,0},{12,4},{1,9},{5,13},{9,1},{13,5},{2,10},{6,14},... | collective-permute-start | bytes 24584 | tf_op jit(solution)/shard_map/ppermute | solution.py:258
  22.7 5.4 %collective-permute-start.8 = (bf16[16,256]{1,0:T(8,128)(2,1)S(1)}, bf16[16,256]{1,0:T(8,128)(2,1)S(1)}, u32[]{:S(2)}, u32[]{:S(2)}) collective-permute-start(bf16[16,256]{1,0:T(8,128)(2,1)S(1)} %get-tuple-element.36), channel_id=1, source_target_pairs={{0,12},{4,8},{8,4},{12,0},{1,13},{5,9},{9,5},{13,1},{2,14},{6,10},... | collective-permute-start | bytes 24584 | tf_op jit(solution)/shard_map/ppermute | solution.py:258
  24.2 4.0 %collective-permute-start.9 = (bf16[16,256]{1,0:T(8,128)(2,1)S(1)}, bf16[16,256]{1,0:T(8,128)(2,1)S(1)}, u32[]{:S(2)}, u32[]{:S(2)}) collective-permute-start(bf16[16,256]{1,0:T(8,128)(2,1)S(1)} %get-tuple-element.37), channel_id=1, source_target_pairs={{0,4},{4,0},{8,12},{12,8},{1,5},{5,1},{9,13},{13,9},{2,6},{6,2},{1... | collective-permute-start | bytes 24584 | tf_op jit(solution)/shard_map/ppermute | solution.py:258

commit v9 on v8

--- a/solution.py
+++ b/solution.py
@@ -110,59 +110,62 @@
     lax.fori_loop(0, CAP, step, 0)
 
 
-def base_kernel(tensors, early, down_hbm, up_hbm, x_ref, w_ref, *refs):
-    block_refs, refs = refs[:early], refs[early:]
-    keep_ref, send_ref, chosen_ref, up_ref, slot_ref, down_sems, up_sems = refs
-    layers, _, depth = x_ref.shape
-    width = keep_ref.shape[3]
-    read_slots(block_refs, depth // HALVES, slot_ref)
-
+def multiply_layer(layer, x_ref, w_ref, keep_ref, send_ref):
+    half = keep_ref.shape[0]
+    width = keep_ref.shape[-1]
+    me = lax.axis_index("tensor")
+    for i, mask in enumerate(chunk_order(2 * half)):
+        out_ref = keep_ref if i < half else send_ref
+        columns = pl.ds(pl.multiple_of((me ^ mask) * width, width), width)
+        out_ref[i % half, layer] = jnp.dot(
+            x_ref[layer], w_ref[layer, :, columns], preferred_element_type=F32
+        )
+
+
+def both_copies(down_hbm, up_hbm, slot_ref, chosen_ref, up_ref, down_sems, up_sems):
     def copy_down(i, c):
         return fetch(down_hbm, slot_ref[i * CAP + c], chosen_ref.at[i], down_sems.at[i, c], c)
 
     def copy_up(i, c):
         return fetch(up_hbm, slot_ref[i * CAP + c], up_ref.at[i], up_sems.at[i, c], c)
 
-    for copy in (copy_down, copy_up):
-        for i in range(early):
-            each_slot(lambda c, i=i, copy=copy: copy(i, c).start())
-    me = lax.axis_index("tensor")
-    for i, mask in enumerate(chunk_order(tensors)):
-        out_ref = keep_ref if i < tensors // 2 else send_ref
-        columns = pl.ds(pl.multiple_of((me ^ mask) * width, width), width)
-        for layer in range(layers):
-            out_ref[i % (tensors // 2), layer] = jnp.dot(
-                x_ref[layer], w_ref[layer, :, columns], preferred_element_type=F32
-            )
-    for copy in (copy_down, copy_up):
-        for i in range(early):
-            each_slot(lambda c, i=i, copy=copy: copy(i, c).wait())
-
-
-def down_kernel(early, down_hbm, up_hbm, early_ref, *refs):
-    stores = len(refs) - 7
+    return copy_down, copy_up
+
+
+def early_kernel(down_hbm, up_hbm, x_ref, w_ref, block_ref, *refs):
+    keep_ref, send_ref, chosen_ref, up_ref, slot_ref, down_sems, up_sems = refs
+    read_slots([block_ref], x_ref.shape[2] // HALVES, slot_ref)
+    copies = both_copies(down_hbm, up_hbm, slot_ref, chosen_ref, up_ref, down_sems, up_sems)
+    for copy in copies:
+        each_slot(lambda c, copy=copy: copy(0, c).start())
+    multiply_layer(0, x_ref, w_ref, keep_ref, send_ref)
+    for copy in copies:
+        each_slot(lambda c, copy=copy: copy(0, c).wait())
+
+
+def late_kernel(down_hbm, up_hbm, x_ref, w_ref, keep0_ref, send0_ref, early_ref, *refs):
+    stores = len(refs) - 9
     block_refs, refs = refs[:stores], refs[stores:]
-    low_ref, up_ref, late_ref, slot_ref, down_sems, up_sems, kept_ref = refs
+    keep_ref, send_ref, low_ref, up_ref, late_ref, slot_ref, down_sems, up_sems, kept_ref = refs
     layers, _, rank, depth = down_hbm.shape
     half = depth // HALVES
     block = layers * HALVES * CAP
-    late = stores - early
-    read_slots(block_refs[early:], half, slot_ref)
-
-    def copy_down(i, c):
-        return fetch(down_hbm, slot_ref[i * CAP + c], late_ref.at[i], down_sems.at[i, c], c)
-
-    def copy_up(i, c):
-        return fetch(up_hbm, slot_ref[i * CAP + c], up_ref.at[i], up_sems.at[i, c], c)
-
+    read_slots(block_refs[1:], half, slot_ref)
+    copy_down, copy_up = both_copies(
+        down_hbm, up_hbm, slot_ref, late_ref, up_ref, down_sems, up_sems
+    )
     for copy in (copy_down, copy_up):
-        for i in range(late):
+        for i in range(stores - 1):
             each_slot(lambda c, i=i, copy=copy: copy(i, c).start())
+    keep_ref[:, 0] = keep0_ref[:, 0]
+    send_ref[:, 0] = send0_ref[:, 0]
+    for layer in range(1, layers):
+        multiply_layer(layer, x_ref, w_ref, keep_ref, send_ref)
     row, column = iota((CAP * rank, block), 0), iota((CAP * rank, block), 1)
     for i in range(stores):
-        chosen_ref = early_ref.at[i] if i < early else late_ref.at[i - early]
-        if i >= early:
-            each_slot(lambda c, i=i: copy_down(i - early, c).wait())
+        chosen_ref = early_ref.at[0] if i == 0 else late_ref.at[i - 1]
+        if i > 0:
+            each_slot(lambda c, i=i: copy_down(i - 1, c).wait())
         total = jnp.zeros((rank, block), F32)
         for layer in range(layers):
             for part in range(HALVES):
@@ -184,7 +187,7 @@
             low_ref[(i * layers + layer) * CAP : (i * layers + layer + 1) * CAP] = (
                 turned[at : at + CAP] + turned[at + CAP : at + 2 * CAP]
             )
-    for i in range(late):
+    for i in range(stores - 1):
         each_slot(lambda c, i=i: copy_up(i, c).wait())
 
 
@@ -279,35 +282,38 @@
     )(*(pltpu.with_memory_space_constraint(v, pltpu.HBM) for v in (owner_row, slot_row, x)))
     blocks = [swap(payloads[k], "store", stores, k) for k in order]
 
-    early = min(2, stores)
+    def sums(some_layers):
+        return [jax.ShapeDtypeStruct((tensors // 2, some_layers, rows, width), F32)] * 2
+
     keep, send, chosen, early_up = pl.pallas_call(
-        functools.partial(base_kernel, tensors, early),
-        out_shape=[jax.ShapeDtypeStruct((tensors // 2, layers, rows, width), F32)] * 2
+        early_kernel,
+        out_shape=sums(1)
         + [
-            jax.ShapeDtypeStruct((early, layers, CAP * rank, depth), BF16),
-            jax.ShapeDtypeStruct((early, layers, CAP * rank, width), BF16),
-        ],
-        in_specs=[HBM] * 2 + [VMEM] * (2 + early),
+            jax.ShapeDtypeStruct((1, layers, CAP * rank, depth), BF16),
+            jax.ShapeDtypeStruct((1, layers, CAP * rank, width), BF16),
+        ],
+        in_specs=[HBM] * 2 + [VMEM] * 3,
         out_specs=[VMEM] * 4,
         scratch_shapes=[
-            pltpu.SMEM((early * CAP,), jnp.int32),
-            pltpu.SemaphoreType.DMA((early, CAP)),
-            pltpu.SemaphoreType.DMA((early, CAP)),
-        ],
-        compiler_params=params(),
-        cost_estimate=cost(6),
-        name="base",
-    )(down, up, x, w, *blocks[:early])
-
-    late = stores - early
-    low, late_up = pl.pallas_call(
-        functools.partial(down_kernel, early),
-        out_shape=[
+            pltpu.SMEM((CAP,), jnp.int32),
+            pltpu.SemaphoreType.DMA((1, CAP)),
+            pltpu.SemaphoreType.DMA((1, CAP)),
+        ],
+        compiler_params=params(),
+        cost_estimate=cost(3),
+        name="early",
+    )(down, up, x, w, blocks[0])
+
+    late = stores - 1
+    keep, send, low, late_up = pl.pallas_call(
+        late_kernel,
+        out_shape=sums(layers)
+        + [
             jax.ShapeDtypeStruct((stores * layers * CAP, rank), F32),
             jax.ShapeDtypeStruct((late, layers, CAP * rank, width), BF16),
         ],
-        in_specs=[HBM] * 2 + [VMEM] * (1 + stores),
-        out_specs=[VMEM] * 2,
+        in_specs=[HBM] * 2 + [VMEM] * (5 + stores),
+        out_specs=[VMEM] * 4,
         scratch_shapes=[
             pltpu.VMEM((late, layers, CAP * rank, depth), BF16),
             pltpu.SMEM((late * CAP,), jnp.int32),
@@ -316,9 +322,9 @@
             pltpu.VMEM((rank, stores * block), F32),
         ],
         compiler_params=params(LARGE),
-        cost_estimate=cost(4),
-        name="down",
-    )(down, up, chosen, *blocks)
+        cost_estimate=cost(6),
+        name="late",
+    )(down, up, x, w, keep, send, chosen, *blocks)
     lows = [low] + [swap(low, "tensor", tensors, j) for j in range(tensors - 1, 0, -1)]
     got = swap(send, "tensor", tensors, 1)
     bit = 2

time: 29 us -> 29.3 us (1.010)
  starting transfers between devices: 13.9 us -> 13 us
  waiting for transfers between devices: 5.82 us -> 6.59 us
  Pallas kernels: 8.45 us -> 8.9 us
    ppermute x11, starting transfers between devices: 13.9 us -> 13 us  [swap(): return lax.ppermute(value, axis, [(i, i ^ by) for i in range(size)])]
    ppermute x11, waiting for transfers between devices: 5.82 us -> 6.59 us  [swap(): return lax.ppermute(value, axis, [(i, i ^ by) for i in range(size)])]
    pallas_call x2, Pallas kernels: 6.03 us -> 6.48 us  [the longest x1 4.7 us: local(): pl.pallas_call(late_kernel, out_shape=sums(layers) + [jax.ShapeDtypeStruc...]
  transfers between devices with their start and end apart: 11 -> 11, of which waited for: 4 -> 4; matrix products, arithmetic and copies ran while one was open for 0% -> 0% of each run, Pallas kernels for 22% -> 7%
where the time goes in v9:
time: 29.3 us; the launch traced here: 29.2 us
  starting transfers between devices  13 us (44%)
  Pallas kernels  8.9 us (30%)
  waiting for transfers between devices  6.59 us (22%)
  between operations  0.71 us (2%)
    ppermute x11, starting transfers between devices, swap(): return lax.ppermute(value, axis, [(i, i ^ by) for i in range(size)])  13 us
    ppermute x11, waiting for transfers between devices, swap(): return lax.ppermute(value, axis, [(i, i ^ by) for i in range(size)])  6.59 us
    pallas_call x1, Pallas kernels, local(): pl.pallas_call(late_kernel, out_shape=sums(layers) + [jax.ShapeDtypeStruc...  4.7 us
    pallas_call x1, Pallas kernels, local(): pl.pallas_call(early_kernel, out_shape=sums(1) + [jax.ShapeDtypeStruct((1...  1.78 us
    pallas_call x1, Pallas kernels, local(): pl.pallas_call(functools.partial(prepare_kernel, back), out_shape=[jax.Sh...  1.28 us
    pallas_call x1, Pallas kernels, local(): pl.pallas_call(final_kernel, out_shape=jax.ShapeDtypeStruct((layers, rows...  0.75 us
  transfers between devices with their start and end apart: 11, of which 4 were waited for; matrix products, arithmetic and copies ran while one was open for 0% of the time, Pallas kernels for 7%

profile of v9, /device:TPU:0, one launch (start us, length us, event | category | flops | bytes accessed | tf_op | source)
XLA Modules:
  0.0 29.2 jit_solution(7149849826514337661)
XLA Ops:
  0.0 1.3 %prepare.1 = (bf16[16,1152]{1,0:T(8,128)(2,1)S(1)}, bf16[16,1152]{1,0:T(8,128)(2,1)S(1)}, bf16[16,1152]{1,0:T(8,128)(2,1)S(1)}, bf16[16,1152]{1,0:T(8,128)(2,1)S(1)}, bf16[32,32]{1,0:T(8,128)(2,1)S(1)}) custom-call(s32[1,16]{1,0:T(1,128)} %bitcast.5, s32[1,16]{1,0:T(1,128)} %bitcast.6, bf16[2,16,2048]{2,1,0:T(8,128)(2,1)} %x_ref.3), custom_call_target="tpu_custom_call" | custom-call | flops 6920999936 | tf_op jit(solution)/shard_map/prepare/pallas_call | solution.py:265
  1.3 4.1 %collective-permute-start = (bf16[16,1152]{1,0:T(8,128)(2,1)S(1)}, bf16[16,1152]{1,0:T(8,128)(2,1)S(1)}, u32[]{:S(2)}, u32[]{:S(2)}) collective-permute-start(bf16[16,1152]{1,0:T(8,128)(2,1)S(1)} %get-tuple-element.29), channel_id=1, source_target_pairs={{0,8},{4,12},{8,0},{12,4},{1,9},{5,13},{9,1},{13,5},{2,10},{6,14},... | collective-permute-start | bytes 110600 | tf_op jit(solution)/shard_map/ppermute | solution.py:261
  5.4 1.4 %collective-permute-start.1 = (bf16[16,1152]{1,0:T(8,128)(2,1)S(1)}, bf16[16,1152]{1,0:T(8,128)(2,1)S(1)}, u32[]{:S(2)}, u32[]{:S(2)}) collective-permute-start(bf16[16,1152]{1,0:T(8,128)(2,1)S(1)} %get-tuple-element.30), channel_id=1, source_target_pairs={{0,12},{4,8},{8,4},{12,0},{1,13},{5,9},{9,5},{13,1},{2,14},{6,10},... | collective-permute-start | bytes 110600 | tf_op jit(solution)/shard_map/ppermute | solution.py:261
  6.7 0.2 collective-permute-start.2
  7.0 1.8 %early.1 = (f32[2,1,16,512]{3,2,1,0:T(8,128)S(1)}, f32[2,1,16,512]{3,2,1,0:T(8,128)S(1)}, bf16[1,2,256,2048]{3,2,1,0:T(8,128)(2,1)S(1)}, bf16[1,2,256,512]{3,2,1,0:T(8,128)(2,1)S(1)}) custom-call(bf16[2,32,64,2048]{3,2,1,0:T(8,128)(2,1)} %bitcast.3, bf16[2,32,64,512]{3,2,1,0:T(8,128)(2,1)} %up_hbm.3, bf16[2,16,2048]{2,1,0:T(8,128)(2,1)S(1)} %copy-done.1, ...), custom_call_target="tpu_custom_call" | custom-call | flops 3460499968 | tf_op jit(solution)/shard_map/early/pallas_call | solution.py:288
  8.8 0.0 collective-permute-done.refs_1_
  8.8 2.4 %collective-permute-done.1.refs_2_ = bf16[16,1152]{1,0:T(8,128)(2,1)S(1)} collective-permute-done((bf16[16,1152]{1,0:T(8,128)(2,1)S(1)}, bf16[16,1152]{1,0:T(8,128)(2,1)S(1)}, u32[]{:S(2)}, u32[]{:S(2)}) %collective-permute-start.1) | collective-permute-done | bytes 36896 | tf_op jit(solution)/shard_map/ppermute | solution.py:261
  11.1 0.0 collective-permute-done.2.refs_3_
  11.1 4.7 %late.1 = (f32[2,2,16,512]{3,2,1,0:T(8,128)S(1)}, f32[2,2,16,512]{3,2,1,0:T(8,128)S(1)}, f32[32,64]{1,0:T(8,128)S(1)}, bf16[3,2,256,512]{3,2,1,0:T(8,128)(2,1)S(1)}) custom-call(bf16[2,32,64,2048]{3,2,1,0:T(8,128)(2,1)} %bitcast.4, bf16[2,32,64,512]{3,2,1,0:T(8,128)(2,1)} %up_hbm.3, bf16[2,16,2048]{2,1,0:T(8,128)(2,1)S(1)} %copy-done.1, ...), custom_call_target="tpu_custom_call" | custom-call | flops 6920999936 | tf_op jit(solution)/shard_map/late/pallas_call | solution.py:308
  15.9 0.1 collective-permute-start.3
  15.9 1.6 %collective-permute-start.5 = (f32[32,64]{1,0:T(8,128)S(1)}, f32[32,64]{1,0:T(8,128)S(1)}, u32[]{:S(2)}, u32[]{:S(2)}) collective-permute-start(f32[32,64]{1,0:T(8,128)S(1)} %get-tuple-element.32._.refs_0_), channel_id=1, source_target_pairs={{0,3},{1,2},{2,1},{3,0},{4,7},{5,6},{6,5},{7,4},{8,11},{9,10},{10,... | collective-permute-start | bytes 24584 | tf_op jit(solution)/shard_map/ppermute | solution.py:261
  17.5 0.5 %collective-permute-start.6 = (f32[32,64]{1,0:T(8,128)S(1)}, f32[32,64]{1,0:T(8,128)S(1)}, u32[]{:S(2)}, u32[]{:S(2)}) collective-permute-start(f32[32,64]{1,0:T(8,128)S(1)} %get-tuple-element.32._.refs_0_), channel_id=1, source_target_pairs={{0,2},{1,3},{2,0},{3,1},{4,6},{5,7},{6,4},{7,5},{8,10},{9,11},{10,... | collective-permute-start | bytes 24584 | tf_op jit(solution)/shard_map/ppermute | solution.py:261
  18.1 0.0 collective-permute-start.7
  18.1 0.0 collective-permute-done.3.got_ref
  18.1 1.5 %collective-permute-start.4 = (f32[2,16,512]{2,1,0:T(8,128)S(1)}, f32[2,16,512]{2,1,0:T(8,128)S(1)}, u32[]{:S(2)}, u32[]{:S(2)}) collective-permute-start(f32[2,16,512]{2,1,0:T(8,128)S(1)} %get-tuple-element.36), channel_id=1, source_target_pairs={{0,2},{1,3},{2,0},{3,1},{4,6},{5,7},{6,4},{7,5},{8,10},{9,11},{10,... | collective-permute-start | bytes 196616 | tf_op jit(solution)/shard_map/ppermute | solution.py:261
  19.7 1.6 %collective-permute-done.6.refs_2_ = f32[32,64]{1,0:T(8,128)S(1)} collective-permute-done((f32[32,64]{1,0:T(8,128)S(1)}, f32[32,64]{1,0:T(8,128)S(1)}, u32[]{:S(2)}, u32[]{:S(2)}) %collective-permute-start.6) | collective-permute-done | bytes 8224 | tf_op jit(solution)/shard_map/ppermute | solution.py:261
  21.3 0.0 collective-permute-done.7.refs_3_
  21.3 0.4 %up.1 = (bf16[16,256]{1,0:T(8,128)(2,1)S(1)}, bf16[16,256]{1,0:T(8,128)(2,1)S(1)}, bf16[16,256]{1,0:T(8,128)(2,1)S(1)}, bf16[16,256]{1,0:T(8,128)(2,1)S(1)}) custom-call(f32[2,16,512]{2,1,0:T(8,128)S(1)} %get-tuple-element.35._.own_ref, bf16[1,2,256,512]{3,2,1,0:T(8,128)(2,1)S(1)} %get-tuple-element.37.early_ref, ...), custom_call_target="tpu_custom_call" | custom-call | flops 1153500032 | tf_op jit(solution)/shard_map/up/pallas_call | solution.py:347
  21.7 1.3 %collective-permute-start.10 = (bf16[16,256]{1,0:T(8,128)(2,1)S(1)}, bf16[16,256]{1,0:T(8,128)(2,1)S(1)}, u32[]{:S(2)}, u32[]{:S(2)}) collective-permute-start(bf16[16,256]{1,0:T(8,128)(2,1)S(1)} %get-tuple-element.42), channel_id=1, source_target_pairs={{0,8},{4,12},{8,0},{12,4},{1,9},{5,13},{9,1},{13,5},{2,10},{6,14},... | collective-permute-start | bytes 24584 | tf_op jit(solution)/shard_map/ppermute | solution.py:261
  23.0 1.0 %collective-permute-start.8 = (bf16[16,256]{1,0:T(8,128)(2,1)S(1)}, bf16[16,256]{1,0:T(8,128)(2,1)S(1)}, u32[]{:S(2)}, u32[]{:S(2)}) collective-permute-start(bf16[16,256]{1,0:T(8,128)(2,1)S(1)} %get-tuple-element.40), channel_id=1, source_target_pairs={{0,12},{4,8},{8,4},{12,0},{1,13},{5,9},{9,5},{13,1},{2,14},{6,10},... | collective-permute-start | bytes 24584 | tf_op jit(solution)/shard_map/ppermute | solution.py:261
  24.0 1.2 %collective-permute-start.9 = (bf16[16,256]{1,0:T(8,128)(2,1)S(1)}, bf16[16,256]{1,0:T(8,128)(2,1)S(1)}, u32[]{:S(2)}, u32[]{:S(2)}) collective-permute-start(bf16[16,256]{1,0:T(8,128)(2,1)S(1)} %get-tuple-element.41), channel_id=1, source_target_pairs={{0,4},{4,0},{8,12},{12,8},{1,5},{5,1},{9,13},{13,9},{2,6},{6,2},{1... | collective-permute-start | bytes 24584 | tf_op jit(solution)/shard_map/ppermute | solution.py:261
  25.9 0.4 %collective-permute-done.10.refs_3_ = bf16[16,256]{1,0:T(8,128)(2,1)S(1)} collective-permute-done((bf16[16,256]{1,0:T(8,128)(2,1)S(1)}, bf16[16,256]{1,0:T(8,128)(2,1)S(1)}, u32[]{:S(2)}, u32[]{:S(2)}) %collective-permute-start.10) | collective-permute-done | bytes 8224 | tf_op jit(solution)/shard_map/ppermute | solution.py:261
  26.3 2.2 %collective-permute-done.8.refs_1_ = bf16[16,256]{1,0:T(8,128)(2,1)S(1)} collective-permute-done((bf16[16,256]{1,0:T(8,128)(2,1)S(1)}, bf16[16,256]{1,0:T(8,128)(2,1)S(1)}, u32[]{:S(2)}, u32[]{:S(2)}) %collective-permute-start.8) | collective-permute-done | bytes 8224 | tf_op jit(solution)/shard_map/ppermute | solution.py:261
  28.4 0.7 %final.1 = bf16[2,16,512]{2,1,0:T(8,128)(2,1)} custom-call(s32[1]{0:T(128)S(6)} %copy.8.count_ref, bf16[32,32]{1,0:T(8,128)(2,1)S(1)} %get-tuple-element.24.pick_ref, f32[2,16,512]{2,1,0:T(8,128)S(1)} %get-tuple-element.35._.own_ref, f32[2,16,512]{2,1,0:T(8,128)S(1)} %collective-permute-done.4.got_ref, bf16[16,256]{1,0:T(8,128)(2,1)S(1)} %get-tuple-element.39.refs_0_, ...), custom_call_target="tpu_custom_call" | custom-call | flops 1153500032 | tf_op jit(solution)/shard_map/final/pallas_call | solution.py:358
  (8 shorter events, 0.0 us)
Async XLA Ops:
  0.0 7.0 %copy-start = (bf16[2,2048,2048]{2,1,0:T(8,128)(2,1)S(1)}, bf16[2,2048,2048]{2,1,0:T(8,128)(2,1)}, u32[]{:S(2)}) copy-start(bf16[2,2048,2048]{2,1,0:T(8,128)(2,1)} %w_ref.3) | copy-start | bytes 50331652
  0.0 7.0 %copy-start.1 = (bf16[2,16,2048]{2,1,0:T(8,128)(2,1)S(1)}, bf16[2,16,2048]{2,1,0:T(8,128)(2,1)}, u32[]{:S(2)}) copy-start(bf16[2,16,2048]{2,1,0:T(8,128)(2,1)} %x_ref.3) | copy-start | bytes 393220
  1.3 7.5 %collective-permute-start = (bf16[16,1152]{1,0:T(8,128)(2,1)S(1)}, bf16[16,1152]{1,0:T(8,128)(2,1)S(1)}, u32[]{:S(2)}, u32[]{:S(2)}) collective-permute-start(bf16[16,1152]{1,0:T(8,128)(2,1)S(1)} %get-tuple-element.29), channel_id=1, source_target_pairs={{0,8},{4,12},{8,0},{12,4},{1,9},{5,13},{9,1},{13,5},{2,10},{6,14},... | collective-permute-start | bytes 110600 | tf_op jit(solution)/shard_map/ppermute | solution.py:261
  5.4 5.8 %collective-permute-start.1 = (bf16[16,1152]{1,0:T(8,128)(2,1)S(1)}, bf16[16,1152]{1,0:T(8,128)(2,1)S(1)}, u32[]{:S(2)}, u32[]{:S(2)}) collective-permute-start(bf16[16,1152]{1,0:T(8,128)(2,1)S(1)} %get-tuple-element.30), channel_id=1, source_target_pairs={{0,12},{4,8},{8,4},{12,0},{1,13},{5,9},{9,5},{13,1},{2,14},{6,10},... | collective-permute-start | bytes 110600 | tf_op jit(solution)/shard_map/ppermute | solution.py:261
  6.7 4.4 %collective-permute-start.2 = (bf16[16,1152]{1,0:T(8,128)(2,1)S(1)}, bf16[16,1152]{1,0:T(8,128)(2,1)S(1)}, u32[]{:S(2)}, u32[]{:S(2)}) collective-permute-start(bf16[16,1152]{1,0:T(8,128)(2,1)S(1)} %get-tuple-element.31), channel_id=1, source_target_pairs={{0,4},{4,0},{8,12},{12,8},{1,5},{5,1},{9,13},{13,9},{2,6},{6,2},{1... | collective-permute-start | bytes 110600 | tf_op jit(solution)/shard_map/ppermute | solution.py:261
  15.9 2.2 %collective-permute-start.3 = (f32[2,2,16,512]{3,2,1,0:T(8,128)S(1)}, f32[2,2,16,512]{3,2,1,0:T(8,128)S(1)}, u32[]{:S(2)}, u32[]{:S(2)}) collective-permute-start(f32[2,2,16,512]{3,2,1,0:T(8,128)S(1)} %get-tuple-element.34), channel_id=1, source_target_pairs={{0,1},{1,0},{2,3},{3,2},{4,5},{5,4},{6,7},{7,6},{8,9},{9,8},{10,11... | collective-permute-start | bytes 393224 | tf_op jit(solution)/shard_map/ppermute | solution.py:261
  15.9 3.7 %collective-permute-start.5 = (f32[32,64]{1,0:T(8,128)S(1)}, f32[32,64]{1,0:T(8,128)S(1)}, u32[]{:S(2)}, u32[]{:S(2)}) collective-permute-start(f32[32,64]{1,0:T(8,128)S(1)} %get-tuple-element.32._.refs_0_), channel_id=1, source_target_pairs={{0,3},{1,2},{2,1},{3,0},{4,7},{5,6},{6,5},{7,4},{8,11},{9,10},{10,... | collective-permute-start | bytes 24584 | tf_op jit(solution)/shard_map/ppermute | solution.py:261
  17.5 3.7 %collective-permute-start.6 = (f32[32,64]{1,0:T(8,128)S(1)}, f32[32,64]{1,0:T(8,128)S(1)}, u32[]{:S(2)}, u32[]{:S(2)}) collective-permute-start(f32[32,64]{1,0:T(8,128)S(1)} %get-tuple-element.32._.refs_0_), channel_id=1, source_target_pairs={{0,2},{1,3},{2,0},{3,1},{4,6},{5,7},{6,4},{7,5},{8,10},{9,11},{10,... | collective-permute-start | bytes 24584 | tf_op jit(solution)/shard_map/ppermute | solution.py:261
  18.1 3.2 %collective-permute-start.7 = (f32[32,64]{1,0:T(8,128)S(1)}, f32[32,64]{1,0:T(8,128)S(1)}, u32[]{:S(2)}, u32[]{:S(2)}) collective-permute-start(f32[32,64]{1,0:T(8,128)S(1)} %get-tuple-element.32._.refs_0_), channel_id=1, source_target_pairs={{0,1},{1,0},{2,3},{3,2},{4,5},{5,4},{6,7},{7,6},{8,9},{9,8},{10,11... | collective-permute-start | bytes 24584 | tf_op jit(solution)/shard_map/ppermute | solution.py:261
  18.1 10.3 %collective-permute-start.4 = (f32[2,16,512]{2,1,0:T(8,128)S(1)}, f32[2,16,512]{2,1,0:T(8,128)S(1)}, u32[]{:S(2)}, u32[]{:S(2)}) collective-permute-start(f32[2,16,512]{2,1,0:T(8,128)S(1)} %get-tuple-element.36), channel_id=1, source_target_pairs={{0,2},{1,3},{2,0},{3,1},{4,6},{5,7},{6,4},{7,5},{8,10},{9,11},{10,... | collective-permute-start | bytes 196616 | tf_op jit(solution)/shard_map/ppermute | solution.py:261
  21.7 4.6 %collective-permute-start.10 = (bf16[16,256]{1,0:T(8,128)(2,1)S(1)}, bf16[16,256]{1,0:T(8,128)(2,1)S(1)}, u32[]{:S(2)}, u32[]{:S(2)}) collective-permute-start(bf16[16,256]{1,0:T(8,128)(2,1)S(1)} %get-tuple-element.42), channel_id=1, source_target_pairs={{0,8},{4,12},{8,0},{12,4},{1,9},{5,13},{9,1},{13,5},{2,10},{6,14},... | collective-permute-start | bytes 24584 | tf_op jit(solution)/shard_map/ppermute | solution.py:261
  23.0 5.4 %collective-permute-start.8 = (bf16[16,256]{1,0:T(8,128)(2,1)S(1)}, bf16[16,256]{1,0:T(8,128)(2,1)S(1)}, u32[]{:S(2)}, u32[]{:S(2)}) collective-permute-start(bf16[16,256]{1,0:T(8,128)(2,1)S(1)} %get-tuple-element.40), channel_id=1, source_target_pairs={{0,12},{4,8},{8,4},{12,0},{1,13},{5,9},{9,5},{13,1},{2,14},{6,10},... | collective-permute-start | bytes 24584 | tf_op jit(solution)/shard_map/ppermute | solution.py:261
  24.0 4.4 %collective-permute-start.9 = (bf16[16,256]{1,0:T(8,128)(2,1)S(1)}, bf16[16,256]{1,0:T(8,128)(2,1)S(1)}, u32[]{:S(2)}, u32[]{:S(2)}) collective-permute-start(bf16[16,256]{1,0:T(8,128)(2,1)S(1)} %get-tuple-element.41), channel_id=1, source_target_pairs={{0,4},{4,0},{8,12},{12,8},{1,5},{5,1},{9,13},{13,9},{2,6},{6,2},{1... | collective-permute-start | bytes 24584 | tf_op jit(solution)/shard_map/ppermute | solution.py:261

commit v10 on v8

--- a/solution.py
+++ b/solution.py
@@ -279,7 +279,7 @@
     )(*(pltpu.with_memory_space_constraint(v, pltpu.HBM) for v in (owner_row, slot_row, x)))
     blocks = [swap(payloads[k], "store", stores, k) for k in order]
 
-    early = min(2, stores)
+    early = 1
     keep, send, chosen, early_up = pl.pallas_call(
         functools.partial(base_kernel, tensors, early),
         out_shape=[jax.ShapeDtypeStruct((tensors // 2, layers, rows, width), F32)] * 2

time: 29 us -> 28.9 us (level)
  Pallas kernels: 8.45 us -> 9.12 us
  starting transfers between devices: 13.9 us -> 13.5 us
  waiting for transfers between devices: 5.82 us -> 5.43 us
    pallas_call x1, Pallas kernels: 3.35 us -> 4.21 us  [local(): pl.pallas_call(functools.partial(down_kernel, early), out_shape=[jax.Shap...]
    ppermute x11, starting transfers between devices: 13.9 us -> 13.5 us  [swap(): return lax.ppermute(value, axis, [(i, i ^ by) for i in range(size)])]
    ppermute x11, waiting for transfers between devices: 5.82 us -> 5.43 us  [swap(): return lax.ppermute(value, axis, [(i, i ^ by) for i in range(size)])]
  transfers between devices with their start and end apart: 11 -> 11, of which waited for: 4 -> 3; matrix products, arithmetic and copies ran while one was open for 0% -> 0% of each run, Pallas kernels for 22% -> 25%
where the time goes in v10:
time: 28.9 us; the launch traced here: 28.8 us
  starting transfers between devices  13.5 us (47%)
  Pallas kernels  9.12 us (32%)
  waiting for transfers between devices  5.43 us (19%)
  between operations  0.72 us (2%)
    ppermute x11, starting transfers between devices, swap(): return lax.ppermute(value, axis, [(i, i ^ by) for i in range(size)])  13.5 us
    ppermute x11, waiting for transfers between devices, swap(): return lax.ppermute(value, axis, [(i, i ^ by) for i in range(size)])  5.43 us
    pallas_call x1, Pallas kernels, local(): pl.pallas_call(functools.partial(down_kernel, early), out_shape=[jax.Shap...  4.21 us
    pallas_call x1, Pallas kernels, local(): pl.pallas_call(functools.partial(base_kernel, tensors, early), out_shape=...  2.49 us
    pallas_call x1, Pallas kernels, local(): pl.pallas_call(functools.partial(prepare_kernel, back), out_shape=[jax.Sh...  1.28 us
    pallas_call x1, Pallas kernels, local(): pl.pallas_call(final_kernel, out_shape=jax.ShapeDtypeStruct((layers, rows...  0.75 us
  transfers between devices with their start and end apart: 11, of which 3 were waited for; matrix products, arithmetic and copies ran while one was open for 0% of the time, Pallas kernels for 25%

profile of v10, /device:TPU:0, one launch (start us, length us, event | category | flops | bytes accessed | tf_op | source)
XLA Modules:
  0.0 28.8 jit_solution(1211396427215065351)
XLA Ops:
  0.0 1.3 %prepare.1 = (bf16[16,1152]{1,0:T(8,128)(2,1)S(1)}, bf16[16,1152]{1,0:T(8,128)(2,1)S(1)}, bf16[16,1152]{1,0:T(8,128)(2,1)S(1)}, bf16[16,1152]{1,0:T(8,128)(2,1)S(1)}, bf16[32,32]{1,0:T(8,128)(2,1)S(1)}) custom-call(s32[1,16]{1,0:T(1,128)} %bitcast.5, s32[1,16]{1,0:T(1,128)} %bitcast.6, bf16[2,16,2048]{2,1,0:T(8,128)(2,1)} %x_ref.1), custom_call_target="tpu_custom_call" | custom-call | flops 6920999936 | tf_op jit(solution)/shard_map/prepare/pallas_call | solution.py:262
  1.3 4.1 %collective-permute-start = (bf16[16,1152]{1,0:T(8,128)(2,1)S(1)}, bf16[16,1152]{1,0:T(8,128)(2,1)S(1)}, u32[]{:S(2)}, u32[]{:S(2)}) collective-permute-start(bf16[16,1152]{1,0:T(8,128)(2,1)S(1)} %get-tuple-element.25), channel_id=1, source_target_pairs={{0,8},{4,12},{8,0},{12,4},{1,9},{5,13},{9,1},{13,5},{2,10},{6,14},... | collective-permute-start | bytes 110600 | tf_op jit(solution)/shard_map/ppermute | solution.py:258
  5.4 1.4 %collective-permute-start.1 = (bf16[16,1152]{1,0:T(8,128)(2,1)S(1)}, bf16[16,1152]{1,0:T(8,128)(2,1)S(1)}, u32[]{:S(2)}, u32[]{:S(2)}) collective-permute-start(bf16[16,1152]{1,0:T(8,128)(2,1)S(1)} %get-tuple-element.26), channel_id=1, source_target_pairs={{0,12},{4,8},{8,4},{12,0},{1,13},{5,9},{9,5},{13,1},{2,14},{6,10},... | collective-permute-start | bytes 110600 | tf_op jit(solution)/shard_map/ppermute | solution.py:258
  6.7 0.2 collective-permute-start.2
  7.0 2.5 %base.1 = (f32[2,2,16,512]{3,2,1,0:T(8,128)S(1)}, f32[2,2,16,512]{3,2,1,0:T(8,128)S(1)}, bf16[1,2,256,2048]{3,2,1,0:T(8,128)(2,1)S(1)}, bf16[1,2,256,512]{3,2,1,0:T(8,128)(2,1)S(1)}) custom-call(bf16[2,32,64,2048]{3,2,1,0:T(8,128)(2,1)} %bitcast.3, bf16[2,32,64,512]{3,2,1,0:T(8,128)(2,1)} %up_hbm.3, bf16[2,16,2048]{2,1,0:T(8,128)(2,1)S(1)} %copy-done.1, ...), custom_call_target="tpu_custom_call" | custom-call | flops 6920999936 | tf_op jit(solution)/shard_map/base/pallas_call | solution.py:283
  9.5 0.1 collective-permute-start.3
  9.5 0.0 collective-permute-done.refs_1_
  9.6 1.6 %collective-permute-done.1.refs_2_ = bf16[16,1152]{1,0:T(8,128)(2,1)S(1)} collective-permute-done((bf16[16,1152]{1,0:T(8,128)(2,1)S(1)}, bf16[16,1152]{1,0:T(8,128)(2,1)S(1)}, u32[]{:S(2)}, u32[]{:S(2)}) %collective-permute-start.1) | collective-permute-done | bytes 36896 | tf_op jit(solution)/shard_map/ppermute | solution.py:258
  11.1 0.0 collective-permute-done.2.refs_3_
  11.1 4.2 %down.1 = (f32[32,64]{1,0:T(8,128)S(1)}, bf16[3,2,256,512]{3,2,1,0:T(8,128)(2,1)S(1)}) custom-call(bf16[2,32,64,2048]{3,2,1,0:T(8,128)(2,1)} %bitcast.4, bf16[2,32,64,512]{3,2,1,0:T(8,128)(2,1)} %up_hbm.3, bf16[1,2,256,2048]{3,2,1,0:T(8,128)(2,1)S(1)} %get-tuple-element.24.early_ref, bf16[16,1152]{1,0:T(8,128)(2,1)S(1)} %get-tuple-element.23.refs_0_, ...), custom_call_target="tpu_custom_call" | custom-call | flops 4614000128 | tf_op jit(solution)/shard_map/down/pallas_call | solution.py:303
  15.4 0.4 %collective-permute-start.5 = (f32[32,64]{1,0:T(8,128)S(1)}, f32[32,64]{1,0:T(8,128)S(1)}, u32[]{:S(2)}, u32[]{:S(2)}) collective-permute-start(f32[32,64]{1,0:T(8,128)S(1)} %get-tuple-element.28._.refs_0_), channel_id=1, source_target_pairs={{0,3},{1,2},{2,1},{3,0},{4,7},{5,6},{6,5},{7,4},{8,11},{9,10},{10,... | collective-permute-start | bytes 24584 | tf_op jit(solution)/shard_map/ppermute | solution.py:258
  15.8 1.2 %collective-permute-start.6 = (f32[32,64]{1,0:T(8,128)S(1)}, f32[32,64]{1,0:T(8,128)S(1)}, u32[]{:S(2)}, u32[]{:S(2)}) collective-permute-start(f32[32,64]{1,0:T(8,128)S(1)} %get-tuple-element.28._.refs_0_), channel_id=1, source_target_pairs={{0,2},{1,3},{2,0},{3,1},{4,6},{5,7},{6,4},{7,5},{8,10},{9,11},{10,... | collective-permute-start | bytes 24584 | tf_op jit(solution)/shard_map/ppermute | solution.py:258
  17.0 0.3 %collective-permute-start.7 = (f32[32,64]{1,0:T(8,128)S(1)}, f32[32,64]{1,0:T(8,128)S(1)}, u32[]{:S(2)}, u32[]{:S(2)}) collective-permute-start(f32[32,64]{1,0:T(8,128)S(1)} %get-tuple-element.28._.refs_0_), channel_id=1, source_target_pairs={{0,1},{1,0},{2,3},{3,2},{4,5},{5,4},{6,7},{7,6},{8,9},{9,8},{10,11... | collective-permute-start | bytes 24584 | tf_op jit(solution)/shard_map/ppermute | solution.py:258
  17.3 0.0 collective-permute-done.3.got_ref
  17.3 1.6 %collective-permute-start.4 = (f32[2,16,512]{2,1,0:T(8,128)S(1)}, f32[2,16,512]{2,1,0:T(8,128)S(1)}, u32[]{:S(2)}, u32[]{:S(2)}) collective-permute-start(f32[2,16,512]{2,1,0:T(8,128)S(1)} %get-tuple-element.32), channel_id=1, source_target_pairs={{0,2},{1,3},{2,0},{3,1},{4,6},{5,7},{6,4},{7,5},{8,10},{9,11},{10,... | collective-permute-start | bytes 196616 | tf_op jit(solution)/shard_map/ppermute | solution.py:258
  18.9 0.6 %collective-permute-done.6.refs_2_ = f32[32,64]{1,0:T(8,128)S(1)} collective-permute-done((f32[32,64]{1,0:T(8,128)S(1)}, f32[32,64]{1,0:T(8,128)S(1)}, u32[]{:S(2)}, u32[]{:S(2)}) %collective-permute-start.6) | collective-permute-done | bytes 8224 | tf_op jit(solution)/shard_map/ppermute | solution.py:258
  19.5 0.0 collective-permute-done.7.refs_3_
  19.5 0.4 %up.1 = (bf16[16,256]{1,0:T(8,128)(2,1)S(1)}, bf16[16,256]{1,0:T(8,128)(2,1)S(1)}, bf16[16,256]{1,0:T(8,128)(2,1)S(1)}, bf16[16,256]{1,0:T(8,128)(2,1)S(1)}) custom-call(f32[2,16,512]{2,1,0:T(8,128)S(1)} %get-tuple-element.31._.own_ref, bf16[1,2,256,512]{3,2,1,0:T(8,128)(2,1)S(1)} %get-tuple-element.33.early_ref, ...), custom_call_target="tpu_custom_call" | custom-call | flops 1153500032 | tf_op jit(solution)/shard_map/up/pallas_call | solution.py:341
  19.9 2.7 %collective-permute-start.10 = (bf16[16,256]{1,0:T(8,128)(2,1)S(1)}, bf16[16,256]{1,0:T(8,128)(2,1)S(1)}, u32[]{:S(2)}, u32[]{:S(2)}) collective-permute-start(bf16[16,256]{1,0:T(8,128)(2,1)S(1)} %get-tuple-element.38), channel_id=1, source_target_pairs={{0,8},{4,12},{8,0},{12,4},{1,9},{5,13},{9,1},{13,5},{2,10},{6,14},... | collective-permute-start | bytes 24584 | tf_op jit(solution)/shard_map/ppermute | solution.py:258
  22.6 1.3 %collective-permute-start.8 = (bf16[16,256]{1,0:T(8,128)(2,1)S(1)}, bf16[16,256]{1,0:T(8,128)(2,1)S(1)}, u32[]{:S(2)}, u32[]{:S(2)}) collective-permute-start(bf16[16,256]{1,0:T(8,128)(2,1)S(1)} %get-tuple-element.36), channel_id=1, source_target_pairs={{0,12},{4,8},{8,4},{12,0},{1,13},{5,9},{9,5},{13,1},{2,14},{6,10},... | collective-permute-start | bytes 24584 | tf_op jit(solution)/shard_map/ppermute | solution.py:258
  23.9 0.3 collective-permute-start.9
  24.8 0.0 collective-permute-done.10.refs_3_
  24.8 3.2 %collective-permute-done.8.refs_1_ = bf16[16,256]{1,0:T(8,128)(2,1)S(1)} collective-permute-done((bf16[16,256]{1,0:T(8,128)(2,1)S(1)}, bf16[16,256]{1,0:T(8,128)(2,1)S(1)}, u32[]{:S(2)}, u32[]{:S(2)}) %collective-permute-start.8) | collective-permute-done | bytes 8224 | tf_op jit(solution)/shard_map/ppermute | solution.py:258
  28.0 0.7 %final.1 = bf16[2,16,512]{2,1,0:T(8,128)(2,1)} custom-call(s32[1]{0:T(128)S(6)} %copy.8.count_ref, bf16[32,32]{1,0:T(8,128)(2,1)S(1)} %get-tuple-element.22.pick_ref, f32[2,16,512]{2,1,0:T(8,128)S(1)} %get-tuple-element.31._.own_ref, f32[2,16,512]{2,1,0:T(8,128)S(1)} %collective-permute-done.4.got_ref, bf16[16,256]{1,0:T(8,128)(2,1)S(1)} %get-tuple-element.35.refs_0_, ...), custom_call_target="tpu_custom_call" | custom-call | flops 1153500032 | tf_op jit(solution)/shard_map/final/pallas_call | solution.py:352
  (8 shorter events, 0.0 us)
Async XLA Ops:
  0.0 7.0 %copy-start = (bf16[2,2048,2048]{2,1,0:T(8,128)(2,1)S(1)}, bf16[2,2048,2048]{2,1,0:T(8,128)(2,1)}, u32[]{:S(2)}) copy-start(bf16[2,2048,2048]{2,1,0:T(8,128)(2,1)} %w_ref.1) | copy-start | bytes 50331652
  0.0 7.0 %copy-start.1 = (bf16[2,16,2048]{2,1,0:T(8,128)(2,1)S(1)}, bf16[2,16,2048]{2,1,0:T(8,128)(2,1)}, u32[]{:S(2)}) copy-start(bf16[2,16,2048]{2,1,0:T(8,128)(2,1)} %x_ref.1) | copy-start | bytes 393220
  1.3 8.3 %collective-permute-start = (bf16[16,1152]{1,0:T(8,128)(2,1)S(1)}, bf16[16,1152]{1,0:T(8,128)(2,1)S(1)}, u32[]{:S(2)}, u32[]{:S(2)}) collective-permute-start(bf16[16,1152]{1,0:T(8,128)(2,1)S(1)} %get-tuple-element.25), channel_id=1, source_target_pairs={{0,8},{4,12},{8,0},{12,4},{1,9},{5,13},{9,1},{13,5},{2,10},{6,14},... | collective-permute-start | bytes 110600 | tf_op jit(solution)/shard_map/ppermute | solution.py:258
  5.4 5.8 %collective-permute-start.1 = (bf16[16,1152]{1,0:T(8,128)(2,1)S(1)}, bf16[16,1152]{1,0:T(8,128)(2,1)S(1)}, u32[]{:S(2)}, u32[]{:S(2)}) collective-permute-start(bf16[16,1152]{1,0:T(8,128)(2,1)S(1)} %get-tuple-element.26), channel_id=1, source_target_pairs={{0,12},{4,8},{8,4},{12,0},{1,13},{5,9},{9,5},{13,1},{2,14},{6,10},... | collective-permute-start | bytes 110600 | tf_op jit(solution)/shard_map/ppermute | solution.py:258
  6.7 4.4 %collective-permute-start.2 = (bf16[16,1152]{1,0:T(8,128)(2,1)S(1)}, bf16[16,1152]{1,0:T(8,128)(2,1)S(1)}, u32[]{:S(2)}, u32[]{:S(2)}) collective-permute-start(bf16[16,1152]{1,0:T(8,128)(2,1)S(1)} %get-tuple-element.27), channel_id=1, source_target_pairs={{0,4},{4,0},{8,12},{12,8},{1,5},{5,1},{9,13},{13,9},{2,6},{6,2},{1... | collective-permute-start | bytes 110600 | tf_op jit(solution)/shard_map/ppermute | solution.py:258
  9.5 7.8 %collective-permute-start.3 = (f32[2,2,16,512]{3,2,1,0:T(8,128)S(1)}, f32[2,2,16,512]{3,2,1,0:T(8,128)S(1)}, u32[]{:S(2)}, u32[]{:S(2)}) collective-permute-start(f32[2,2,16,512]{3,2,1,0:T(8,128)S(1)} %get-tuple-element.30), channel_id=1, source_target_pairs={{0,1},{1,0},{2,3},{3,2},{4,5},{5,4},{6,7},{7,6},{8,9},{9,8},{10,11... | collective-permute-start | bytes 393224 | tf_op jit(solution)/shard_map/ppermute | solution.py:258
  15.4 3.5 %collective-permute-start.5 = (f32[32,64]{1,0:T(8,128)S(1)}, f32[32,64]{1,0:T(8,128)S(1)}, u32[]{:S(2)}, u32[]{:S(2)}) collective-permute-start(f32[32,64]{1,0:T(8,128)S(1)} %get-tuple-element.28._.refs_0_), channel_id=1, source_target_pairs={{0,3},{1,2},{2,1},{3,0},{4,7},{5,6},{6,5},{7,4},{8,11},{9,10},{10,... | collective-permute-start | bytes 24584 | tf_op jit(solution)/shard_map/ppermute | solution.py:258
  15.8 3.7 %collective-permute-start.6 = (f32[32,64]{1,0:T(8,128)S(1)}, f32[32,64]{1,0:T(8,128)S(1)}, u32[]{:S(2)}, u32[]{:S(2)}) collective-permute-start(f32[32,64]{1,0:T(8,128)S(1)} %get-tuple-element.28._.refs_0_), channel_id=1, source_target_pairs={{0,2},{1,3},{2,0},{3,1},{4,6},{5,7},{6,4},{7,5},{8,10},{9,11},{10,... | collective-permute-start | bytes 24584 | tf_op jit(solution)/shard_map/ppermute | solution.py:258
  17.0 2.5 %collective-permute-start.7 = (f32[32,64]{1,0:T(8,128)S(1)}, f32[32,64]{1,0:T(8,128)S(1)}, u32[]{:S(2)}, u32[]{:S(2)}) collective-permute-start(f32[32,64]{1,0:T(8,128)S(1)} %get-tuple-element.28._.refs_0_), channel_id=1, source_target_pairs={{0,1},{1,0},{2,3},{3,2},{4,5},{5,4},{6,7},{7,6},{8,9},{9,8},{10,11... | collective-permute-start | bytes 24584 | tf_op jit(solution)/shard_map/ppermute | solution.py:258
  17.3 10.7 %collective-permute-start.4 = (f32[2,16,512]{2,1,0:T(8,128)S(1)}, f32[2,16,512]{2,1,0:T(8,128)S(1)}, u32[]{:S(2)}, u32[]{:S(2)}) collective-permute-start(f32[2,16,512]{2,1,0:T(8,128)S(1)} %get-tuple-element.32), channel_id=1, source_target_pairs={{0,2},{1,3},{2,0},{3,1},{4,6},{5,7},{6,4},{7,5},{8,10},{9,11},{10,... | collective-permute-start | bytes 196616 | tf_op jit(solution)/shard_map/ppermute | solution.py:258
  19.9 4.9 %collective-permute-start.10 = (bf16[16,256]{1,0:T(8,128)(2,1)S(1)}, bf16[16,256]{1,0:T(8,128)(2,1)S(1)}, u32[]{:S(2)}, u32[]{:S(2)}) collective-permute-start(bf16[16,256]{1,0:T(8,128)(2,1)S(1)} %get-tuple-element.38), channel_id=1, source_target_pairs={{0,8},{4,12},{8,0},{12,4},{1,9},{5,13},{9,1},{13,5},{2,10},{6,14},... | collective-permute-start | bytes 24584 | tf_op jit(solution)/shard_map/ppermute | solution.py:258
  22.6 5.4 %collective-permute-start.8 = (bf16[16,256]{1,0:T(8,128)(2,1)S(1)}, bf16[16,256]{1,0:T(8,128)(2,1)S(1)}, u32[]{:S(2)}, u32[]{:S(2)}) collective-permute-start(bf16[16,256]{1,0:T(8,128)(2,1)S(1)} %get-tuple-element.36), channel_id=1, source_target_pairs={{0,12},{4,8},{8,4},{12,0},{1,13},{5,9},{9,5},{13,1},{2,14},{6,10},... | collective-permute-start | bytes 24584 | tf_op jit(solution)/shard_map/ppermute | solution.py:258
  23.9 4.1 %collective-permute-start.9 = (bf16[16,256]{1,0:T(8,128)(2,1)S(1)}, bf16[16,256]{1,0:T(8,128)(2,1)S(1)}, u32[]{:S(2)}, u32[]{:S(2)}) collective-permute-start(bf16[16,256]{1,0:T(8,128)(2,1)S(1)} %get-tuple-element.37), channel_id=1, source_target_pairs={{0,4},{4,0},{8,12},{12,8},{1,5},{5,1},{9,13},{13,9},{2,6},{6,2},{1... | collective-permute-start | bytes 24584 | tf_op jit(solution)/shard_map/ppermute | solution.py:258

commit v11 on v10

--- a/solution.py
+++ b/solution.py
@@ -8,6 +8,7 @@
 from jax.sharding import PartitionSpec as P
 
 CAP = 4
+FIRST, LAST = -1, -2
 HALVES = 2
 LANES = 128
 F32 = jnp.float32
@@ -215,12 +216,13 @@
         out_ref[...] = jnp.concatenate(parts, axis=0).astype(BF16)
 
 
-def final_kernel(count_ref, pick_ref, own_ref, got_ref, *refs):
+def final_kernel(lanes, count_ref, pick_ref, own_ref, got_ref, *refs):
     term_refs, out_ref = refs[:-1], refs[-1]
     layers, rows, width = out_ref.shape
     half = width // HALVES
     live = iota((rows, 1), 0) < count_ref[0]
-    terms = [term_ref[...].astype(F32) for term_ref in term_refs]
+    named = {k: term_ref[...].astype(F32) for k, term_ref in zip([0, *lanes], term_refs)}
+    terms = [named[k] for k in range(len(lanes) - 1)] + [named[FIRST] + named[LAST]]
     for part in range(HALVES):
         span = slice(part * half, (part + 1) * half)
         mine = slice(part * layers * CAP, (part + 1) * layers * CAP)
@@ -258,9 +260,21 @@
         return lax.ppermute(value, axis, [(i, i ^ by) for i in range(size)])
 
     order = [0] + list(range(stores // 2, stores)) + list(range(stores // 2 - 1, 0, -1))
-    back = [0] + order[2:] + order[1:2]
+    far = stores - 1
+
+    def spread_back(values):
+        pairs = [(i, i ^ far) for i in range(stores)]
+        chosen = {FIRST: pairs[-1:], LAST: pairs[:-1]}
+        return [
+            lax.ppermute(values[far], "store", chosen[k])
+            if k in chosen
+            else swap(values[k], "store", stores, k)
+            for k in back_lanes
+        ]
+
+    back_lanes = [LAST, FIRST] + list(range(1, far))
     *payloads, pick = pl.pallas_call(
-        functools.partial(prepare_kernel, back),
+        functools.partial(prepare_kernel, list(range(stores))),
         out_shape=[jax.ShapeDtypeStruct((block, half + LANES), BF16)] * stores
         + [
             jax.ShapeDtypeStruct((layers * rows, stores * layers * CAP), BF16),
@@ -347,12 +361,13 @@
         cost_estimate=cost(1),
         name="up",
     )(own, early_up, late_up, *lows)
-    returned = [swap(terms[order.index(k)], "store", stores, k) for k in back]
+    terms = {k: term for k, term in zip(order, terms)}
+    returned = [terms[0], *spread_back(terms)]
 
     return pl.pallas_call(
-        final_kernel,
+        functools.partial(final_kernel, back_lanes),
         out_shape=jax.ShapeDtypeStruct((layers, rows, width), BF16),
-        in_specs=[SMEM] + [VMEM] * (3 + stores),
+        in_specs=[SMEM] + [VMEM] * (4 + stores),
         out_specs=VMEM,
         compiler_params=params(),
         cost_estimate=cost(1),

time: 28.9 us -> 34.5 us (1.19)
  starting transfers between devices: 13.5 us -> 16.9 us
  waiting for transfers between devices: 5.43 us -> 7.61 us
    ppermute x0 -> x2, waiting for transfers between devices: none -> 5.37 us  [spread_back(): lax.ppermute(values[far], 'store', chosen[k])]
    ppermute x0 -> x2, starting transfers between devices: none -> 3.36 us  [spread_back(): lax.ppermute(values[far], 'store', chosen[k])]
    ppermute x11 -> x10, waiting for transfers between devices: 5.43 us -> 2.24 us  [swap(): return lax.ppermute(value, axis, [(i, i ^ by) for i in range(size)])]
    ppermute x11 -> x10, starting transfers between devices: 13.5 us -> 13.5 us  [swap(): return lax.ppermute(value, axis, [(i, i ^ by) for i in range(size)])]
  transfers between devices with their start and end apart: 11 -> 12, of which waited for: 3 -> 3; matrix products, arithmetic and copies ran while one was open for 0% -> 0% of each run, Pallas kernels for 25% -> 21%
where the time goes in v11:
time: 34.5 us; the launch traced here: 34.3 us
  starting transfers between devices  16.9 us (49%)
  Pallas kernels  9.12 us (26%)
  waiting for transfers between devices  7.61 us (22%)
  between operations  0.74 us (2%)
    ppermute x10, starting transfers between devices, swap(): return lax.ppermute(value, axis, [(i, i ^ by) for i in range(size)])  13.5 us
    ppermute x2, waiting for transfers between devices, spread_back(): lax.ppermute(values[far], 'store', chosen[k])  5.37 us
    pallas_call x1, Pallas kernels, local(): pl.pallas_call(functools.partial(down_kernel, early), out_shape=[jax.Shap...  4.21 us
    ppermute x2, starting transfers between devices, spread_back(): lax.ppermute(values[far], 'store', chosen[k])  3.36 us
    pallas_call x1, Pallas kernels, local(): pl.pallas_call(functools.partial(base_kernel, tensors, early), out_shape=...  2.49 us
    ppermute x10, waiting for transfers between devices, swap(): return lax.ppermute(value, axis, [(i, i ^ by) for i in range(size)])  2.24 us
    pallas_call x1, Pallas kernels, local(): pl.pallas_call(functools.partial(prepare_kernel, list(range(stores))), ou...  1.28 us
    pallas_call x1, Pallas kernels, local(): pl.pallas_call(functools.partial(final_kernel, back_lanes), out_shape=jax...  0.75 us
  transfers between devices with their start and end apart: 12, of which 3 were waited for; matrix products, arithmetic and copies ran while one was open for 0% of the time, Pallas kernels for 21%

profile of v11, /device:TPU:0, one launch (start us, length us, event | category | flops | bytes accessed | tf_op | source)
XLA Modules:
  0.0 34.3 jit_solution(12502334240583258530)
XLA Ops:
  0.0 1.3 %prepare.1 = (bf16[16,1152]{1,0:T(8,128)(2,1)S(1)}, bf16[16,1152]{1,0:T(8,128)(2,1)S(1)}, bf16[16,1152]{1,0:T(8,128)(2,1)S(1)}, bf16[16,1152]{1,0:T(8,128)(2,1)S(1)}, bf16[32,32]{1,0:T(8,128)(2,1)S(1)}) custom-call(s32[1,16]{1,0:T(1,128)} %bitcast.5, s32[1,16]{1,0:T(1,128)} %bitcast.6, bf16[2,16,2048]{2,1,0:T(8,128)(2,1)} %x_ref.1), custom_call_target="tpu_custom_call" | custom-call | flops 6920999936 | tf_op jit(solution)/shard_map/prepare/pallas_call | solution.py:276
  1.3 4.1 %collective-permute-start = (bf16[16,1152]{1,0:T(8,128)(2,1)S(1)}, bf16[16,1152]{1,0:T(8,128)(2,1)S(1)}, u32[]{:S(2)}, u32[]{:S(2)}) collective-permute-start(bf16[16,1152]{1,0:T(8,128)(2,1)S(1)} %get-tuple-element.25), channel_id=1, source_target_pairs={{0,8},{4,12},{8,0},{12,4},{1,9},{5,13},{9,1},{13,5},{2,10},{6,14},... | collective-permute-start | bytes 110600 | tf_op jit(solution)/shard_map/ppermute | solution.py:260
  5.4 1.4 %collective-permute-start.1 = (bf16[16,1152]{1,0:T(8,128)(2,1)S(1)}, bf16[16,1152]{1,0:T(8,128)(2,1)S(1)}, u32[]{:S(2)}, u32[]{:S(2)}) collective-permute-start(bf16[16,1152]{1,0:T(8,128)(2,1)S(1)} %get-tuple-element.26), channel_id=1, source_target_pairs={{0,12},{4,8},{8,4},{12,0},{1,13},{5,9},{9,5},{13,1},{2,14},{6,10},... | collective-permute-start | bytes 110600 | tf_op jit(solution)/shard_map/ppermute | solution.py:260
  6.7 0.2 collective-permute-start.2
  7.0 2.5 %base.1 = (f32[2,2,16,512]{3,2,1,0:T(8,128)S(1)}, f32[2,2,16,512]{3,2,1,0:T(8,128)S(1)}, bf16[1,2,256,2048]{3,2,1,0:T(8,128)(2,1)S(1)}, bf16[1,2,256,512]{3,2,1,0:T(8,128)(2,1)S(1)}) custom-call(bf16[2,32,64,2048]{3,2,1,0:T(8,128)(2,1)} %bitcast.3, bf16[2,32,64,512]{3,2,1,0:T(8,128)(2,1)} %up_hbm.3, bf16[2,16,2048]{2,1,0:T(8,128)(2,1)S(1)} %copy-done.1, ...), custom_call_target="tpu_custom_call" | custom-call | flops 6920999936 | tf_op jit(solution)/shard_map/base/pallas_call | solution.py:297
  9.5 0.1 collective-permute-start.3
  9.5 0.0 collective-permute-done.refs_1_
  9.6 1.6 %collective-permute-done.1.refs_2_ = bf16[16,1152]{1,0:T(8,128)(2,1)S(1)} collective-permute-done((bf16[16,1152]{1,0:T(8,128)(2,1)S(1)}, bf16[16,1152]{1,0:T(8,128)(2,1)S(1)}, u32[]{:S(2)}, u32[]{:S(2)}) %collective-permute-start.1) | collective-permute-done | bytes 36896 | tf_op jit(solution)/shard_map/ppermute | solution.py:260
  11.1 0.0 collective-permute-done.2.refs_3_
  11.1 4.2 %down.1 = (f32[32,64]{1,0:T(8,128)S(1)}, bf16[3,2,256,512]{3,2,1,0:T(8,128)(2,1)S(1)}) custom-call(bf16[2,32,64,2048]{3,2,1,0:T(8,128)(2,1)} %bitcast.4, bf16[2,32,64,512]{3,2,1,0:T(8,128)(2,1)} %up_hbm.3, bf16[1,2,256,2048]{3,2,1,0:T(8,128)(2,1)S(1)} %get-tuple-element.24.early_ref, bf16[16,1152]{1,0:T(8,128)(2,1)S(1)} %get-tuple-element.23.refs_0_, ...), custom_call_target="tpu_custom_call" | custom-call | flops 4614000128 | tf_op jit(solution)/shard_map/down/pallas_call | solution.py:317
  15.4 0.4 %collective-permute-start.5 = (f32[32,64]{1,0:T(8,128)S(1)}, f32[32,64]{1,0:T(8,128)S(1)}, u32[]{:S(2)}, u32[]{:S(2)}) collective-permute-start(f32[32,64]{1,0:T(8,128)S(1)} %get-tuple-element.28._.refs_0_), channel_id=1, source_target_pairs={{0,3},{1,2},{2,1},{3,0},{4,7},{5,6},{6,5},{7,4},{8,11},{9,10},{10,... | collective-permute-start | bytes 24584 | tf_op jit(solution)/shard_map/ppermute | solution.py:260
  15.8 1.2 %collective-permute-start.6 = (f32[32,64]{1,0:T(8,128)S(1)}, f32[32,64]{1,0:T(8,128)S(1)}, u32[]{:S(2)}, u32[]{:S(2)}) collective-permute-start(f32[32,64]{1,0:T(8,128)S(1)} %get-tuple-element.28._.refs_0_), channel_id=1, source_target_pairs={{0,2},{1,3},{2,0},{3,1},{4,6},{5,7},{6,4},{7,5},{8,10},{9,11},{10,... | collective-permute-start | bytes 24584 | tf_op jit(solution)/shard_map/ppermute | solution.py:260
  17.0 0.3 collective-permute-start.7
  17.3 0.0 collective-permute-done.3.got_ref
  17.3 1.6 %collective-permute-start.4 = (f32[2,16,512]{2,1,0:T(8,128)S(1)}, f32[2,16,512]{2,1,0:T(8,128)S(1)}, u32[]{:S(2)}, u32[]{:S(2)}) collective-permute-start(f32[2,16,512]{2,1,0:T(8,128)S(1)} %get-tuple-element.32), channel_id=1, source_target_pairs={{0,2},{1,3},{2,0},{3,1},{4,6},{5,7},{6,4},{7,5},{8,10},{9,11},{10,... | collective-permute-start | bytes 196616 | tf_op jit(solution)/shard_map/ppermute | solution.py:260
  18.9 0.6 %collective-permute-done.6.refs_2_ = f32[32,64]{1,0:T(8,128)S(1)} collective-permute-done((f32[32,64]{1,0:T(8,128)S(1)}, f32[32,64]{1,0:T(8,128)S(1)}, u32[]{:S(2)}, u32[]{:S(2)}) %collective-permute-start.6) | collective-permute-done | bytes 8224 | tf_op jit(solution)/shard_map/ppermute | solution.py:260
  19.5 0.0 collective-permute-done.7.refs_3_
  19.5 0.4 %up.1 = (bf16[16,256]{1,0:T(8,128)(2,1)S(1)}, bf16[16,256]{1,0:T(8,128)(2,1)S(1)}, bf16[16,256]{1,0:T(8,128)(2,1)S(1)}, bf16[16,256]{1,0:T(8,128)(2,1)S(1)}) custom-call(f32[2,16,512]{2,1,0:T(8,128)S(1)} %get-tuple-element.31._.own_ref, bf16[1,2,256,512]{3,2,1,0:T(8,128)(2,1)S(1)} %get-tuple-element.33.early_ref, ...), custom_call_target="tpu_custom_call" | custom-call | flops 1153500032 | tf_op jit(solution)/shard_map/up/pallas_call | solution.py:355
  19.9 1.6 %collective-permute-start.10 = (bf16[16,256]{1,0:T(8,128)(2,1)S(1)}, bf16[16,256]{1,0:T(8,128)(2,1)S(1)}, u32[]{:S(2)}, u32[]{:S(2)}) collective-permute-start(bf16[16,256]{1,0:T(8,128)(2,1)S(1)} %get-tuple-element.37), channel_id=1, source_target_pairs={{0,4},{4,0},{8,12},{12,8},{1,5},{5,1},{9,13},{13,9},{2,6},{6,2},{1... | collective-permute-start | bytes 24584 | tf_op jit(solution)/shard_map/ppermute | solution.py:260
  21.5 2.6 %collective-permute-start.11 = (bf16[16,256]{1,0:T(8,128)(2,1)S(1)}, bf16[16,256]{1,0:T(8,128)(2,1)S(1)}, u32[]{:S(2)}, u32[]{:S(2)}) collective-permute-start(bf16[16,256]{1,0:T(8,128)(2,1)S(1)} %get-tuple-element.38), channel_id=1, source_target_pairs={{0,8},{4,12},{8,0},{12,4},{1,9},{5,13},{9,1},{13,5},{2,10},{6,14},... | collective-permute-start | bytes 24584 | tf_op jit(solution)/shard_map/ppermute | solution.py:260
  24.2 2.1 %collective-permute-start.8 = (bf16[16,256]{1,0:T(8,128)(2,1)S(1)}, bf16[16,256]{1,0:T(8,128)(2,1)S(1)}, u32[]{:S(2)}, u32[]{:S(2)}) collective-permute-start(bf16[16,256]{1,0:T(8,128)(2,1)S(1)} %get-tuple-element.36), channel_id=1, source_target_pairs={{0,12},{4,8},{8,4},{1,13},{5,9},{9,5},{2,14},{6,10},{10,6},{3,15},... | collective-permute-start | bytes 24584 | tf_op jit(solution)/shard_map/ppermute | solution.py:269
  26.2 1.3 %collective-permute-start.9 = (bf16[16,256]{1,0:T(8,128)(2,1)S(1)}, bf16[16,256]{1,0:T(8,128)(2,1)S(1)}, u32[]{:S(2)}, u32[]{:S(2)}) collective-permute-start(bf16[16,256]{1,0:T(8,128)(2,1)S(1)} %get-tuple-element.36), channel_id=1, source_target_pairs={{12,0},{13,1},{14,2},{15,3},{28,16},{29,17},{30,18},{31,19}} | collective-permute-start | bytes 24584 | tf_op jit(solution)/shard_map/ppermute | solution.py:269
  28.2 5.4 %collective-permute-done.9.refs_2_ = bf16[16,256]{1,0:T(8,128)(2,1)S(1)} collective-permute-done((bf16[16,256]{1,0:T(8,128)(2,1)S(1)}, bf16[16,256]{1,0:T(8,128)(2,1)S(1)}, u32[]{:S(2)}, u32[]{:S(2)}) %collective-permute-start.9) | collective-permute-done | bytes 8224 | tf_op jit(solution)/shard_map/ppermute | solution.py:269
  33.6 0.7 %final.1 = bf16[2,16,512]{2,1,0:T(8,128)(2,1)} custom-call(s32[1]{0:T(128)S(6)} %copy.8.count_ref, bf16[32,32]{1,0:T(8,128)(2,1)S(1)} %get-tuple-element.22.pick_ref, f32[2,16,512]{2,1,0:T(8,128)S(1)} %get-tuple-element.31._.own_ref, f32[2,16,512]{2,1,0:T(8,128)S(1)} %collective-permute-done.4.got_ref, bf16[16,256]{1,0:T(8,128)(2,1)S(1)} %get-tuple-element.35.refs_0_, ...), custom_call_target="tpu_custom_call" | custom-call | flops 1153500032 | tf_op jit(solution)/shard_map/final/pallas_call | solution.py:367
  (10 shorter events, 0.0 us)
Async XLA Ops:
  0.0 7.0 %copy-start = (bf16[2,2048,2048]{2,1,0:T(8,128)(2,1)S(1)}, bf16[2,2048,2048]{2,1,0:T(8,128)(2,1)}, u32[]{:S(2)}) copy-start(bf16[2,2048,2048]{2,1,0:T(8,128)(2,1)} %w_ref.1) | copy-start | bytes 50331652
  0.0 7.0 %copy-start.1 = (bf16[2,16,2048]{2,1,0:T(8,128)(2,1)S(1)}, bf16[2,16,2048]{2,1,0:T(8,128)(2,1)}, u32[]{:S(2)}) copy-start(bf16[2,16,2048]{2,1,0:T(8,128)(2,1)} %x_ref.1) | copy-start | bytes 393220
  1.3 8.3 %collective-permute-start = (bf16[16,1152]{1,0:T(8,128)(2,1)S(1)}, bf16[16,1152]{1,0:T(8,128)(2,1)S(1)}, u32[]{:S(2)}, u32[]{:S(2)}) collective-permute-start(bf16[16,1152]{1,0:T(8,128)(2,1)S(1)} %get-tuple-element.25), channel_id=1, source_target_pairs={{0,8},{4,12},{8,0},{12,4},{1,9},{5,13},{9,1},{13,5},{2,10},{6,14},... | collective-permute-start | bytes 110600 | tf_op jit(solution)/shard_map/ppermute | solution.py:260
  5.4 5.8 %collective-permute-start.1 = (bf16[16,1152]{1,0:T(8,128)(2,1)S(1)}, bf16[16,1152]{1,0:T(8,128)(2,1)S(1)}, u32[]{:S(2)}, u32[]{:S(2)}) collective-permute-start(bf16[16,1152]{1,0:T(8,128)(2,1)S(1)} %get-tuple-element.26), channel_id=1, source_target_pairs={{0,12},{4,8},{8,4},{12,0},{1,13},{5,9},{9,5},{13,1},{2,14},{6,10},... | collective-permute-start | bytes 110600 | tf_op jit(solution)/shard_map/ppermute | solution.py:260
  6.7 4.4 %collective-permute-start.2 = (bf16[16,1152]{1,0:T(8,128)(2,1)S(1)}, bf16[16,1152]{1,0:T(8,128)(2,1)S(1)}, u32[]{:S(2)}, u32[]{:S(2)}) collective-permute-start(bf16[16,1152]{1,0:T(8,128)(2,1)S(1)} %get-tuple-element.27), channel_id=1, source_target_pairs={{0,4},{4,0},{8,12},{12,8},{1,5},{5,1},{9,13},{13,9},{2,6},{6,2},{1... | collective-permute-start | bytes 110600 | tf_op jit(solution)/shard_map/ppermute | solution.py:260
  9.5 7.8 %collective-permute-start.3 = (f32[2,2,16,512]{3,2,1,0:T(8,128)S(1)}, f32[2,2,16,512]{3,2,1,0:T(8,128)S(1)}, u32[]{:S(2)}, u32[]{:S(2)}) collective-permute-start(f32[2,2,16,512]{3,2,1,0:T(8,128)S(1)} %get-tuple-element.30), channel_id=1, source_target_pairs={{0,1},{1,0},{2,3},{3,2},{4,5},{5,4},{6,7},{7,6},{8,9},{9,8},{10,11... | collective-permute-start | bytes 393224 | tf_op jit(solution)/shard_map/ppermute | solution.py:260
  15.4 3.5 %collective-permute-start.5 = (f32[32,64]{1,0:T(8,128)S(1)}, f32[32,64]{1,0:T(8,128)S(1)}, u32[]{:S(2)}, u32[]{:S(2)}) collective-permute-start(f32[32,64]{1,0:T(8,128)S(1)} %get-tuple-element.28._.refs_0_), channel_id=1, source_target_pairs={{0,3},{1,2},{2,1},{3,0},{4,7},{5,6},{6,5},{7,4},{8,11},{9,10},{10,... | collective-permute-start | bytes 24584 | tf_op jit(solution)/shard_map/ppermute | solution.py:260
  15.8 3.7 %collective-permute-start.6 = (f32[32,64]{1,0:T(8,128)S(1)}, f32[32,64]{1,0:T(8,128)S(1)}, u32[]{:S(2)}, u32[]{:S(2)}) collective-permute-start(f32[32,64]{1,0:T(8,128)S(1)} %get-tuple-element.28._.refs_0_), channel_id=1, source_target_pairs={{0,2},{1,3},{2,0},{3,1},{4,6},{5,7},{6,4},{7,5},{8,10},{9,11},{10,... | collective-permute-start | bytes 24584 | tf_op jit(solution)/shard_map/ppermute | solution.py:260
  17.0 2.5 %collective-permute-start.7 = (f32[32,64]{1,0:T(8,128)S(1)}, f32[32,64]{1,0:T(8,128)S(1)}, u32[]{:S(2)}, u32[]{:S(2)}) collective-permute-start(f32[32,64]{1,0:T(8,128)S(1)} %get-tuple-element.28._.refs_0_), channel_id=1, source_target_pairs={{0,1},{1,0},{2,3},{3,2},{4,5},{5,4},{6,7},{7,6},{8,9},{9,8},{10,11... | collective-permute-start | bytes 24584 | tf_op jit(solution)/shard_map/ppermute | solution.py:260
  17.3 16.3 %collective-permute-start.4 = (f32[2,16,512]{2,1,0:T(8,128)S(1)}, f32[2,16,512]{2,1,0:T(8,128)S(1)}, u32[]{:S(2)}, u32[]{:S(2)}) collective-permute-start(f32[2,16,512]{2,1,0:T(8,128)S(1)} %get-tuple-element.32), channel_id=1, source_target_pairs={{0,2},{1,3},{2,0},{3,1},{4,6},{5,7},{6,4},{7,5},{8,10},{9,11},{10,... | collective-permute-start | bytes 196616 | tf_op jit(solution)/shard_map/ppermute | solution.py:260
  19.9 8.3 %collective-permute-start.10 = (bf16[16,256]{1,0:T(8,128)(2,1)S(1)}, bf16[16,256]{1,0:T(8,128)(2,1)S(1)}, u32[]{:S(2)}, u32[]{:S(2)}) collective-permute-start(bf16[16,256]{1,0:T(8,128)(2,1)S(1)} %get-tuple-element.37), channel_id=1, source_target_pairs={{0,4},{4,0},{8,12},{12,8},{1,5},{5,1},{9,13},{13,9},{2,6},{6,2},{1... | collective-permute-start | bytes 24584 | tf_op jit(solution)/shard_map/ppermute | solution.py:260
  21.5 6.7 %collective-permute-start.11 = (bf16[16,256]{1,0:T(8,128)(2,1)S(1)}, bf16[16,256]{1,0:T(8,128)(2,1)S(1)}, u32[]{:S(2)}, u32[]{:S(2)}) collective-permute-start(bf16[16,256]{1,0:T(8,128)(2,1)S(1)} %get-tuple-element.38), channel_id=1, source_target_pairs={{0,8},{4,12},{8,0},{12,4},{1,9},{5,13},{9,1},{13,5},{2,10},{6,14},... | collective-permute-start | bytes 24584 | tf_op jit(solution)/shard_map/ppermute | solution.py:260
  24.2 4.0 %collective-permute-start.8 = (bf16[16,256]{1,0:T(8,128)(2,1)S(1)}, bf16[16,256]{1,0:T(8,128)(2,1)S(1)}, u32[]{:S(2)}, u32[]{:S(2)}) collective-permute-start(bf16[16,256]{1,0:T(8,128)(2,1)S(1)} %get-tuple-element.36), channel_id=1, source_target_pairs={{0,12},{4,8},{8,4},{1,13},{5,9},{9,5},{2,14},{6,10},{10,6},{3,15},... | collective-permute-start | bytes 24584 | tf_op jit(solution)/shard_map/ppermute | solution.py:269
  26.2 7.3 %collective-permute-start.9 = (bf16[16,256]{1,0:T(8,128)(2,1)S(1)}, bf16[16,256]{1,0:T(8,128)(2,1)S(1)}, u32[]{:S(2)}, u32[]{:S(2)}) collective-permute-start(bf16[16,256]{1,0:T(8,128)(2,1)S(1)} %get-tuple-element.36), channel_id=1, source_target_pairs={{12,0},{13,1},{14,2},{15,3},{28,16},{29,17},{30,18},{31,19}} | collective-permute-start | bytes 24584 | tf_op jit(solution)/shard_map/ppermute | solution.py:269

commit v12 on v10

--- a/solution.py
+++ b/solution.py
@@ -149,22 +149,28 @@
     late = stores - early
     read_slots(block_refs[early:], half, slot_ref)
 
-    def copy_down(i, c):
-        return fetch(down_hbm, slot_ref[i * CAP + c], late_ref.at[i], down_sems.at[i, c], c)
+    def copy_down(i, layer, c):
+        return pltpu.make_async_copy(
+            down_hbm.at[layer, slot_ref[i * CAP + c]],
+            late_ref.at[i, layer, pl.ds(pl.multiple_of(c * rank, rank), rank)],
+            down_sems.at[i, layer, c],
+        )
 
     def copy_up(i, c):
         return fetch(up_hbm, slot_ref[i * CAP + c], up_ref.at[i], up_sems.at[i, c], c)
 
-    for copy in (copy_down, copy_up):
-        for i in range(late):
-            each_slot(lambda c, i=i, copy=copy: copy(i, c).start())
+    for i in range(late):
+        for layer in range(layers):
+            each_slot(lambda c, i=i, layer=layer: copy_down(i, layer, c).start())
+    for i in range(late):
+        each_slot(lambda c, i=i: copy_up(i, c).start())
     row, column = iota((CAP * rank, block), 0), iota((CAP * rank, block), 1)
     for i in range(stores):
         chosen_ref = early_ref.at[i] if i < early else late_ref.at[i - early]
-        if i >= early:
-            each_slot(lambda c, i=i: copy_down(i - early, c).wait())
         total = jnp.zeros((rank, block), F32)
         for layer in range(layers):
+            if i >= early:
+                each_slot(lambda c, i=i, layer=layer: copy_down(i - early, layer, c).wait())
             for part in range(HALVES):
                 product = lax.dot_general(
                     chosen_ref[layer, :, part * half : (part + 1) * half],
@@ -311,7 +317,7 @@
         scratch_shapes=[
             pltpu.VMEM((late, layers, CAP * rank, depth), BF16),
             pltpu.SMEM((late * CAP,), jnp.int32),
-            pltpu.SemaphoreType.DMA((late, CAP)),
+            pltpu.SemaphoreType.DMA((late, layers, CAP)),
             pltpu.SemaphoreType.DMA((late, CAP)),
             pltpu.VMEM((rank, stores * block), F32),
         ],

time: 28.9 us -> 29.5 us (1.021)
  Pallas kernels: 9.12 us -> 9.43 us
  starting transfers between devices: 13.5 us -> 13.8 us
    pallas_call x1, Pallas kernels: 4.21 us -> 4.53 us  [local(): pl.pallas_call(functools.partial(down_kernel, early), out_shape=[jax.Shap...]
where the time goes in v12:
time: 29.5 us; the launch traced here: 29.3 us
  starting transfers between devices  13.8 us (47%)
  Pallas kernels  9.43 us (32%)
  waiting for transfers between devices  5.34 us (18%)
  between operations  0.72 us (2%)
    ppermute x11, starting transfers between devices, swap(): return lax.ppermute(value, axis, [(i, i ^ by) for i in range(size)])  13.8 us
    ppermute x11, waiting for transfers between devices, swap(): return lax.ppermute(value, axis, [(i, i ^ by) for i in range(size)])  5.34 us
    pallas_call x1, Pallas kernels, local(): pl.pallas_call(functools.partial(down_kernel, early), out_shape=[jax.Shap...  4.53 us
    pallas_call x1, Pallas kernels, local(): pl.pallas_call(functools.partial(base_kernel, tensors, early), out_shape=...  2.49 us
    pallas_call x1, Pallas kernels, local(): pl.pallas_call(functools.partial(prepare_kernel, back), out_shape=[jax.Sh...  1.28 us
    pallas_call x1, Pallas kernels, local(): pl.pallas_call(final_kernel, out_shape=jax.ShapeDtypeStruct((layers, rows...  0.75 us
  transfers between devices with their start and end apart: 11, of which 3 were waited for; matrix products, arithmetic and copies ran while one was open for 0% of the time, Pallas kernels for 25%

profile of v12, /device:TPU:0, one launch (start us, length us, event | category | flops | bytes accessed | tf_op | source)
XLA Modules:
  0.0 29.3 jit_solution(6512029854290394784)
XLA Ops:
  0.0 1.3 %prepare.1 = (bf16[16,1152]{1,0:T(8,128)(2,1)S(1)}, bf16[16,1152]{1,0:T(8,128)(2,1)S(1)}, bf16[16,1152]{1,0:T(8,128)(2,1)S(1)}, bf16[16,1152]{1,0:T(8,128)(2,1)S(1)}, bf16[32,32]{1,0:T(8,128)(2,1)S(1)}) custom-call(s32[1,16]{1,0:T(1,128)} %bitcast.5, s32[1,16]{1,0:T(1,128)} %bitcast.6, bf16[2,16,2048]{2,1,0:T(8,128)(2,1)} %x_ref.1), custom_call_target="tpu_custom_call" | custom-call | flops 6920999936 | tf_op jit(solution)/shard_map/prepare/pallas_call | solution.py:268
  1.3 4.1 %collective-permute-start = (bf16[16,1152]{1,0:T(8,128)(2,1)S(1)}, bf16[16,1152]{1,0:T(8,128)(2,1)S(1)}, u32[]{:S(2)}, u32[]{:S(2)}) collective-permute-start(bf16[16,1152]{1,0:T(8,128)(2,1)S(1)} %get-tuple-element.25), channel_id=1, source_target_pairs={{0,8},{4,12},{8,0},{12,4},{1,9},{5,13},{9,1},{13,5},{2,10},{6,14},... | collective-permute-start | bytes 110600 | tf_op jit(solution)/shard_map/ppermute | solution.py:264
  5.4 1.4 %collective-permute-start.1 = (bf16[16,1152]{1,0:T(8,128)(2,1)S(1)}, bf16[16,1152]{1,0:T(8,128)(2,1)S(1)}, u32[]{:S(2)}, u32[]{:S(2)}) collective-permute-start(bf16[16,1152]{1,0:T(8,128)(2,1)S(1)} %get-tuple-element.26), channel_id=1, source_target_pairs={{0,12},{4,8},{8,4},{12,0},{1,13},{5,9},{9,5},{13,1},{2,14},{6,10},... | collective-permute-start | bytes 110600 | tf_op jit(solution)/shard_map/ppermute | solution.py:264
  6.7 0.2 collective-permute-start.2
  7.0 2.5 %base.1 = (f32[2,2,16,512]{3,2,1,0:T(8,128)S(1)}, f32[2,2,16,512]{3,2,1,0:T(8,128)S(1)}, bf16[1,2,256,2048]{3,2,1,0:T(8,128)(2,1)S(1)}, bf16[1,2,256,512]{3,2,1,0:T(8,128)(2,1)S(1)}) custom-call(bf16[2,32,64,2048]{3,2,1,0:T(8,128)(2,1)} %bitcast.3, bf16[2,32,64,512]{3,2,1,0:T(8,128)(2,1)} %up_hbm.3, bf16[2,16,2048]{2,1,0:T(8,128)(2,1)S(1)} %copy-done.1, ...), custom_call_target="tpu_custom_call" | custom-call | flops 6920999936 | tf_op jit(solution)/shard_map/base/pallas_call | solution.py:289
  9.5 0.1 collective-permute-start.3
  9.5 0.0 collective-permute-done.refs_1_
  9.6 1.6 %collective-permute-done.1.refs_2_ = bf16[16,1152]{1,0:T(8,128)(2,1)S(1)} collective-permute-done((bf16[16,1152]{1,0:T(8,128)(2,1)S(1)}, bf16[16,1152]{1,0:T(8,128)(2,1)S(1)}, u32[]{:S(2)}, u32[]{:S(2)}) %collective-permute-start.1) | collective-permute-done | bytes 36896 | tf_op jit(solution)/shard_map/ppermute | solution.py:264
  11.1 0.0 collective-permute-done.2.refs_3_
  11.1 4.5 %down.1 = (f32[32,64]{1,0:T(8,128)S(1)}, bf16[3,2,256,512]{3,2,1,0:T(8,128)(2,1)S(1)}) custom-call(bf16[2,32,64,2048]{3,2,1,0:T(8,128)(2,1)} %bitcast.4, bf16[2,32,64,512]{3,2,1,0:T(8,128)(2,1)} %up_hbm.3, bf16[1,2,256,2048]{3,2,1,0:T(8,128)(2,1)S(1)} %get-tuple-element.24.early_ref, bf16[16,1152]{1,0:T(8,128)(2,1)S(1)} %get-tuple-element.23.refs_0_, ...), custom_call_target="tpu_custom_call" | custom-call | flops 4614000128 | tf_op jit(solution)/shard_map/down/pallas_call | solution.py:309
  15.7 0.4 %collective-permute-start.5 = (f32[32,64]{1,0:T(8,128)S(1)}, f32[32,64]{1,0:T(8,128)S(1)}, u32[]{:S(2)}, u32[]{:S(2)}) collective-permute-start(f32[32,64]{1,0:T(8,128)S(1)} %get-tuple-element.28._.refs_0_), channel_id=1, source_target_pairs={{0,3},{1,2},{2,1},{3,0},{4,7},{5,6},{6,5},{7,4},{8,11},{9,10},{10,... | collective-permute-start | bytes 24584 | tf_op jit(solution)/shard_map/ppermute | solution.py:264
  16.1 1.2 %collective-permute-start.6 = (f32[32,64]{1,0:T(8,128)S(1)}, f32[32,64]{1,0:T(8,128)S(1)}, u32[]{:S(2)}, u32[]{:S(2)}) collective-permute-start(f32[32,64]{1,0:T(8,128)S(1)} %get-tuple-element.28._.refs_0_), channel_id=1, source_target_pairs={{0,2},{1,3},{2,0},{3,1},{4,6},{5,7},{6,4},{7,5},{8,10},{9,11},{10,... | collective-permute-start | bytes 24584 | tf_op jit(solution)/shard_map/ppermute | solution.py:264
  17.3 0.3 collective-permute-start.7
  17.6 1.6 %collective-permute-start.4 = (f32[2,16,512]{2,1,0:T(8,128)S(1)}, f32[2,16,512]{2,1,0:T(8,128)S(1)}, u32[]{:S(2)}, u32[]{:S(2)}) collective-permute-start(f32[2,16,512]{2,1,0:T(8,128)S(1)} %get-tuple-element.32), channel_id=1, source_target_pairs={{0,2},{1,3},{2,0},{3,1},{4,6},{5,7},{6,4},{7,5},{8,10},{9,11},{10,... | collective-permute-start | bytes 196616 | tf_op jit(solution)/shard_map/ppermute | solution.py:264
  19.2 0.6 %collective-permute-done.6.refs_2_ = f32[32,64]{1,0:T(8,128)S(1)} collective-permute-done((f32[32,64]{1,0:T(8,128)S(1)}, f32[32,64]{1,0:T(8,128)S(1)}, u32[]{:S(2)}, u32[]{:S(2)}) %collective-permute-start.6) | collective-permute-done | bytes 8224 | tf_op jit(solution)/shard_map/ppermute | solution.py:264
  19.8 0.0 collective-permute-done.7.refs_3_
  19.8 0.4 %up.1 = (bf16[16,256]{1,0:T(8,128)(2,1)S(1)}, bf16[16,256]{1,0:T(8,128)(2,1)S(1)}, bf16[16,256]{1,0:T(8,128)(2,1)S(1)}, bf16[16,256]{1,0:T(8,128)(2,1)S(1)}) custom-call(f32[2,16,512]{2,1,0:T(8,128)S(1)} %get-tuple-element.31._.own_ref, bf16[1,2,256,512]{3,2,1,0:T(8,128)(2,1)S(1)} %get-tuple-element.33.early_ref, ...), custom_call_target="tpu_custom_call" | custom-call | flops 1153500032 | tf_op jit(solution)/shard_map/up/pallas_call | solution.py:347
  20.2 2.9 %collective-permute-start.10 = (bf16[16,256]{1,0:T(8,128)(2,1)S(1)}, bf16[16,256]{1,0:T(8,128)(2,1)S(1)}, u32[]{:S(2)}, u32[]{:S(2)}) collective-permute-start(bf16[16,256]{1,0:T(8,128)(2,1)S(1)} %get-tuple-element.38), channel_id=1, source_target_pairs={{0,8},{4,12},{8,0},{12,4},{1,9},{5,13},{9,1},{13,5},{2,10},{6,14},... | collective-permute-start | bytes 24584 | tf_op jit(solution)/shard_map/ppermute | solution.py:264
  23.1 1.6 %collective-permute-start.8 = (bf16[16,256]{1,0:T(8,128)(2,1)S(1)}, bf16[16,256]{1,0:T(8,128)(2,1)S(1)}, u32[]{:S(2)}, u32[]{:S(2)}) collective-permute-start(bf16[16,256]{1,0:T(8,128)(2,1)S(1)} %get-tuple-element.36), channel_id=1, source_target_pairs={{0,12},{4,8},{8,4},{12,0},{1,13},{5,9},{9,5},{13,1},{2,14},{6,10},... | collective-permute-start | bytes 24584 | tf_op jit(solution)/shard_map/ppermute | solution.py:264
  24.7 0.1 collective-permute-start.9
  25.4 3.1 %collective-permute-done.8.refs_1_ = bf16[16,256]{1,0:T(8,128)(2,1)S(1)} collective-permute-done((bf16[16,256]{1,0:T(8,128)(2,1)S(1)}, bf16[16,256]{1,0:T(8,128)(2,1)S(1)}, u32[]{:S(2)}, u32[]{:S(2)}) %collective-permute-start.8) | collective-permute-done | bytes 8224 | tf_op jit(solution)/shard_map/ppermute | solution.py:264
  28.5 0.0 collective-permute-done.9.refs_2_
  28.5 0.0 collective-permute-done.4.got_ref
  28.5 0.7 %final.1 = bf16[2,16,512]{2,1,0:T(8,128)(2,1)} custom-call(s32[1]{0:T(128)S(6)} %copy.8.count_ref, bf16[32,32]{1,0:T(8,128)(2,1)S(1)} %get-tuple-element.22.pick_ref, f32[2,16,512]{2,1,0:T(8,128)S(1)} %get-tuple-element.31._.own_ref, f32[2,16,512]{2,1,0:T(8,128)S(1)} %collective-permute-done.4.got_ref, bf16[16,256]{1,0:T(8,128)(2,1)S(1)} %get-tuple-element.35.refs_0_, ...), custom_call_target="tpu_custom_call" | custom-call | flops 1153500032 | tf_op jit(solution)/shard_map/final/pallas_call | solution.py:358
  (8 shorter events, 0.0 us)
Async XLA Ops:
  0.0 7.0 %copy-start = (bf16[2,2048,2048]{2,1,0:T(8,128)(2,1)S(1)}, bf16[2,2048,2048]{2,1,0:T(8,128)(2,1)}, u32[]{:S(2)}) copy-start(bf16[2,2048,2048]{2,1,0:T(8,128)(2,1)} %w_ref.1) | copy-start | bytes 50331652
  0.0 7.0 %copy-start.1 = (bf16[2,16,2048]{2,1,0:T(8,128)(2,1)S(1)}, bf16[2,16,2048]{2,1,0:T(8,128)(2,1)}, u32[]{:S(2)}) copy-start(bf16[2,16,2048]{2,1,0:T(8,128)(2,1)} %x_ref.1) | copy-start | bytes 393220
  1.3 8.3 %collective-permute-start = (bf16[16,1152]{1,0:T(8,128)(2,1)S(1)}, bf16[16,1152]{1,0:T(8,128)(2,1)S(1)}, u32[]{:S(2)}, u32[]{:S(2)}) collective-permute-start(bf16[16,1152]{1,0:T(8,128)(2,1)S(1)} %get-tuple-element.25), channel_id=1, source_target_pairs={{0,8},{4,12},{8,0},{12,4},{1,9},{5,13},{9,1},{13,5},{2,10},{6,14},... | collective-permute-start | bytes 110600 | tf_op jit(solution)/shard_map/ppermute | solution.py:264
  5.4 5.8 %collective-permute-start.1 = (bf16[16,1152]{1,0:T(8,128)(2,1)S(1)}, bf16[16,1152]{1,0:T(8,128)(2,1)S(1)}, u32[]{:S(2)}, u32[]{:S(2)}) collective-permute-start(bf16[16,1152]{1,0:T(8,128)(2,1)S(1)} %get-tuple-element.26), channel_id=1, source_target_pairs={{0,12},{4,8},{8,4},{12,0},{1,13},{5,9},{9,5},{13,1},{2,14},{6,10},... | collective-permute-start | bytes 110600 | tf_op jit(solution)/shard_map/ppermute | solution.py:264
  6.7 4.4 %collective-permute-start.2 = (bf16[16,1152]{1,0:T(8,128)(2,1)S(1)}, bf16[16,1152]{1,0:T(8,128)(2,1)S(1)}, u32[]{:S(2)}, u32[]{:S(2)}) collective-permute-start(bf16[16,1152]{1,0:T(8,128)(2,1)S(1)} %get-tuple-element.27), channel_id=1, source_target_pairs={{0,4},{4,0},{8,12},{12,8},{1,5},{5,1},{9,13},{13,9},{2,6},{6,2},{1... | collective-permute-start | bytes 110600 | tf_op jit(solution)/shard_map/ppermute | solution.py:264
  9.5 8.1 %collective-permute-start.3 = (f32[2,2,16,512]{3,2,1,0:T(8,128)S(1)}, f32[2,2,16,512]{3,2,1,0:T(8,128)S(1)}, u32[]{:S(2)}, u32[]{:S(2)}) collective-permute-start(f32[2,2,16,512]{3,2,1,0:T(8,128)S(1)} %get-tuple-element.30), channel_id=1, source_target_pairs={{0,1},{1,0},{2,3},{3,2},{4,5},{5,4},{6,7},{7,6},{8,9},{9,8},{10,11... | collective-permute-start | bytes 393224 | tf_op jit(solution)/shard_map/ppermute | solution.py:264
  15.7 3.5 %collective-permute-start.5 = (f32[32,64]{1,0:T(8,128)S(1)}, f32[32,64]{1,0:T(8,128)S(1)}, u32[]{:S(2)}, u32[]{:S(2)}) collective-permute-start(f32[32,64]{1,0:T(8,128)S(1)} %get-tuple-element.28._.refs_0_), channel_id=1, source_target_pairs={{0,3},{1,2},{2,1},{3,0},{4,7},{5,6},{6,5},{7,4},{8,11},{9,10},{10,... | collective-permute-start | bytes 24584 | tf_op jit(solution)/shard_map/ppermute | solution.py:264
  16.1 3.7 %collective-permute-start.6 = (f32[32,64]{1,0:T(8,128)S(1)}, f32[32,64]{1,0:T(8,128)S(1)}, u32[]{:S(2)}, u32[]{:S(2)}) collective-permute-start(f32[32,64]{1,0:T(8,128)S(1)} %get-tuple-element.28._.refs_0_), channel_id=1, source_target_pairs={{0,2},{1,3},{2,0},{3,1},{4,6},{5,7},{6,4},{7,5},{8,10},{9,11},{10,... | collective-permute-start | bytes 24584 | tf_op jit(solution)/shard_map/ppermute | solution.py:264
  17.3 2.5 %collective-permute-start.7 = (f32[32,64]{1,0:T(8,128)S(1)}, f32[32,64]{1,0:T(8,128)S(1)}, u32[]{:S(2)}, u32[]{:S(2)}) collective-permute-start(f32[32,64]{1,0:T(8,128)S(1)} %get-tuple-element.28._.refs_0_), channel_id=1, source_target_pairs={{0,1},{1,0},{2,3},{3,2},{4,5},{5,4},{6,7},{7,6},{8,9},{9,8},{10,11... | collective-permute-start | bytes 24584 | tf_op jit(solution)/shard_map/ppermute | solution.py:264
  17.6 10.9 %collective-permute-start.4 = (f32[2,16,512]{2,1,0:T(8,128)S(1)}, f32[2,16,512]{2,1,0:T(8,128)S(1)}, u32[]{:S(2)}, u32[]{:S(2)}) collective-permute-start(f32[2,16,512]{2,1,0:T(8,128)S(1)} %get-tuple-element.32), channel_id=1, source_target_pairs={{0,2},{1,3},{2,0},{3,1},{4,6},{5,7},{6,4},{7,5},{8,10},{9,11},{10,... | collective-permute-start | bytes 196616 | tf_op jit(solution)/shard_map/ppermute | solution.py:264
  20.2 5.2 %collective-permute-start.10 = (bf16[16,256]{1,0:T(8,128)(2,1)S(1)}, bf16[16,256]{1,0:T(8,128)(2,1)S(1)}, u32[]{:S(2)}, u32[]{:S(2)}) collective-permute-start(bf16[16,256]{1,0:T(8,128)(2,1)S(1)} %get-tuple-element.38), channel_id=1, source_target_pairs={{0,8},{4,12},{8,0},{12,4},{1,9},{5,13},{9,1},{13,5},{2,10},{6,14},... | collective-permute-start | bytes 24584 | tf_op jit(solution)/shard_map/ppermute | solution.py:264
  23.1 5.4 %collective-permute-start.8 = (bf16[16,256]{1,0:T(8,128)(2,1)S(1)}, bf16[16,256]{1,0:T(8,128)(2,1)S(1)}, u32[]{:S(2)}, u32[]{:S(2)}) collective-permute-start(bf16[16,256]{1,0:T(8,128)(2,1)S(1)} %get-tuple-element.36), channel_id=1, source_target_pairs={{0,12},{4,8},{8,4},{12,0},{1,13},{5,9},{9,5},{13,1},{2,14},{6,10},... | collective-permute-start | bytes 24584 | tf_op jit(solution)/shard_map/ppermute | solution.py:264
  24.7 3.8 %collective-permute-start.9 = (bf16[16,256]{1,0:T(8,128)(2,1)S(1)}, bf16[16,256]{1,0:T(8,128)(2,1)S(1)}, u32[]{:S(2)}, u32[]{:S(2)}) collective-permute-start(bf16[16,256]{1,0:T(8,128)(2,1)S(1)} %get-tuple-element.37), channel_id=1, source_target_pairs={{0,4},{4,0},{8,12},{12,8},{1,5},{5,1},{9,13},{13,9},{2,6},{6,2},{1... | collective-permute-start | bytes 24584 | tf_op jit(solution)/shard_map/ppermute | solution.py:264
